TPU v7x, 32 devices: a whole 2x2x4 slice. The times are simulated.
32 devices in a mesh: dp: 4 (over x, core), fsdp: 8 (over z, y).
Axes of the slice: x: 2, y: 2, z: 4, core: 2. Of those that a mesh axis runs over, the one named last changes fastest.
Arguments:
- layer_in: bfloat16 [4096, 2048], P(('dp', 'fsdp')), may hold values from -12 to 12
- cotangent: bfloat16 [4096, 2048], P(('dp', 'fsdp')), may hold values from -6 to 6
- w_qkv: bfloat16 [2048, 6144], P(('dp', 'fsdp')), may hold values from -1 to 1
- w_out: bfloat16 [2048, 2048], P(('dp', 'fsdp')), may hold values from -0.5 to 0.5
- w_up: bfloat16 [2048, 8192], P(('dp', 'fsdp')), may hold values from -0.125 to 0.125
- w_down: bfloat16 [8192, 2048], P(('dp', 'fsdp')), may hold values from -0.0625 to 0.0625
- gain_attn: bfloat16 [2048], P(('dp', 'fsdp')), may hold values from 0.5 to 1.5
- shift_attn: bfloat16 [2048], P(('dp', 'fsdp')), may hold values from -1.5 to 1.5
- bias_query: bfloat16 [2048], P(('dp', 'fsdp')), may hold values from -1.5 to 1.5
- bias_value: bfloat16 [2048], P(('dp', 'fsdp')), may hold values from -1.5 to 1.5
- bias_out: bfloat16 [2048], P(('dp', 'fsdp')), may hold values from -1.5 to 1.5
- gain_mlp: bfloat16 [2048], P(('dp', 'fsdp')), may hold values from 0.5 to 1.5
- shift_mlp: bfloat16 [2048], P(('dp', 'fsdp')), may hold values from -1.5 to 1.5
- bias_up: bfloat16 [8192], P(('dp', 'fsdp')), may hold values from -1.5 to 1.5
- bias_down: bfloat16 [2048], P(('dp', 'fsdp')), may hold values from -1.5 to 1.5
- parents: int32 [4, 13], P('dp'), may hold values from 0 to 4, as said below
- seg_blocks: int32 [4, 32], P('dp'), may hold values from 0 to 12, as said below
- token_valid: int32 [4, 1024], P('dp'), may hold values from 0 to 1, as said below
Outputs:
- layer_out: bfloat16 [4096, 2048], P(('dp', 'fsdp'))
- grad_x: bfloat16 [4096, 2048], P(('dp', 'fsdp'))
- grad_w_qkv: float32 [2048, 6144], P(('dp', 'fsdp'))
- grad_w_out: float32 [2048, 2048], P(('dp', 'fsdp'))
- grad_w_up: float32 [2048, 8192], P(('dp', 'fsdp'))
- grad_w_down: float32 [8192, 2048], P(('dp', 'fsdp'))
- grad_gain_attn: float32 [2048], P(('dp', 'fsdp'))
- grad_shift_attn: float32 [2048], P(('dp', 'fsdp'))
- grad_bias_query: float32 [2048], P(('dp', 'fsdp'))
- grad_bias_value: float32 [2048], P(('dp', 'fsdp'))
- grad_bias_out: float32 [2048], P(('dp', 'fsdp'))
- grad_gain_mlp: float32 [2048], P(('dp', 'fsdp'))
- grad_shift_mlp: float32 [2048], P(('dp', 'fsdp'))
- grad_bias_up: float32 [8192], P(('dp', 'fsdp'))
- grad_bias_down: float32 [2048], P(('dp', 'fsdp'))
- root_squares: float32 [2], replicated
Inputs may be any that keep to these rules, and one draw needn't show every extreme that they name: `parents`: segment 0 of each tree is its trunk and has parent 0; segments 1 to 4 are branches with parent 0; the other segments are leaves, two under each branch. `seg_blocks`: each segment holds one run of whole consecutive blocks, one or more; the trunk holds 16 blocks. `token_valid`: padding lies only at the end of the last block of a segment, which keeps one valid token or more and loses one or more.
All inputs are finite; a program needn't handle non-finite values.
Results may differ from a plain program's by a relative error of at most 0.014.
Values may be sent and summed in bfloat16 or wider, within the bound.
A program may use at most 704 MiB of HBM per device.

v0:
```python
import math

import jax
import jax.numpy as jnp
from jax import lax
from jax.sharding import PartitionSpec as P

D = 2048
H = 32
HD = 64
BLK = 32


EPSILON = 1e-05
MASKED = -1e30


def norm_parts(values):
    center = values - jnp.mean(values, axis=-1, keepdims=True)
    inverse = lax.rsqrt(jnp.mean(center * center, axis=-1, keepdims=True) + EPSILON)
    return (center * inverse, inverse)


def norm_back(grad_normed, normed, inverse):
    mean_grad = jnp.mean(grad_normed, axis=-1, keepdims=True)
    mean_cross = jnp.mean(grad_normed * normed, axis=-1, keepdims=True)
    return inverse * (grad_normed - mean_grad - normed * mean_cross)


def tree_tables(parents, seg_blocks, valid):
    segments = parents.shape[0]
    seg_tokens = jnp.broadcast_to(seg_blocks[:, None], (seg_blocks.shape[0], BLK)).reshape(-1)
    labels = jnp.arange(segments, dtype=jnp.int32)
    member = (seg_tokens[:, None] == labels[None, :]).astype(jnp.int32)
    counted = member * valid[:, None]
    before = jnp.cumsum(counted, axis=0) - counted
    rank = jnp.sum(before * member, axis=1)
    seg_len = jnp.sum(counted, axis=0)
    picked = (parents[:, None] == labels[None, :]).astype(jnp.int32)
    grand = jnp.sum(picked * parents[None, :], axis=1)
    ancestor = ((labels[None, :] == parents[:, None]) | (labels[None, :] == grand[:, None])) & (
        labels[None, :] != labels[:, None]
    )
    offset = jnp.sum(ancestor.astype(jnp.int32) * seg_len[None, :], axis=1)
    position = jnp.sum(member * offset[None, :], axis=1) + rank
    return (seg_tokens, position, ancestor.astype(jnp.float32))


def allowed_pairs(
    seg_query, pos_query, index_query, seg_key, pos_key, index_key, valid_key, ancestor
):
    labels = jnp.arange(ancestor.shape[0], dtype=jnp.int32)
    member_query = (seg_query[:, None] == labels[None, :]).astype(jnp.float32)
    member_key = (seg_key[:, None] == labels[None, :]).astype(jnp.float32)
    reach = jnp.dot(jnp.dot(member_query, ancestor), member_key.T) > 0.5
    causal = (seg_query[:, None] == seg_key[None, :]) & (index_key[None, :] <= index_query[:, None])
    visible = (valid_key[None, :] == 1) | (index_key[None, :] == index_query[:, None])
    distance = (pos_query[:, None] - pos_key[None, :]).astype(jnp.float32)
    return ((reach | causal) & visible, distance)


def gelu_exact(value):
    return jax.nn.gelu(value, approximate=False)


def per_device(
    layer_in,
    cotangent,
    w_qkv,
    w_out,
    w_up,
    w_down,
    gain_attn,
    shift_attn,
    bias_query,
    bias_value,
    bias_out,
    gain_mlp,
    shift_mlp,
    bias_up,
    bias_down,
    parents,
    seg_blocks,
    token_valid,
):
    rows = layer_in.shape[0]
    gathered = (
        lax.all_gather(w_qkv, ("dp", "fsdp"), axis=0, tiled=True),
        lax.all_gather(w_out, ("dp", "fsdp"), axis=0, tiled=True),
        lax.all_gather(gain_attn, ("dp", "fsdp"), axis=0, tiled=True),
        lax.all_gather(shift_attn, ("dp", "fsdp"), axis=0, tiled=True),
        lax.all_gather(bias_query, ("dp", "fsdp"), axis=0, tiled=True),
        lax.all_gather(bias_value, ("dp", "fsdp"), axis=0, tiled=True),
        lax.all_gather(bias_out, ("dp", "fsdp"), axis=0, tiled=True),
        lax.all_gather(gain_mlp, ("dp", "fsdp"), axis=0, tiled=True),
        lax.all_gather(shift_mlp, ("dp", "fsdp"), axis=0, tiled=True),
        lax.all_gather(bias_up, ("dp", "fsdp"), axis=0, tiled=True),
        lax.all_gather(bias_down, ("dp", "fsdp"), axis=0, tiled=True),
    )
    full_qkv = gathered[0]
    full_out = gathered[1]
    vectors = [piece.astype(jnp.float32) for piece in gathered[2:]]
    (
        gain_one,
        shift_one,
        query_bias,
        value_bias,
        out_bias,
        gain_two,
        shift_two,
        up_bias,
        down_bias,
    ) = vectors
    valid_tokens = token_valid[0]
    seg_tokens, position, ancestor = tree_tables(parents[0], seg_blocks[0], valid_tokens)
    tree = valid_tokens.shape[0]
    first = lax.axis_index("fsdp") * rows
    index_query = first + jnp.arange(rows, dtype=jnp.int32)
    seg_query = lax.dynamic_slice_in_dim(seg_tokens, first, rows, 0)
    pos_query = lax.dynamic_slice_in_dim(position, first, rows, 0)
    slopes = jnp.exp2(-8.0 * (jnp.arange(H, dtype=jnp.float32) + 1.0) / H)
    key_block = math.gcd(tree, 512)
    block_count = tree // key_block
    numbers = jnp.arange(block_count, dtype=jnp.int32)
    inputs = layer_in.astype(jnp.float32)
    normed_one, inverse_one = norm_parts(inputs)
    attn_in = (normed_one * gain_one + shift_one).astype(jnp.bfloat16)
    joined = jnp.dot(attn_in, full_qkv, preferred_element_type=jnp.float32)
    joined = (
        joined + jnp.concatenate([query_bias, jnp.zeros_like(query_bias), value_bias])
    ).astype(jnp.bfloat16)
    width = joined.shape[1] // 3
    queries = joined[:, :width]
    query_heads = queries.reshape(rows, H, HD)
    keys_all, values_all = (
        lax.all_gather(joined[:, width : 2 * width], "fsdp", axis=0, tiled=True),
        lax.all_gather(joined[:, 2 * width :], "fsdp", axis=0, tiled=True),
    )

    def logits_at(keys_src, values_src, start, count):
        key_heads = lax.dynamic_slice_in_dim(keys_src, start, count, 0).reshape(count, H, HD)
        value_heads = lax.dynamic_slice_in_dim(values_src, start, count, 0).reshape(count, H, HD)
        seg_key = lax.dynamic_slice_in_dim(seg_tokens, start, count, 0)
        pos_key = lax.dynamic_slice_in_dim(position, start, count, 0)
        valid_key = lax.dynamic_slice_in_dim(valid_tokens, start, count, 0)
        index_key = start + jnp.arange(count, dtype=jnp.int32)
        mask, distance = allowed_pairs(
            seg_query, pos_query, index_query, seg_key, pos_key, index_key, valid_key, ancestor
        )
        raw = jnp.einsum("qhd,khd->hqk", query_heads, key_heads, preferred_element_type=jnp.float32)
        logits = jnp.where(
            mask[None], raw * HD ** (-0.5) - slopes[:, None, None] * distance[None], MASKED
        )
        return (logits, key_heads, value_heads)

    def stat_step(carry, number):
        peak, total = carry
        logits, key_heads, value_heads = logits_at(
            keys_all, values_all, number * key_block, key_block
        )
        new_peak = jnp.maximum(peak, jnp.max(logits, axis=-1))
        total = total * jnp.exp(peak - new_peak) + jnp.sum(
            jnp.exp(logits - new_peak[..., None]), axis=-1
        )
        return ((new_peak, total), None)

    start_peak = jnp.full((H, rows), MASKED, jnp.float32)
    start_total = jnp.zeros((H, rows), jnp.float32)
    (peak, total), _ = lax.scan(stat_step, (start_peak, start_total), numbers)

    def mix_step(rounded_sum, number):
        logits, key_heads, value_heads = logits_at(
            keys_all, values_all, number * key_block, key_block
        )
        probs = jnp.exp(logits - peak[..., None]) / total[..., None]
        rounded_sum = rounded_sum + jnp.einsum(
            "hqk,khd->qhd",
            probs.astype(jnp.bfloat16),
            value_heads,
            preferred_element_type=jnp.float32,
        )
        return (rounded_sum, None)

    zero_heads = jnp.zeros((rows, H, HD), jnp.float32)
    rounded_sum, _ = lax.scan(mix_step, zero_heads, numbers)
    mixed = rounded_sum.reshape(rows, H * HD).astype(jnp.bfloat16)
    branch = jnp.dot(mixed, full_out, preferred_element_type=jnp.float32) + out_bias
    middle = inputs + branch
    normed_two, inverse_two = norm_parts(middle)
    mlp_in = (normed_two * gain_two + shift_two).astype(jnp.bfloat16)
    mlp_pair = (
        lax.all_gather(w_up, ("dp", "fsdp"), axis=0, tiled=True),
        lax.all_gather(w_down, ("dp", "fsdp"), axis=0, tiled=True),
    )
    hidden = jnp.dot(mlp_in, mlp_pair[0], preferred_element_type=jnp.float32) + up_bias
    active_float, gelu_pull = jax.vjp(gelu_exact, hidden)
    active = active_float.astype(jnp.bfloat16)
    update = jnp.dot(active, mlp_pair[1], preferred_element_type=jnp.float32) + down_bias
    result = middle + update
    squares = lax.psum((jnp.sum(result * result), jnp.sum(branch * branch)), ("dp", "fsdp"))
    entries = lax.axis_size(("dp", "fsdp")) * rows * D
    root_squares = jnp.sqrt(jnp.stack(squares) / entries)
    back_up, back_down = (
        lax.all_gather(w_up, ("dp", "fsdp"), axis=0, tiled=True),
        lax.all_gather(w_down, ("dp", "fsdp"), axis=0, tiled=True),
    )
    grad_bias_down = jnp.sum(cotangent.astype(jnp.float32), axis=0)
    grad_active = jnp.einsum("td,fd->tf", cotangent, back_down, preferred_element_type=jnp.float32)
    grad_hidden = gelu_pull(grad_active)[0].astype(jnp.bfloat16)
    grad_bias_up = jnp.sum(grad_hidden.astype(jnp.float32), axis=0)
    grad_mlp_in = jnp.einsum("tf,df->td", grad_hidden, back_up, preferred_element_type=jnp.float32)
    grad_gain_two = jnp.sum(grad_mlp_in * normed_two, axis=0)
    grad_shift_two = jnp.sum(grad_mlp_in, axis=0)
    grad_middle = cotangent.astype(jnp.float32) + norm_back(
        grad_mlp_in * gain_two, normed_two, inverse_two
    )
    grad_down_w = jnp.einsum("tf,td->fd", active, cotangent, preferred_element_type=jnp.float32)
    grad_up_w = jnp.einsum("td,tf->df", mlp_in, grad_hidden, preferred_element_type=jnp.float32)
    grad_up_part, grad_down_part = (
        lax.psum_scatter(grad_up_w, ("dp", "fsdp"), scatter_dimension=0, tiled=True),
        lax.psum_scatter(grad_down_w, ("dp", "fsdp"), scatter_dimension=0, tiled=True),
    )
    back_qkv, back_out = (
        lax.all_gather(w_qkv, ("dp", "fsdp"), axis=0, tiled=True),
        lax.all_gather(w_out, ("dp", "fsdp"), axis=0, tiled=True),
    )
    grad_branch = grad_middle.astype(jnp.bfloat16)
    grad_bias_out = jnp.sum(grad_branch.astype(jnp.float32), axis=0)
    grad_mixed = jnp.einsum(
        "te,de->td", grad_branch, back_out, preferred_element_type=jnp.float32
    ).astype(jnp.bfloat16)
    grad_heads = grad_mixed.reshape(rows, H, HD)
    delta = jnp.sum(grad_heads.astype(jnp.float32) * rounded_sum, axis=-1).T
    keys_back, values_back = (
        lax.all_gather(joined[:, width : 2 * width], "fsdp", axis=0, tiled=True),
        lax.all_gather(joined[:, 2 * width :], "fsdp", axis=0, tiled=True),
    )

    def score_grads(start, count):
        logits, key_heads, value_heads = logits_at(keys_back, values_back, start, count)
        probs = jnp.exp(logits - peak[..., None]) / total[..., None]
        grad_probs = jnp.einsum(
            "qhd,khd->hqk", grad_heads, value_heads, preferred_element_type=jnp.float32
        )
        grad_raw = (probs * (grad_probs - delta[..., None]) * HD ** (-0.5)).astype(jnp.bfloat16)
        return (probs, grad_raw, key_heads)

    def query_step(carry, number):
        probs, grad_raw, key_heads = score_grads(number * key_block, key_block)
        return (
            carry
            + jnp.einsum("hqk,khd->qhd", grad_raw, key_heads, preferred_element_type=jnp.float32),
            None,
        )

    grad_query, _ = lax.scan(query_step, zero_heads, numbers)
    inner = math.gcd(rows * lax.axis_size("fsdp"), 512)

    def one_piece(number):
        probs, grad_raw, key_heads = score_grads(number * inner, inner)
        grad_keys = jnp.einsum(
            "hqk,qhd->khd", grad_raw, query_heads, preferred_element_type=jnp.float32
        )
        grad_values = jnp.einsum(
            "hqk,qhd->khd",
            probs.astype(jnp.bfloat16),
            grad_heads,
            preferred_element_type=jnp.float32,
        )
        return jnp.concatenate(
            [grad_keys.reshape(inner, H * HD), grad_values.reshape(inner, H * HD)], axis=1
        )

    pieces = lax.map(one_piece, jnp.arange(rows * lax.axis_size("fsdp") // inner, dtype=jnp.int32))
    key_value_grad = lax.psum_scatter(
        pieces.reshape(rows * lax.axis_size("fsdp"), 2 * H * HD).astype(jnp.bfloat16),
        "fsdp",
        scatter_dimension=0,
        tiled=True,
    ).astype(jnp.float32)
    grad_joined = jnp.concatenate(
        [grad_query.reshape(rows, H * HD), key_value_grad], axis=1
    ).astype(jnp.bfloat16)
    grad_bias_q = jnp.sum(grad_joined[:, :width].astype(jnp.float32), axis=0)
    grad_bias_v = jnp.sum(grad_joined[:, 2 * width :].astype(jnp.float32), axis=0)
    grad_attn_in = jnp.einsum(
        "te,de->td", grad_joined, back_qkv, preferred_element_type=jnp.float32
    )
    grad_gain_one = jnp.sum(grad_attn_in * normed_one, axis=0)
    grad_shift_one = jnp.sum(grad_attn_in, axis=0)
    grad_inputs = grad_middle + norm_back(grad_attn_in * gain_one, normed_one, inverse_one)
    small_grads = (
        grad_gain_one,
        grad_shift_one,
        grad_bias_q,
        grad_bias_v,
        grad_bias_out,
        grad_gain_two,
        grad_shift_two,
        grad_bias_up,
        grad_bias_down,
    )
    grad_qkv_w = jnp.einsum("td,te->de", attn_in, grad_joined, preferred_element_type=jnp.float32)
    grad_out_w = jnp.einsum("td,te->de", mixed, grad_branch, preferred_element_type=jnp.float32)
    shares = lax.psum_scatter(
        (grad_qkv_w, grad_out_w) + small_grads, ("dp", "fsdp"), scatter_dimension=0, tiled=True
    )
    qkv_part, out_part = (shares[0], shares[1])
    small_parts = shares[2:]
    return (
        result.astype(jnp.bfloat16),
        grad_inputs.astype(jnp.bfloat16),
        qkv_part,
        out_part,
        grad_up_part,
        grad_down_part,
        small_parts[0],
        small_parts[1],
        small_parts[2],
        small_parts[3],
        small_parts[4],
        small_parts[5],
        small_parts[6],
        small_parts[7],
        small_parts[8],
        root_squares,
    )


def solution(mesh):
    placed = (
        P(("dp", "fsdp"), None),
        P(("dp", "fsdp"), None),
        P(("dp", "fsdp"), None),
        P(("dp", "fsdp"), None),
        P(("dp", "fsdp"), None),
        P(("dp", "fsdp"), None),
        P(("dp", "fsdp")),
        P(("dp", "fsdp")),
        P(("dp", "fsdp")),
        P(("dp", "fsdp")),
        P(("dp", "fsdp")),
        P(("dp", "fsdp")),
        P(("dp", "fsdp")),
        P(("dp", "fsdp")),
        P(("dp", "fsdp")),
        P("dp", None),
        P("dp", None),
        P("dp", None),
    )
    return jax.shard_map(
        per_device,
        mesh=mesh,
        in_specs=placed,
        out_specs=(
            P(("dp", "fsdp"), None),
            P(("dp", "fsdp"), None),
            P(("dp", "fsdp"), None),
            P(("dp", "fsdp"), None),
            P(("dp", "fsdp"), None),
            P(("dp", "fsdp"), None),
            P(("dp", "fsdp")),
            P(("dp", "fsdp")),
            P(("dp", "fsdp")),
            P(("dp", "fsdp")),
            P(("dp", "fsdp")),
            P(("dp", "fsdp")),
            P(("dp", "fsdp")),
            P(("dp", "fsdp")),
            P(("dp", "fsdp")),
            P(),
        ),
        check_vma=False,
    )
```

profile of v0, /device:TPU:0, one launch (start us, length us, event | category | flops | bytes accessed | tf_op | source)
XLA Modules:
  0.0 4697.8 jit_solution(16611737130590732819)
XLA Ops:
  14.8 43.8 all-reduce.18
  61.2 108.6 %all-gather.8.cloned.1.call-done = bf16[2048,6144]{1,0:T(8,128)(2,1)} async-done(((bf16[64,6144]{1,0:T(8,128)(2,1)}), bf16[2048,6144]{1,0:T(8,128)(2,1)}) %all-gather.8.cloned.1.call-update) | async-done | bytes 25165840 | tf_op jit(solution)/shard_map/all_gather | solution.py:88
  169.8 11.9 fusion.145
  194.4 66.4 %all-gather = bf16[32,1,256]{2,1,0:T(2,128)(2,1)S(1)} all-gather(bf16[1,1,256]{2,1,0:T(2,128)(2,1)S(1)} %reshape.354), channel_id=1, replica_groups=mesh['dp'=4,'fsdp'=8] {'dp','fsdp'}, dimensions={0}, use_global_device_ids=true | all-gather | bytes 16896 | tf_op jit(solution)/shard_map/all_gather | solution.py:97
  261.8 6.4 copy.124
  268.2 61.2 %all-gather.10.cloned.1.call-done = bf16[1024,2048]{1,0:T(8,128)(2,1)} async-done(((bf16[128,2048]{1,0:T(8,128)(2,1)}), bf16[1024,2048]{1,0:T(8,128)(2,1)}) %all-gather.10.cloned.1.call-update) | async-done | bytes 4194320 | tf_op jit(solution)/shard_map/all_gather | solution.py:137
  329.4 6.4 copy.123
  335.8 31.4 while.47
  340.6 6.1 fusion.280
  346.7 4.7 exponential_reduce_fusion.2
  356.3 6.1 fusion.280
  362.4 4.7 exponential_reduce_fusion.2
  367.2 27.8 while.48
  374.1 6.7 fusion.289
  387.8 7.0 fusion.289
  396.4 11.7 all-gather.14.cloned.1.call-done
  408.0 5.4 fusion.185
  413.7 190.6 %all-gather.16.cloned.1.call-done = bf16[2048,8192]{1,0:T(8,128)(2,1)} async-done(((bf16[64,8192]{1,0:T(8,128)(2,1)}), bf16[2048,8192]{1,0:T(8,128)(2,1)}) %all-gather.16.cloned.1.call-update) | async-done | bytes 33554448 | tf_op jit(solution)/shard_map/all_gather | solution.py:192
  604.3 18.0 convolution_add_fusion
  622.3 177.8 %all-gather.18.cloned.1.call-done = bf16[8192,2048]{1,0:T(8,128)(2,1)} async-done(((bf16[256,2048]{1,0:T(8,128)(2,1)}), bf16[8192,2048]{1,0:T(8,128)(2,1)}) %all-gather.18.cloned.1.call-update) | async-done | bytes 33554448 | tf_op jit(solution)/shard_map/all_gather | solution.py:193
  800.1 27.3 convert_reduce_fusion
  827.4 19.9 multiply_reduce_fusion.2
  849.8 7.5 convolution_convert_fusion
  858.8 74.5 %while.46 = (s32[]{:T(128)}, bf16[2,512,4096]{2,1,0:T(8,128)(2,1)}, s32[128]{0:T(128)}, s32[2]{0:T(128)S(1)}, s32[1024]{0:T(1024)S(1)}, /*index=5*/s32[1024]{0:T...) while((s32[]{:T(128)}, bf16[2,512,4096]{2,1,0:T(8,128)(2,1)}, ...), condition=%wide.region_23.24_spmd.clone, body=%wide.region_22.23_spmd.clone.sunk | while | flops 1107612160 | bytes 78452888 | solution.py:274
  864.3 5.6 fusion.272
  869.9 7.7 fusion.274
  877.7 5.1 fusion.273
  885.0 6.4 copy.165
  901.5 5.6 fusion.272
  907.2 7.7 fusion.274
  914.9 5.1 fusion.273
  922.2 6.4 copy.165
  928.6 4.6 constant_dynamic-update-slice_fusion.2
  934.6 8.6 fusion.178
  944.2 45.9 while.49
  956.8 10.1 fusion.300
  979.8 10.3 fusion.300
  991.9 88.7 %reduce-scatter.6.cloned.1.call-done = bf16[128,4096]{1,0:T(8,128)(2,1)} async-done(((bf16[1024,4096]{1,0:T(8,128)(2,1)}), bf16[128,4096]{1,0:T(8,128)(2,1)}) %reduce-scatter.6.cloned.1.call-update) | async-done | bytes 1048592 | tf_op jit(solution)/shard_map/reduce_scatter | solution.py:275
  1080.6 21.4 fusion.168
  1103.9 23.6 fusion.183
  1131.5 23.5 fusion.188
  1155.8 14.9 multiply_reduce_fusion.1
  1170.8 14.0 fusion.166
  1184.9 47.6 %all-reduce.20 = (f32[2048]{0:T(1024)S(1)}, f32[2048]{0:T(1024)S(1)}, f32[2048]{0:T(1024)S(1)}, f32[2048]{0:T(1024)S(1)}, f32[2048]{0:T(1024)S(1)}, /*index=5*/f...) all-reduce(f32[2048]{0:T(1024)S(1)} %get-tuple-element.915, ...), channel_id=7, replica_groups=mesh['dp'=4,'fsdp'=8] {'dp','fsdp'}, use_global_device_ids=true, to_apply=%region_32.33.clone | all-reduce | flops 24578 | bytes 196624
  1240.9 201.2 %reduce-scatter.10.cloned.1.call-done = f32[64,2048]{1,0:T(8,128)} async-done(((f32[2048,2048]{1,0:T(8,128)}), f32[64,2048]{1,0:T(8,128)}) %reduce-scatter.10.cloned.1.call-update) | async-done | bytes 524304 | tf_op jit(solution)/shard_map/reduce_scatter | solution.py:305
  1442.1 438.9 %reduce-scatter.8.cloned.1.call-done = f32[64,6144]{1,0:T(8,128)} async-done(((f32[2048,6144]{1,0:T(8,128)}), f32[64,6144]{1,0:T(8,128)}) %reduce-scatter.8.cloned.1.call-update) | async-done | bytes 1572880 | tf_op jit(solution)/shard_map/reduce_scatter | solution.py:305
  1881.0 1404.4 %reduce-scatter.12.cloned.1.call-done = f32[64,8192]{1,0:T(8,128)} async-done(((f32[2048,8192]{1,0:T(8,128)}), f32[64,8192]{1,0:T(8,128)}) %reduce-scatter.12.cloned.1.call-update) | async-done | bytes 2097168 | tf_op jit(solution)/shard_map/reduce_scatter | solution.py:220
  3285.4 1405.6 %reduce-scatter.14.cloned.1.call-done = f32[256,2048]{1,0:T(8,128)} async-done(((f32[8192,2048]{1,0:T(8,128)}), f32[256,2048]{1,0:T(8,128)}) %reduce-scatter.14.cloned.1.call-update) | async-done | bytes 2097168 | tf_op jit(solution)/shard_map/reduce_scatter | solution.py:221
  (308 shorter events, 112.0 us)
Async XLA Ops:
  7.2 162.6 %all-gather.8.cloned.1.call-start = ((), (), s32[]{:S(2)}) async-start(), calls=%async_computation.5 | async-start | bytes 25952256 | tf_op jit(solution)/shard_map/all_gather | solution.py:88
  7.9 253.9 %all-gather.12.cloned.1.call-start = ((), (), s32[]{:S(2)}) async-start(), calls=%async_computation.7 | async-start | bytes 4718592 | tf_op jit(solution)/shard_map/all_gather | solution.py:136
  58.6 111.2 %copy-start.19 = (f32[2048]{0:T(1024)}, f32[2048]{0:T(1024)S(1)}, u32[]{:S(2)}) copy-start(f32[2048]{0:T(1024)S(1)} %convert_element_type.145) | copy-start | bytes 24580
  58.6 111.2 %copy-start.23 = (f32[2048]{0:T(1024)}, f32[2048]{0:T(1024)S(1)}, u32[]{:S(2)}) copy-start(f32[2048]{0:T(1024)S(1)} %convert_element_type.146) | copy-start | bytes 24580
  59.9 109.9 %copy-start.35 = (f32[128]{0:T(128)}, f32[128]{0:T(128)S(1)}, u32[]{:S(2)}) copy-start(f32[128]{0:T(128)S(1)} %broadcast_multiply_fusion.5) | copy-start | bytes 1540
  61.2 108.6 %copy-start.37 = (f32[128]{0:T(128)}, f32[128]{0:T(128)S(1)}, u32[]{:S(2)}) copy-start(f32[128]{0:T(128)S(1)} %add_rsqrt_fusion.1) | copy-start | bytes 1540
  181.7 3.7 copy-start.40
  181.7 5.3 copy-start.16
  181.7 12.6 copy-start.41
  182.8 146.5 %all-gather.10.cloned.1.call-start = ((), (), s32[]{:S(2)}) async-start(), calls=%async_computation.6 | async-start | bytes 4718592 | tf_op jit(solution)/shard_map/all_gather | solution.py:137
  183.6 224.5 %all-gather.14.cloned.1.call-start = ((), (), s32[]{:S(2)}) async-start(), calls=%async_computation.8 | async-start | bytes 8650752 | tf_op jit(solution)/shard_map/all_gather | solution.py:89
  184.2 420.1 %all-gather.16.cloned.1.call-start = ((), (), s32[]{:S(2)}) async-start(), calls=%async_computation.9 | async-start | bytes 34603008 | tf_op jit(solution)/shard_map/all_gather | solution.py:192
  184.7 615.4 %all-gather.18.cloned.1.call-start = ((), (), s32[]{:S(2)}) async-start(), calls=%async_computation.10 | async-start | bytes 34603008 | tf_op jit(solution)/shard_map/all_gather | solution.py:193
  185.3 895.2 %reduce-scatter.6.cloned.1.call-start = ((), (), s32[]{:S(2)}) async-start(), calls=%async_computation.11 | async-start | bytes 9437184 | tf_op jit(solution)/shard_map/reduce_scatter | solution.py:275
  194.3 652.9 %copy-start.17 = (f32[2048]{0:T(1024)}, f32[2048]{0:T(1024)S(1)}, u32[]{:S(2)}) copy-start(f32[2048]{0:T(1024)S(1)} %convert_element_type.155) | copy-start | bytes 24580
  194.4 409.9 %copy-start.21 = (f32[2048]{0:T(1024)}, f32[2048]{0:T(1024)S(1)}, u32[]{:S(2)}) copy-start(f32[2048]{0:T(1024)S(1)} %convert_element_type.156) | copy-start | bytes 24580
  367.2 40.9 copy-start.3
  374.1 6.8 copy-start.43
  387.8 7.1 copy-start.43
  396.3 17.1 copy-start.9
  408.0 196.3 %copy-start.25 = (f32[32,1,256]{2,1,0:T(1,128)S(1)}, f32[32,1,256]{2,1,0:T(1,128)}, u32[]{:S(2)}) copy-start(f32[32,1,256]{2,1,0:T(1,128)} %convert_element_type.174) | copy-start | bytes 98308
  413.5 433.8 %copy-start.1 = (f32[128,2048]{1,0:T(8,128)}, f32[128,2048]{1,0:T(8,128)S(1)}, u32[]{:S(2)}) copy-start(f32[128,2048]{1,0:T(8,128)S(1)} %get-tuple-element.1082) | copy-start | bytes 3145732
  413.5 433.8 %copy-start.26 = (f32[128]{0:T(128)}, f32[128]{0:T(128)S(1)}, u32[]{:S(2)}) copy-start(f32[128]{0:T(128)S(1)} %broadcast_multiply_fusion.4) | copy-start | bytes 1540
  413.7 433.6 %copy-start.28 = (f32[128]{0:T(128)}, f32[128]{0:T(128)S(1)}, u32[]{:S(2)}) copy-start(f32[128]{0:T(128)S(1)} %add_rsqrt_fusion) | copy-start | bytes 1540
  604.3 195.8 %copy-start.13 = (bf16[128,2048]{1,0:T(8,128)(2,1)S(1)}, bf16[128,2048]{1,0:T(8,128)(2,1)}, u32[]{:S(2)}) copy-start(bf16[128,2048]{1,0:T(8,128)(2,1)} %param.27) | copy-start | bytes 1572868
  849.8 7.5 copy-start.5
  849.8 8.8 copy-start.11
  877.7 5.1 copy-start
  914.9 5.1 copy-start
  933.2 508.8 %reduce-scatter.10.cloned.1.call-start = ((), (), s32[]{:S(2)}) async-start(), calls=%async_computation.13 | async-start | bytes 17301504 | tf_op jit(solution)/shard_map/reduce_scatter | solution.py:305
  943.2 937.8 %reduce-scatter.8.cloned.1.call-start = ((), (), s32[]{:S(2)}) async-start(), calls=%async_computation.12 | async-start | bytes 51904512 | tf_op jit(solution)/shard_map/reduce_scatter | solution.py:305
  944.2 136.4 %copy-start.20 = (f32[2048]{0:T(1024)S(1)}, f32[2048]{0:T(1024)}, u32[]{:S(2)}) copy-start(f32[2048]{0:T(1024)} %copy-done.19) | copy-start | bytes 24580
  944.2 136.4 %copy-start.24 = (f32[2048]{0:T(1024)S(1)}, f32[2048]{0:T(1024)}, u32[]{:S(2)}) copy-start(f32[2048]{0:T(1024)} %copy-done.23) | copy-start | bytes 24580
  991.9 110.1 %copy-start.15 = (bf16[128,2048]{1,0:T(8,128)(2,1)}, bf16[128,2048]{1,0:T(8,128)(2,1)S(1)}, u32[]{:S(2)}) copy-start(bf16[128,2048]{1,0:T(8,128)(2,1)S(1)} %copy.131) | copy-start | bytes 1572868
  1101.9 1.9 copy-start.8
  1102.0 2183.4 %reduce-scatter.12.cloned.1.call-start = ((), (), s32[]{:S(2)}) async-start(), calls=%async_computation.14 | async-start | bytes 69206016 | tf_op jit(solution)/shard_map/reduce_scatter | solution.py:220
  1127.4 3563.6 %reduce-scatter.14.cloned.1.call-start = ((), (), s32[]{:S(2)}) async-start(), calls=%async_computation.15 | async-start | bytes 69206016 | tf_op jit(solution)/shard_map/reduce_scatter | solution.py:221
  1127.5 4.0 copy-start.14
  1155.7 14.9 copy-start.12
  1155.7 15.0 copy-start.36
  1155.8 15.0 copy-start.38
  1170.7 14.1 copy-start.30
  1170.7 14.1 copy-start.31
  1170.7 14.1 copy-start.32
  1170.8 14.1 copy-start.33
  1170.8 14.1 copy-start.34
  1170.8 68.9 %copy-start.4 = (bf16[128,2048]{1,0:T(8,128)(2,1)S(1)}, bf16[128,2048]{1,0:T(8,128)(2,1)}, u32[]{:S(2)}) copy-start(bf16[128,2048]{1,0:T(8,128)(2,1)} %param.26) | copy-start | bytes 1572868
  1170.8 68.9 %copy-start.7 = (f32[128,2048]{1,0:T(8,128)S(1)}, f32[128,2048]{1,0:T(8,128)}, u32[]{:S(2)}) copy-start(f32[128,2048]{1,0:T(8,128)} %copy-done.5) | copy-start | bytes 3145732
  (10 other events, 14.8 us)
Sparse Core Ops, SparseCore 0:
  10.9 158.8 all-gather.7
  183.0 71.9 all-gather.11
  257.7 71.6 all-gather.9
  332.2 75.7 all-gather.13
  410.9 193.3 all-gather.15
  607.1 192.9 all-gather.17
  933.4 147.1 reduce-scatter.5
  1083.5 358.5 reduce-scatter.9
  1450.2 430.7 reduce-scatter.7
  1883.9 1401.4 reduce-scatter.11
  3288.5 1402.5 reduce-scatter.13
where the time goes:
time: 4710 us; the launch traced here: 4700 us
  waiting for transfers between devices  4090 us (87%)
  matrix products  298 us (6%)
  blocking collectives  158 us (3%)
  local copies, waits for them, and re-layouts  88.6 us (2%)
    reduce_scatter x1, waiting for transfers between devices, per_device(): lax.psum_scatter(grad_down_w, ('dp', 'fsdp'), scatter_dimension=0, tiled=...  1410 us
    reduce_scatter x1, waiting for transfers between devices, per_device(): lax.psum_scatter(grad_up_w, ('dp', 'fsdp'), scatter_dimension=0, tiled=True)  1400 us
    reduce_scatter x2, waiting for transfers between devices, per_device(): lax.psum_scatter((grad_qkv_w, grad_out_w) + small_grads, ('dp', 'fsdp'),...  640 us
    all_gather x1, waiting for transfers between devices, per_device(): lax.all_gather(w_up, ('dp', 'fsdp'), axis=0, tiled=True)  191 us
    all_gather x1, waiting for transfers between devices, per_device(): lax.all_gather(w_down, ('dp', 'fsdp'), axis=0, tiled=True)  178 us
    all_gather x1, waiting for transfers between devices, per_device(): lax.all_gather(w_qkv, ('dp', 'fsdp'), axis=0, tiled=True)  109 us
  transfers between devices with their start and end apart: 11, of which 10 were waited for; matrix products, arithmetic and copies ran while one was open for 6% of the time, Pallas kernels for 0%

commit v1 on v0

v1 whole, which is shorter than its diff:
```python
import jax
import jax.numpy as jnp
from jax import lax
from jax.sharding import PartitionSpec as P

H = 32
HD = 64
BLK = 32

EPSILON = 1e-05
MASKED = -1e30
BF = jnp.bfloat16
F32 = jnp.float32
BOTH = ("dp", "fsdp")


def norm_parts(values):
    center = values - jnp.mean(values, axis=-1, keepdims=True)
    inverse = lax.rsqrt(jnp.mean(center * center, axis=-1, keepdims=True) + EPSILON)
    return (center * inverse, inverse)


def norm_back(grad_normed, normed, inverse):
    mean_grad = jnp.mean(grad_normed, axis=-1, keepdims=True)
    mean_cross = jnp.mean(grad_normed * normed, axis=-1, keepdims=True)
    return inverse * (grad_normed - mean_grad - normed * mean_cross)


def tree_tables(parents, seg_blocks, valid):
    segments = parents.shape[0]
    seg_tokens = jnp.broadcast_to(seg_blocks[:, None], (seg_blocks.shape[0], BLK)).reshape(-1)
    labels = jnp.arange(segments, dtype=jnp.int32)
    member = (seg_tokens[:, None] == labels[None, :]).astype(jnp.int32)
    counted = member * valid[:, None]
    before = jnp.cumsum(counted, axis=0) - counted
    rank = jnp.sum(before * member, axis=1)
    seg_len = jnp.sum(counted, axis=0)
    picked = (parents[:, None] == labels[None, :]).astype(jnp.int32)
    grand = jnp.sum(picked * parents[None, :], axis=1)
    ancestor = ((labels[None, :] == parents[:, None]) | (labels[None, :] == grand[:, None])) & (
        labels[None, :] != labels[:, None]
    )
    offset = jnp.sum(ancestor.astype(jnp.int32) * seg_len[None, :], axis=1)
    position = jnp.sum(member * offset[None, :], axis=1) + rank
    return (seg_tokens, position, ancestor.astype(jnp.float32))


def allowed_mask(seg, index, valid, ancestor):
    labels = jnp.arange(ancestor.shape[0], dtype=jnp.int32)
    member = (seg[:, None] == labels[None, :]).astype(jnp.float32)
    reach = jnp.dot(jnp.dot(member, ancestor), member.T) > 0.5
    causal = (seg[:, None] == seg[None, :]) & (index[None, :] <= index[:, None])
    visible = (valid[None, :] == 1) | (index[None, :] == index[:, None])
    return (reach | causal) & visible


def gelu_exact(value):
    return jax.nn.gelu(value, approximate=False)


def mm(spec, a, b):
    return jnp.einsum(spec, a, b, preferred_element_type=F32)


def gather_tokens(x):
    return lax.all_gather(x, "fsdp", axis=0, tiled=True)


def scatter_tokens(x):
    return lax.psum_scatter(x.astype(BF), "fsdp", scatter_dimension=0, tiled=True).astype(F32)


def scatter_dp(x):
    return lax.psum_scatter(x, "dp", scatter_dimension=0, tiled=True)


def gather_dp(x):
    return lax.all_gather(x, "dp", axis=0, tiled=True)


def per_device(
    layer_in,
    cotangent,
    w_qkv,
    w_out,
    w_up,
    w_down,
    gain_attn,
    shift_attn,
    bias_query,
    bias_value,
    bias_out,
    gain_mlp,
    shift_mlp,
    bias_up,
    bias_down,
    parents,
    seg_blocks,
    token_valid,
):
    rows, width = layer_in.shape
    dp, fsdp = lax.axis_size("dp"), lax.axis_size("fsdp")
    devices = dp * fsdp
    rank = lax.axis_index("fsdp")
    heads = H // fsdp
    cols = heads * HD
    tree = token_valid.shape[1]
    part = w_qkv.shape[0]
    unit = w_down.shape[0]

    vec = jnp.concatenate(
        [gain_attn, shift_attn, bias_query, bias_value, bias_out, gain_mlp, shift_mlp, bias_down, bias_up]
    )
    vec = lax.all_gather(vec, BOTH, axis=0, tiled=False).astype(F32)
    (gain_one, shift_one, query_bias, value_bias, out_bias, gain_two, shift_two, down_bias) = [
        vec[:, i * part : (i + 1) * part].reshape(-1) for i in range(8)
    ]
    up_bias = vec[:, 8 * part :].reshape(dp, fsdp, unit)
    up_bias = lax.dynamic_index_in_dim(up_bias, rank, 1, keepdims=False).reshape(-1)

    inputs = layer_in.astype(F32)
    normed_one, inverse_one = norm_parts(inputs)
    attn_in = gather_tokens((normed_one * gain_one + shift_one).astype(BF))

    def to_rank(w):
        return gather_dp(lax.all_to_all(w, "fsdp", split_axis=2, concat_axis=0, tiled=True))

    qkv_w = to_rank(w_qkv.reshape(part, 3, fsdp, cols)).reshape(width, 3 * cols)
    out_w = lax.all_gather(w_out, BOTH, axis=0, tiled=True)
    up_w = to_rank(w_up.reshape(part, dp, fsdp, unit)).reshape(width, dp * unit)
    down_w = gather_dp(w_down)
    cot = gather_tokens(cotangent)

    def own_cols(v):
        return lax.dynamic_slice_in_dim(v, rank * cols, cols, 0)

    joined_bias = jnp.concatenate([own_cols(query_bias), jnp.zeros((cols,), F32), own_cols(value_bias)])
    joined = (jnp.dot(attn_in, qkv_w, preferred_element_type=F32) + joined_bias).astype(BF)
    joined = joined.reshape(tree, 3, heads, HD)
    queries, keys, values = joined[:, 0], joined[:, 1], joined[:, 2]

    valid = token_valid[0]
    seg, position, ancestor = tree_tables(parents[0], seg_blocks[0], valid)
    index = jnp.arange(tree, dtype=jnp.int32)
    mask = allowed_mask(seg, index, valid, ancestor)
    distance = (position[:, None] - position[None, :]).astype(F32)
    numbers = (rank * heads + jnp.arange(heads)).astype(F32)
    slopes = jnp.exp2(-8.0 * (numbers + 1.0) / H)
    raw = mm("qhd,khd->hqk", queries, keys)
    logits = jnp.where(mask[None], raw * HD ** (-0.5) - slopes[:, None, None] * distance[None], MASKED)
    peak = jnp.max(logits, axis=-1, keepdims=True)
    weights = jnp.exp(logits - peak)
    probs = weights / jnp.sum(weights, axis=-1, keepdims=True)
    probs_low = probs.astype(BF)
    mixed = mm("hqk,khd->qhd", probs_low, values).reshape(tree, cols).astype(BF)

    mixed_own = lax.all_to_all(mixed, "fsdp", split_axis=0, concat_axis=1, tiled=True)
    branch = jnp.dot(mixed_own, out_w, preferred_element_type=F32) + out_bias
    middle = inputs + branch
    normed_two, inverse_two = norm_parts(middle)
    mlp_in = gather_tokens((normed_two * gain_two + shift_two).astype(BF))
    hidden = jnp.dot(mlp_in, up_w, preferred_element_type=F32) + up_bias
    active_float, gelu_pull = jax.vjp(gelu_exact, hidden)
    active = active_float.astype(BF)
    grad_active = mm("td,fd->tf", cot, down_w)
    grad_hidden = gelu_pull(grad_active)[0].astype(BF)
    grad_mlp_in = scatter_tokens(mm("tf,df->td", grad_hidden, up_w))
    update = scatter_tokens(jnp.dot(active, down_w, preferred_element_type=F32)) + down_bias
    result = middle + update

    cot_own = cotangent.astype(F32)
    grad_middle = cot_own + norm_back(grad_mlp_in * gain_two, normed_two, inverse_two)
    grad_branch = grad_middle.astype(BF)
    grad_mixed = mm("te,de->td", grad_branch, out_w).astype(BF)
    grad_heads = lax.all_to_all(grad_mixed, "fsdp", split_axis=1, concat_axis=0, tiled=True)
    grad_heads = grad_heads.reshape(tree, heads, HD)
    grad_probs = mm("qhd,khd->hqk", grad_heads, values)
    delta = jnp.sum(probs * grad_probs, axis=-1, keepdims=True)
    grad_raw = (probs * (grad_probs - delta) * HD ** (-0.5)).astype(BF)
    grad_q = mm("hqk,khd->qhd", grad_raw, keys)
    grad_k = mm("hqk,qhd->khd", grad_raw, queries)
    grad_v = mm("hqk,qhd->khd", probs_low, grad_heads)
    grad_joined = jnp.stack([grad_q, grad_k, grad_v], axis=1).reshape(tree, 3 * cols).astype(BF)
    grad_attn_in = scatter_tokens(mm("te,de->td", grad_joined, qkv_w))
    grad_inputs = grad_middle + norm_back(grad_attn_in * gain_one, normed_one, inverse_one)

    def to_owner(g, outer, inner):
        g = scatter_dp(g.astype(BF)).reshape(fsdp, part, outer * inner)
        g = lax.all_to_all(g, "fsdp", split_axis=0, concat_axis=0, tiled=True)
        g = g.reshape(fsdp, part, outer, inner).transpose(1, 2, 0, 3)
        return g.reshape(part, outer * fsdp * inner).astype(F32)

    grad_down_w = scatter_dp(mm("tf,td->fd", active, cot).astype(BF)).astype(F32)
    grad_up_w = to_owner(mm("td,tf->df", mlp_in, grad_hidden), dp, unit)
    grad_out_w = scatter_dp(mm("td,te->de", mixed_own, grad_branch).astype(BF))
    grad_out_w = lax.psum_scatter(grad_out_w, "fsdp", scatter_dimension=0, tiled=True).astype(F32)
    grad_qkv_w = to_owner(mm("td,te->de", attn_in, grad_joined), 3, cols)

    col = jnp.sum(grad_joined.astype(F32), axis=0)

    def spread(v):
        return lax.dynamic_update_slice_in_dim(jnp.zeros((width,), F32), v, rank * cols, 0)

    smalls = [
        jnp.sum(grad_attn_in * normed_one, axis=0),
        jnp.sum(grad_attn_in, axis=0),
        spread(col[:cols]),
        spread(col[2 * cols :]),
        jnp.sum(grad_branch.astype(F32), axis=0),
        jnp.sum(grad_mlp_in * normed_two, axis=0),
        jnp.sum(grad_mlp_in, axis=0),
        jnp.sum(cot_own, axis=0),
    ]
    grad_bias_up = jnp.sum(grad_hidden.astype(F32), axis=0)
    grad_bias_up = lax.dynamic_update_slice_in_dim(
        jnp.zeros((dp, fsdp, unit), F32), grad_bias_up.reshape(dp, 1, unit), rank, 1
    )
    packed = jnp.concatenate(
        [v.reshape(devices, part) for v in smalls] + [grad_bias_up.reshape(devices, unit)], axis=1
    )
    packed = lax.psum_scatter(packed, BOTH, scatter_dimension=0, tiled=True)[0]
    small = [packed[i * part : (i + 1) * part] for i in range(8)]
    squares = lax.psum(jnp.stack([jnp.sum(result * result), jnp.sum(branch * branch)]), BOTH)
    root_squares = jnp.sqrt(squares / (devices * rows * width))
    return (
        result.astype(BF),
        grad_inputs.astype(BF),
        grad_qkv_w,
        grad_out_w,
        grad_up_w,
        grad_down_w,
        small[0],
        small[1],
        small[2],
        small[3],
        small[4],
        small[5],
        small[6],
        packed[8 * part :],
        small[7],
        root_squares,
    )


def solution(mesh):
    matrix, vector, table = P(BOTH, None), P(BOTH), P("dp", None)
    return jax.shard_map(
        per_device,
        mesh=mesh,
        in_specs=(matrix,) * 6 + (vector,) * 9 + (table,) * 3,
        out_specs=(matrix,) * 6 + (vector,) * 9 + (P(),),
        check_vma=False,
    )
```

time: 4710 us -> 1290 us (0.27)
  waiting for transfers between devices: 4090 us -> 835 us
  matrix products: 298 us -> 192 us
    reduce_scatter x5 -> x8, waiting for transfers between devices: 3540 us -> 417 us  [the longest x3 235 us: scatter_tokens(): lax.psum_scatter(x.astype(BF), 'fsdp', scatter_dimension=0, tiled=True)]
    all_gather x6 -> x7, waiting for transfers between devices: 550 us -> 255 us  [the longest x3 174 us: gather_tokens(): return lax.all_gather(x, 'fsdp', axis=0, tiled=True)]
    dot_general x34 -> x18, matrix products: 298 us -> 179 us  [the longest x13 148 us: mm(): return jnp.einsum(spec, a, b, preferred_element_type=F32)]
    unnamed x11 -> x17, waiting for transfers between devices: 3.04 us -> 111 us
    unnamed x2 -> x0, blocking collectives: 91.4 us -> none
    all_to_all x0 -> x4, waiting for transfers between devices: none -> 52.4 us  [the longest x1 33.8 us: to_rank(): lax.all_to_all(w, 'fsdp', split_axis=2, concat_axis=0, tiled=True)]
  transfers between devices with their start and end apart: 11 -> 20, of which waited for: 10 -> 15; matrix products, arithmetic and copies ran while one was open for 6% -> 18% of each run, Pallas kernels for 0% -> 0%
where the time goes in v1:
time: 1290 us; the launch traced here: 1280 us
  waiting for transfers between devices  835 us (65%)
  matrix products  192 us (15%)
  blocking collectives  154 us (12%)
  local copies, waits for them, and re-layouts  43.7 us (3%)
  other arithmetic  25.9 us (2%)
  starting transfers between devices  17.7 us (1%)
  between operations  14.8 us (1%)
    reduce_scatter x3, waiting for transfers between devices, scatter_tokens(): lax.psum_scatter(x.astype(BF), 'fsdp', scatter_dimension=0, tiled=True)  235 us
    all_gather x3, waiting for transfers between devices, gather_tokens(): return lax.all_gather(x, 'fsdp', axis=0, tiled=True)  174 us
    dot_general x13, matrix products, mm(): return jnp.einsum(spec, a, b, preferred_element_type=F32)  148 us
    reduce_scatter x4, waiting for transfers between devices, scatter_dp(): return lax.psum_scatter(x, 'dp', scatter_dimension=0, tiled=True)  112 us
    unnamed x17, waiting for transfers between devices  111 us
    reduce_scatter x1, waiting for transfers between devices, per_device(): lax.psum_scatter(grad_out_w, 'fsdp', scatter_dimension=0, tiled=True)  69.5 us
    all_gather x1, blocking collectives, per_device(): vec = lax.all_gather(vec, BOTH, axis=0, tiled=False).astype(F32)  66.5 us
    all_gather x3, waiting for transfers between devices, gather_dp(): return lax.all_gather(x, 'dp', axis=0, tiled=True)  51.2 us
  transfers between devices with their start and end apart: 20, of which 15 were waited for; matrix products, arithmetic and copies ran while one was open for 18% of the time, Pallas kernels for 0%

profile of v1, /device:TPU:0, one launch (start us, length us, event | category | flops | bytes accessed | tf_op | source)
XLA Modules:
  0.0 1282.9 jit_solution(17886919629627529330)
XLA Ops:
  8.9 27.4 %all_to_all.78 = bf16[64,3,8,256]{3,0,1,2:T(8,128)(2,1)S(1)} all-to-all(bf16[64,3,8,256]{3,0,1,2:T(8,128)(2,1)S(1)} %copy.107), channel_id=1, replica_groups=mesh['dp'=4,'fsdp'=8] {'fsdp'}, dimensions={2} | all-to-all | bytes 1572864 | tf_op jit(solution)/shard_map/all_to_all | solution.py:126
  37.5 66.5 %all-gather.1 = bf16[32,1,768]{2,1,0:T(2,128)(2,1)S(1)} all-gather(bf16[1,1,768]{2,1,0:T(2,128)(2,1)S(1)} %reshape.298), channel_id=2, replica_groups=mesh['dp'=4,'fsdp'=8] {'dp','fsdp'}, dimensions={0}, use_global_device_ids=true | all-gather | bytes 50688 | tf_op jit(solution)/shard_map/all_gather | solution.py:114
  108.4 3.6 all-to-all-start.2
  113.6 3.7 reduce-window.6
  117.9 33.8 %all-to-all-done.2 = bf16[64,4,8,256]{3,1,0,2:T(4,128)(2,1)S(1)} async-done(((bf16[64,4,8,256]{3,1,0,2:T(4,128)(2,1)}), bf16[64,4,8,256]{3,1,0,2:T(4,128)(2,1)S(1)}, u32[]{:S(2)}, u32[]{:S(2)}) %all-to-all-start.2) | async-done | bytes 1048608 | tf_op jit(solution)/shard_map/all_to_all | solution.py:126
  159.6 4.7 copy.109
  164.4 29.3 %all-gather.10.cloned.1.call-done = bf16[1024,2048]{1,0:T(8,128)(2,1)} async-done(((bf16[128,2048]{1,0:T(8,128)(2,1)}), bf16[1024,2048]{1,0:T(8,128)(2,1)}) %all-gather.10.cloned.1.call-update) | async-done | bytes 4194320 | tf_op jit(solution)/shard_map/all_gather | solution.py:66
  193.6 7.8 add_convert_fusion.1
  201.4 13.2 %fusion.94 = (f32[4,1024]{1,0:T(4,128)S(1)}, f32[4,1024,1024]{1,2,0:T(8,128)}) fusion(f32[1024,1024]{0,1:T(8,128)} %subtract_convert_fusion, f32[4]{0:T(128)S(1)} %multiply_exponential_fusion, pred[1024,1024]{0,1:T(8,128)(4,1)S(1)} %copy.110, bf16[1024,3,4,64]{0,3,2,1:T(8,128)(2,1)} %bitcast.185), kind=kOutput, calls=%fused_computation.164 | convolution fusion | flops 562037760 | bytes 23085072 | tf_op jit(solution)/shard_map/sub | solution.py:152
  214.6 10.5 fusion.48
  226.1 3.5 all-to-all-start.1
  229.9 18.6 %all-to-all-done.1 = bf16[8,128,256]{1,2,0:T(8,128)(2,1)S(1)} async-done(((bf16[8,128,256]{1,2,0:T(8,128)(2,1)}), bf16[8,128,256]{1,2,0:T(8,128)(2,1)S(1)}, u32[]{:S(2)}, u32[]{:S(2)}) %all-to-all-start.1) | async-done | bytes 524320 | tf_op jit(solution)/shard_map/all_to_all | solution.py:157
  248.5 29.8 %all-gather.14.cloned.1.call-done = bf16[2048,2048]{1,0:T(8,128)(2,1)} async-done(((bf16[64,2048]{1,0:T(8,128)(2,1)}), bf16[2048,2048]{1,0:T(8,128)(2,1)}) %all-gather.14.cloned.1.call-update) | async-done | bytes 8388624 | tf_op jit(solution)/shard_map/all_gather | solution.py:129
  278.2 5.4 fusion.91
  286.4 27.0 %all-gather.18.cloned.1.call-done = bf16[2048,4,1,256]{3,0,1,2:T(8,128)(2,1)} async-done(((bf16[512,4,1,256]{3,0,1,2:T(8,128)(2,1)}), bf16[2048,4,1,256]{3,0,1,2:T(8,128)(2,1)}) %all-gather.18.cloned.1.call-update) | async-done | bytes 4194320 | tf_op jit(solution)/shard_map/all_gather | solution.py:78
  313.4 6.7 copy.117
  320.1 69.2 %all-gather.16.cloned.1.call-done = bf16[1024,2048]{1,0:T(8,128)(2,1)} async-done(((bf16[128,2048]{1,0:T(8,128)(2,1)}), bf16[1024,2048]{1,0:T(8,128)(2,1)}) %all-gather.16.cloned.1.call-update) | async-done | bytes 4194320 | tf_op jit(solution)/shard_map/all_gather | solution.py:66
  389.3 9.9 fusion.95
  399.2 24.2 %all-gather.20.cloned.1.call-done = bf16[1024,2048]{1,0:T(8,128)(2,1)} async-done(((bf16[256,2048]{1,0:T(8,128)(2,1)}), bf16[1024,2048]{1,0:T(8,128)(2,1)}) %all-gather.20.cloned.1.call-update) | async-done | bytes 4194320 | tf_op jit(solution)/shard_map/all_gather | solution.py:78
  423.5 75.6 %all-gather.22.cloned.1.call-done = bf16[1024,2048]{1,0:T(8,128)(2,1)} async-done(((bf16[128,2048]{1,0:T(8,128)(2,1)}), bf16[1024,2048]{1,0:T(8,128)(2,1)}) %all-gather.22.cloned.1.call-update) | async-done | bytes 4194320 | tf_op jit(solution)/shard_map/all_gather | solution.py:66
  499.0 18.0 %convert_reduce_fusion = (f32[1024]{0:T(1024)S(1)}, bf16[1024,1024]{1,0:T(8,128)(2,1)}, f32[1024,1024]{1,0:T(8,128)S(1)}) fusion(f32[1024,1024]{1,0:T(8,128)} %fusion.95, f32[1024]{0:T(1024)S(1)} %bitcast.196, bf16[1024,2048]{1,0:T(8,128)(2,1)} %all-gather.22.cloned.1.call-done, bf16[1024,2048]{1,0:T(8,128)(2,1)} %all-gather.20.cloned.1.call-done), kind=kOutput, calls=%fused_computation.19 | convolution fusion | flops 4373609472 | bytes 18882560 | tf_op jit(solution)/shard_map/td,fd->tf/dot_general | solution.py:62
  519.6 6.1 convolution_convert_fusion.5
  525.9 9.4 convolution_convert_fusion.4
  535.3 9.4 convolution_convert_fusion.3
  544.9 67.1 %reduce-scatter.9.cloned.1.call-done = bf16[128,2048]{1,0:T(8,128)(2,1)} async-done(((bf16[1024,2048]{1,0:T(8,128)(2,1)}), bf16[128,2048]{1,0:T(8,128)(2,1)}) %reduce-scatter.9.cloned.1.call-update) | async-done | bytes 524304 | tf_op jit(solution)/shard_map/reduce_scatter | solution.py:70
  612.0 91.8 %reduce-scatter.11.cloned.1.call-done = bf16[128,2048]{1,0:T(8,128)(2,1)} async-done(((bf16[1024,2048]{1,0:T(8,128)(2,1)}), bf16[128,2048]{1,0:T(8,128)(2,1)}) %reduce-scatter.11.cloned.1.call-update) | async-done | bytes 524304 | tf_op jit(solution)/shard_map/reduce_scatter | solution.py:70
  703.7 3.2 fusion.68
  708.6 6.9 convolution_convert_fusion.7
  715.6 18.6 %all_to_all.79 = bf16[128,8,256]{2,0,1:T(8,128)(2,1)S(1)} all-to-all(bf16[128,8,256]{2,0,1:T(8,128)(2,1)S(1)} %bitcast.173), channel_id=1, replica_groups=mesh['dp'=4,'fsdp'=8] {'fsdp'}, dimensions={1} | all-to-all | bytes 1048576 | tf_op jit(solution)/shard_map/all_to_all | solution.py:175
  734.8 9.1 fusion.71
  743.9 22.3 %fusion.39 = bf16[1024,1,4,64]{0,3,2,1:T(8,128)(2,1)S(1)} fusion(f32[4,1024,1024]{1,2,0:T(8,128)} %fusion.71, bf16[1024,3,4,64]{0,3,2,1:T(8,128)(2,1)} %bitcast.188, f32[4,1024,1024]{1,2,0:T(8,128)} %get-tuple-element.58, f32[4,1024]{1,0:T(4,128)S(1)} %get-tuple-element.57), kind=kOutput, calls=%fused_computation.73 | convolution fusion | flops 566236160 | bytes 68190208 | tf_op jit(solution)/shard_map/hqk,khd->qhd/dot_general | solution.py:62
  766.2 22.3 %fusion.42 = bf16[1024,1,4,64]{0,3,2,1:T(8,128)(2,1)S(1)} fusion(f32[4,1024,1024]{1,2,0:T(8,128)} %fusion.71, bf16[1024,3,4,64]{0,3,2,1:T(8,128)(2,1)} %bitcast.189, f32[4,1024,1024]{1,2,0:T(8,128)} %get-tuple-element.58, f32[4,1024]{1,0:T(4,128)S(1)} %get-tuple-element.57), kind=kOutput, calls=%fused_computation.74 | convolution fusion | flops 566236160 | bytes 68190208 | tf_op jit(solution)/shard_map/hqk,qhd->khd/dot_general | solution.py:62
  788.5 11.0 fusion.45
  801.0 6.9 convolution_convert_fusion.1
  808.9 5.6 convolution_convert_fusion
  814.6 8.1 convolution_convert_fusion.6
  822.7 8.3 convolution_convert_fusion.2
  831.4 4.0 all-to-all-start.5
  836.2 76.2 %reduce-scatter.13.cloned.1.call-done = bf16[128,2048]{1,0:T(8,128)(2,1)} async-done(((bf16[1024,2048]{1,0:T(8,128)(2,1)}), bf16[128,2048]{1,0:T(8,128)(2,1)}) %reduce-scatter.13.cloned.1.call-update) | async-done | bytes 524304 | tf_op jit(solution)/shard_map/reduce_scatter | solution.py:70
  914.9 71.4 %reduce-scatter.17.cloned.1.call-done = bf16[512,2048]{1,0:T(8,128)(2,1)} async-done(((bf16[2048,2048]{1,0:T(8,128)(2,1)}), bf16[512,2048]{1,0:T(8,128)(2,1)}) %reduce-scatter.17.cloned.1.call-update) | async-done | bytes 2097168 | tf_op jit(solution)/shard_map/reduce_scatter | solution.py:74
  986.4 40.6 %reduce-scatter.15.cloned.1.call-done = bf16[512,768]{1,0:T(8,128)(2,1)} async-done(((bf16[2048,768]{1,0:T(8,128)(2,1)}), bf16[512,768]{1,0:T(8,128)(2,1)}) %reduce-scatter.15.cloned.1.call-update) | async-done | bytes 786448 | tf_op jit(solution)/shard_map/reduce_scatter | solution.py:74
  1027.0 5.5 all-to-all-start.4
  1033.9 41.6 %psum.7 = f32[2]{0:T(128)S(1)} all-reduce(f32[2]{0:T(128)S(1)} %pad_maximum_fusion.1), channel_id=1, replica_groups=mesh['dp'=4,'fsdp'=8] {'dp','fsdp'}, use_global_device_ids=true, to_apply=%region_37.38 | all-reduce | flops 2 | bytes 16 | tf_op jit(solution)/shard_map/psum | solution.py:223
  1075.5 2.8 convert_element_type.195
  1080.7 2.8 copy.124
  1083.5 2.5 copy.136
  1093.3 108.8 %all-reduce.3.cloned.1.call-done = f32[32,768]{1,0:T(8,128)} async-done(((f32[32,768]{1,0:T(8,128)}), f32[32,768]{1,0:T(8,128)}) %all-reduce.3.cloned.1.call-update) | async-done | bytes 98320
  1204.9 69.5 %reduce-scatter.19.cloned.1.call-done = bf16[64,2048]{1,0:T(8,128)(2,1)} async-done(((bf16[512,2048]{1,0:T(8,128)(2,1)}), bf16[64,2048]{1,0:T(8,128)(2,1)}) %reduce-scatter.19.cloned.1.call-update) | async-done | bytes 262160 | tf_op jit(solution)/shard_map/reduce_scatter | solution.py:196
  (198 shorter events, 48.0 us)
Async XLA Ops:
  7.2 30.1 %copy-start.21 = (bf16[64]{0:T(256)(128)(2,1)S(1)}, bf16[64]{0:T(256)(128)(2,1)}, u32[]{:S(2)}) copy-start(bf16[64]{0:T(256)(128)(2,1)} %param.24) | copy-start | bytes 388
  7.2 30.1 %copy-start.22 = (bf16[64]{0:T(256)(128)(2,1)S(1)}, bf16[64]{0:T(256)(128)(2,1)}, u32[]{:S(2)}) copy-start(bf16[64]{0:T(256)(128)(2,1)} %param.25) | copy-start | bytes 388
  7.2 30.1 %copy-start.23 = (bf16[64]{0:T(256)(128)(2,1)S(1)}, bf16[64]{0:T(256)(128)(2,1)}, u32[]{:S(2)}) copy-start(bf16[64]{0:T(256)(128)(2,1)} %param.26) | copy-start | bytes 388
  7.2 30.1 %copy-start.24 = (bf16[64]{0:T(256)(128)(2,1)S(1)}, bf16[64]{0:T(256)(128)(2,1)}, u32[]{:S(2)}) copy-start(bf16[64]{0:T(256)(128)(2,1)} %param.27) | copy-start | bytes 388
  7.2 30.1 %copy-start.25 = (bf16[64]{0:T(256)(128)(2,1)S(1)}, bf16[64]{0:T(256)(128)(2,1)}, u32[]{:S(2)}) copy-start(bf16[64]{0:T(256)(128)(2,1)} %param.28) | copy-start | bytes 388
  7.2 30.1 %copy-start.26 = (bf16[64]{0:T(256)(128)(2,1)S(1)}, bf16[64]{0:T(256)(128)(2,1)}, u32[]{:S(2)}) copy-start(bf16[64]{0:T(256)(128)(2,1)} %param.29) | copy-start | bytes 388
  7.2 30.1 %copy-start.27 = (bf16[64]{0:T(256)(128)(2,1)S(1)}, bf16[64]{0:T(256)(128)(2,1)}, u32[]{:S(2)}) copy-start(bf16[64]{0:T(256)(128)(2,1)} %param.30) | copy-start | bytes 388
  7.3 30.1 %copy-start.29 = (bf16[256]{0:T(256)(128)(2,1)S(1)}, bf16[256]{0:T(256)(128)(2,1)}, u32[]{:S(2)}) copy-start(bf16[256]{0:T(256)(128)(2,1)} %param.31) | copy-start | bytes 1540
  7.3 30.1 %copy-start.28 = (bf16[64]{0:T(256)(128)(2,1)S(1)}, bf16[64]{0:T(256)(128)(2,1)}, u32[]{:S(2)}) copy-start(bf16[64]{0:T(256)(128)(2,1)} %param.32) | copy-start | bytes 388
  7.3 97.0 %copy-start = (bf16[128,2048]{1,0:T(8,128)(2,1)S(1)}, bf16[128,2048]{1,0:T(8,128)(2,1)}, u32[]{:S(2)}) copy-start(bf16[128,2048]{1,0:T(8,128)(2,1)} %param.18) | copy-start | bytes 1572868
  7.3 152.4 %all-gather.12.cloned.1.call-start = ((), (), s32[]{:S(2)}) async-start(), calls=%async_computation.15 | async-start | bytes 3932160 | tf_op jit(solution)/shard_map/all_gather | solution.py:78
  8.7 98.0 %copy-start.10 = (bf16[64,8192]{1,0:T(8,128)(2,1)S(1)}, bf16[64,8192]{1,0:T(8,128)(2,1)}, u32[]{:S(2)}) copy-start(bf16[64,8192]{1,0:T(8,128)(2,1)} %param.22) | copy-start | bytes 3145732
  37.2 156.4 %all-gather.10.cloned.1.call-start = ((), (), s32[]{:S(2)}) async-start(), calls=%async_computation.14 | async-start | bytes 4718592 | tf_op jit(solution)/shard_map/all_gather | solution.py:66
  104.2 4.2 copy-start.12
  104.4 4.0 copy-start.15
  104.7 8.0 copy-start.19
  104.7 8.9 copy-start.14
  104.7 12.6 copy-start.17
  104.8 12.9 %copy-start.20 = (s32[1,13]{1,0:T(1,128)S(1)}, s32[1,13]{1,0:T(1,128)}, u32[]{:S(2)}) copy-start(s32[1,13]{1,0:T(1,128)} %param.33) | copy-start | bytes 160
  106.0 172.2 %all-gather.14.cloned.1.call-start = ((), (), s32[]{:S(2)}) async-start(), calls=%async_computation.16 | async-start | bytes 8650752 | tf_op jit(solution)/shard_map/all_gather | solution.py:129
  108.4 43.4 %all-to-all-start.2 = ((bf16[64,4,8,256]{3,1,0,2:T(4,128)(2,1)}), bf16[64,4,8,256]{3,1,0,2:T(4,128)(2,1)S(1)}, u32[]{:S(2)}, u32[]{:S(2)}) async-start(bf16[64,4,8,256]{3,1,0,2:T(4,128)(2,1)} %copy.115), calls=%async_computation.2 | async-start | bytes 2097152 | tf_op jit(solution)/shard_map/all_to_all | solution.py:126
  112.0 201.4 %all-gather.18.cloned.1.call-start = ((), (), s32[]{:S(2)}) async-start(), calls=%async_computation.18 | async-start | bytes 5242880 | tf_op jit(solution)/shard_map/all_gather | solution.py:78
  156.9 57.7 %copy-start.11 = (pred[1024,1024]{0,1:T(8,128)(4,1)}, pred[1024,1024]{0,1:T(8,128)(4,1)S(1)}, u32[]{:S(2)}) copy-start(pred[1024,1024]{0,1:T(8,128)(4,1)S(1)} %copy.110) | copy-start | bytes 3145732
  226.1 22.3 %all-to-all-start.1 = ((bf16[8,128,256]{1,2,0:T(8,128)(2,1)}), bf16[8,128,256]{1,2,0:T(8,128)(2,1)S(1)}, u32[]{:S(2)}, u32[]{:S(2)}) async-start(bf16[8,128,256]{1,2,0:T(8,128)(2,1)} %copy.114), calls=%async_computation.1 | async-start | bytes 1048576 | tf_op jit(solution)/shard_map/all_to_all | solution.py:157
  229.6 159.7 %all-gather.16.cloned.1.call-start = ((), (), s32[]{:S(2)}) async-start(), calls=%async_computation.17 | async-start | bytes 4718592 | tf_op jit(solution)/shard_map/all_gather | solution.py:66
  248.5 35.2 %copy-start.2 = (bf16[8,128,256]{1,2,0:T(8,128)(2,1)}, bf16[8,128,256]{1,2,0:T(8,128)(2,1)S(1)}, u32[]{:S(2)}) copy-start(bf16[8,128,256]{1,2,0:T(8,128)(2,1)S(1)} %all-to-all-done.1) | copy-start | bytes 1572868
  285.0 138.5 %all-gather.20.cloned.1.call-start = ((), (), s32[]{:S(2)}) async-start(), calls=%async_computation.19 | async-start | bytes 5242880 | tf_op jit(solution)/shard_map/all_gather | solution.py:78
  285.6 213.5 %all-gather.22.cloned.1.call-start = ((), (), s32[]{:S(2)}) async-start(), calls=%async_computation.21 | async-start | bytes 4718592 | tf_op jit(solution)/shard_map/all_gather | solution.py:66
  286.3 325.7 %reduce-scatter.9.cloned.1.call-start = ((), (), s32[]{:S(2)}) async-start(), calls=%async_computation.20 | async-start | bytes 4718592 | tf_op jit(solution)/shard_map/reduce_scatter | solution.py:70
  499.0 18.0 %copy-start.4 = (f32[1024,1024]{1,0:T(8,128)S(1)}, f32[1024,1024]{1,0:T(8,128)}, u32[]{:S(2)}) copy-start(f32[1024,1024]{1,0:T(8,128)} %fusion.95) | copy-start | bytes 12582916
  517.1 2.5 copy-start.30
  525.7 178.1 %reduce-scatter.11.cloned.1.call-start = ((), (), s32[]{:S(2)}) async-start(), calls=%async_computation.22 | async-start | bytes 4718592 | tf_op jit(solution)/shard_map/reduce_scatter | solution.py:70
  535.3 296.2 %reduce-scatter.21.cloned.1.call-start = ((), (), s32[]{:S(2)}) async-start(), calls=%async_computation.27 | async-start | bytes 5242880 | tf_op jit(solution)/shard_map/reduce_scatter | solution.py:74
  544.7 162.2 %copy-start.7 = (bf16[128,2048]{1,0:T(8,128)(2,1)S(1)}, bf16[128,2048]{1,0:T(8,128)(2,1)}, u32[]{:S(2)}) copy-start(bf16[128,2048]{1,0:T(8,128)(2,1)} %param.19) | copy-start | bytes 1572868
  544.8 367.7 %reduce-scatter.13.cloned.1.call-start = ((), (), s32[]{:S(2)}) async-start(), calls=%async_computation.23 | async-start | bytes 4718592 | tf_op jit(solution)/shard_map/reduce_scatter | solution.py:70
  807.9 178.5 %reduce-scatter.17.cloned.1.call-start = ((), (), s32[]{:S(2)}) async-start(), calls=%async_computation.25 | async-start | bytes 10485760 | tf_op jit(solution)/shard_map/reduce_scatter | solution.py:74
  814.5 8.2 copy-start.6
  814.5 212.5 %reduce-scatter.15.cloned.1.call-start = ((), (), s32[]{:S(2)}) async-start(), calls=%async_computation.24 | async-start | bytes 3932160 | tf_op jit(solution)/shard_map/reduce_scatter | solution.py:74
  822.7 252.8 %reduce-scatter.23.cloned.1.call-start = ((), (), s32[]{:S(2)}) async-start(), calls=%async_computation.28 | async-start | bytes 5242880 | tf_op jit(solution)/shard_map/reduce_scatter | solution.py:74
  831.0 81.4 %copy-start.1 = (bf16[128,2048]{1,0:T(8,128)(2,1)S(1)}, bf16[128,2048]{1,0:T(8,128)(2,1)}, u32[]{:S(2)}) copy-start(bf16[128,2048]{1,0:T(8,128)(2,1)} %param.18) | copy-start | bytes 1572868
  831.0 81.4 %copy-start.13 = (f32[2048]{0:T(1024)S(1)}, f32[2048]{0:T(1024)}, u32[]{:S(2)}) copy-start(f32[2048]{0:T(1024)} %copy-done.12) | copy-start | bytes 24580
  831.0 81.4 %copy-start.16 = (f32[128]{0:T(128)S(1)}, f32[128]{0:T(128)}, u32[]{:S(2)}) copy-start(f32[128]{0:T(128)} %copy-done.15) | copy-start | bytes 1540
  831.0 81.4 %copy-start.18 = (f32[128]{0:T(128)S(1)}, f32[128]{0:T(128)}, u32[]{:S(2)}) copy-start(f32[128]{0:T(128)} %copy-done.17) | copy-start | bytes 1540
  831.4 155.0 %all-to-all-start.5 = ((bf16[8,64,1024]{2,1,0:T(8,128)(2,1)}), bf16[8,64,1024]{2,1,0:T(8,128)(2,1)S(1)}, u32[]{:S(2)}, u32[]{:S(2)}) async-start(bf16[8,64,1024]{2,1,0:T(8,128)(2,1)} %bitcast.179), calls=%async_computation.12 | async-start | bytes 2097152 | tf_op jit(solution)/shard_map/all_to_all | solution.py:189
  835.4 366.7 %all-reduce.3.cloned.1.call-start = ((), (), s32[]{:S(2)}) async-start(), calls=%async_computation.29 | async-start | bytes 196608
  914.9 359.5 %reduce-scatter.19.cloned.1.call-start = ((), (), s32[]{:S(2)}) async-start(), calls=%async_computation.26 | async-start | bytes 2359296 | tf_op jit(solution)/shard_map/reduce_scatter | solution.py:196
  1027.0 59.0 %all-to-all-start.4 = ((bf16[8,64,768]{2,1,0:T(8,128)(2,1)}), bf16[8,64,768]{2,1,0:T(8,128)(2,1)S(1)}, u32[]{:S(2)}, u32[]{:S(2)}) async-start(bf16[8,64,768]{2,1,0:T(8,128)(2,1)} %bitcast.181), calls=%async_computation.8 | async-start | bytes 1572864 | tf_op jit(solution)/shard_map/all_to_all | solution.py:189
  1086.0 6.0 copy-start.8
  (3 other events, 3.5 us)
Sparse Core Ops, SparseCore 0:
  37.4 27.5 all-gather.11
  106.1 87.4 all-gather.9
  196.6 81.5 all-gather.13
  280.2 33.1 all-gather.17
  315.9 73.3 all-gather.15
  390.7 32.7 all-gather.19
  425.6 73.3 all-gather.21
  525.8 86.1 reduce-scatter.8
  616.0 87.6 reduce-scatter.10
  706.1 44.2 reduce-scatter.20
  808.0 104.3 reduce-scatter.12
  914.9 71.4 reduce-scatter.16
  989.1 37.9 reduce-scatter.14
  1029.4 44.7 reduce-scatter.22
  1081.1 120.8 all-reduce.2
  1205.9 68.4 reduce-scatter.18

commit v2 on v1

v2 whole, which is shorter than its diff:
```python
import functools

import jax
import jax.numpy as jnp
from jax import lax
from jax.experimental import pallas as pl
from jax.experimental.pallas import tpu as pltpu
from jax.sharding import PartitionSpec as P

H = 32
HD = 64
BLK = 32

EPSILON = 1e-05
MASKED = -1e30
BF = jnp.bfloat16
F32 = jnp.float32
BOTH = ("dp", "fsdp")
MESH = pl.DeviceIdType.MESH
HBM = pl.BlockSpec(memory_space=pl.ANY)
VM = pl.BlockSpec(memory_space=pltpu.VMEM)
MIB = 2**20


def place():
    d, f = lax.axis_index("dp"), lax.axis_index("fsdp")
    return d // 2, d % 2, f // 2, f % 2


def at(x, c, z, y):
    return (x * 2 + c, z * 2 + y)


def remote(src, dst, send, recv, target):
    return pltpu.make_async_remote_copy(
        src_ref=src, dst_ref=dst, send_sem=send, recv_sem=recv, device_id=target, device_id_type=MESH
    )


def greet(partners):
    barrier = pltpu.get_barrier_semaphore()
    count = 0
    for condition, device in partners:

        @pl.when(condition)
        def _():
            pl.semaphore_signal(barrier, inc=1, device_id=device, device_id_type=MESH)

        count = count + jnp.asarray(condition).astype(jnp.int32)
    pl.semaphore_wait(barrier, count)


def greet_all(devices, fsdp, me):
    barrier = pltpu.get_barrier_semaphore()

    def one(k, _):
        other = (me + k) % devices
        pl.semaphore_signal(barrier, inc=1, device_id=(other // fsdp, other % fsdp), device_id_type=MESH)
        return 0

    lax.fori_loop(1, devices, one, 0)
    pl.semaphore_wait(barrier, devices - 1)


def line_partners(nz, pos):
    x, c, z, y = pos
    return [(z >= 0, at(x, 1 - c, z, y)), (z > 0, at(x, c, z - 1, y)), (z < nz - 1, at(x, c, z + 1, y))]


def rank_partners(nz, pos):
    x, c, z, y = pos
    n = 2 * nz
    others = [(z * 2 + c + k) % n for k in range(1, n)]
    return [(z >= 0, at(x, p % 2, p // 2, y)) for p in others]


def group_partners(pos):
    x, c, z, y = pos
    return [(z >= 0, at(x ^ (m // 2), c, z, y ^ (m % 2))) for m in (1, 2, 3)]


def line_gather(src, dst, send, recv, nz, swap, pos):
    x, c, z, y = pos
    own = z * 2 + c
    sib = at(x, 1 - c, z, y)
    up_dev, dn_dev = at(x, c, z + 1, y), at(x, c, z - 1, y)
    UP, DN, SU, SD = 0, nz, 2 * nz, 3 * nz
    OWN = 4 * nz

    def block(b, moved):
        return dst.at[b] if moved else src

    def up(k):
        b = (z - k) * 2 + c
        return remote(block(b, k or swap), dst.at[b], send.at[UP + k], recv.at[UP + k], up_dev)

    def dn(k):
        b = (z + k) * 2 + c
        return remote(block(b, k or swap), dst.at[b], send.at[DN + k], recv.at[DN + k], dn_dev)

    def side(k, base, sign):
        b = (z + sign * k) * 2 + c
        return remote(block(b, k or swap), dst.at[b], send.at[base + k], recv.at[base + k], sib)

    def got(b, sem):
        return remote(dst.at[b], dst.at[b], send.at[OWN], recv.at[sem], sib)

    local = pltpu.make_async_copy(src, dst.at[own], recv.at[OWN])
    trade = remote(src, dst.at[z * 2 + y], send.at[OWN], recv.at[OWN], at(x, y, z, c))

    def first():
        if swap:
            pl.when(c == y)(local.start)
            pl.when(c != y)(trade.start)
        else:
            local.start()

    def spread():
        if swap:
            local.wait()
        pl.when(z < nz - 1)(up(0).start)
        pl.when(z > 0)(dn(0).start)
        side(0, SU, 1).start()

    def step(k):
        @pl.when(z >= k)
        def _():
            got((z - k) * 2 + c, UP + k - 1).wait_recv()
            pl.when(z < nz - 1)(up(k).start)
            side(k, SU, -1).start()

        @pl.when(z + k < nz)
        def _():
            got((z + k) * 2 + c, DN + k - 1).wait_recv()
            pl.when(z > 0)(dn(k).start)
            side(k, SD, 1).start()

    def last():
        if swap:
            pl.when(c != y)(trade.wait_send)
        else:
            local.wait()
        got(z * 2 + 1 - c, SU).wait_recv()
        pl.when(z < nz - 1)(up(0).wait_send)
        pl.when(z > 0)(dn(0).wait_send)
        side(0, SU, 1).wait_send()
        for k in range(1, nz):

            @pl.when(z >= k)
            def _():
                got((z - k) * 2 + 1 - c, SU + k).wait_recv()
                pl.when(z < nz - 1)(up(k).wait_send)
                side(k, SU, -1).wait_send()

            @pl.when(z + k < nz)
            def _():
                got((z + k) * 2 + 1 - c, SD + k).wait_recv()
                pl.when(z > 0)(dn(k).wait_send)
                side(k, SD, 1).wait_send()

    return [first, spread] + [functools.partial(step, k) for k in range(1, nz)] + [last]


def gather_sems(nz):
    return [pltpu.SemaphoreType.DMA((4 * nz + 1,))] * 2


def gather_kernel(nz, src, dst, send, recv):
    pos = place()
    greet(line_partners(nz, pos))
    for stage in line_gather(src, dst, send, recv, nz, False, pos):
        stage()


def params(cid, vmem=None):
    return pltpu.CompilerParams(collective_id=cid, has_side_effects=True, vmem_limit_bytes=vmem)


def gather_tokens(a, nz, cid):
    return pl.pallas_call(
        functools.partial(gather_kernel, nz),
        out_shape=jax.ShapeDtypeStruct((2 * nz,) + a.shape, a.dtype),
        in_specs=[HBM],
        out_specs=HBM,
        scratch_shapes=gather_sems(nz),
        compiler_params=params(cid),
        name="gather_tokens",
    )(a)


def scatter_kernel(nz, p, out, acc, ups, dns, send, recv):
    pos = place()
    x, c, z, y = pos
    greet(line_partners(nz, pos))
    sib = at(x, 1 - c, z, y)
    S, U, D = 0, nz, 2 * nz

    def f(v):
        return v.astype(F32)

    def swap(t):
        return remote(p.at[t * 2 + 1 - c], acc.at[t], send.at[S + t], recv.at[S + t], sib)

    def up(t):
        return remote(acc.at[t], ups.at[t], send.at[U + t], recv.at[U + t], at(x, c, z + 1, y))

    def dn(t):
        return remote(acc.at[t], dns.at[t], send.at[D + t], recv.at[D + t], at(x, c, z - 1, y))

    order = []
    for i in range(nz - 1):
        order += [(True, nz - 1 - i), (False, i)]
    for upward, t in order:
        pl.when(z < t if upward else z > t)(swap(t).start)
    swap(z).start()
    for upward, t in order:

        @pl.when(z < t if upward else z > t)
        def _():
            swap(t).wait_recv()
            acc[t] = (f(acc[t]) + f(p[t * 2 + c])).astype(BF)
            move, came = (up, ups) if upward else (dn, dns)

            @pl.when(z > 0 if upward else z < nz - 1)
            def _():
                move(t).wait_recv()
                acc[t] = (f(acc[t]) + f(came[t])).astype(BF)

            move(t).start()

    swap(z).wait_recv()
    out[...] = f(acc[z]) + f(p[z * 2 + c])

    @pl.when(z > 0)
    def _():
        up(z).wait_recv()
        out[...] += f(ups[z])

    @pl.when(z < nz - 1)
    def _():
        dn(z).wait_recv()
        out[...] += f(dns[z])

    for t in range(nz):
        swap(t).wait_send()
        pl.when(z < t)(up(t).wait_send)
        pl.when(z > t)(dn(t).wait_send)


def scatter_tokens(p, nz, cid):
    blocks, rows, width = p.shape
    return pl.pallas_call(
        functools.partial(scatter_kernel, nz),
        out_shape=jax.ShapeDtypeStruct((rows, width), F32),
        in_specs=[VM],
        out_specs=VM,
        scratch_shapes=[pltpu.VMEM((nz, rows, width), BF)] * 3 + [pltpu.SemaphoreType.DMA((3 * nz,))] * 2,
        compiler_params=params(cid, 60 * MIB),
        name="scatter_tokens",
    )(p)


def block_of(x, c, z, y, nz):
    return (x * 2 + c) * 2 * nz + z * 2 + y


def sliced_gather(src, dst, cuts, sems, nz, pos):
    x, c, z, y = pos
    n = 2 * nz
    me = z * 2 + c
    send1, recv1, send2, recv2 = sems

    def pieces(p):
        if cuts is None:
            return [(src.at[p], slice(None))]
        return [(src.at[:, a], b) for a, b in cuts(p)]

    def row(p, gx, gy):
        return block_of(gx, p % 2, p // 2, gy, nz)

    mine = row(me, x, y)

    def out(k):
        p = (me + k) % n
        return [
            remote(a, dst.at[mine, :, b], send1.at[p], recv1.at[me], at(x, p % 2, p // 2, y))
            for a, b in pieces(p)
        ]

    def whole(p, gx, gy, sem):
        b = dst.at[row(p, gx, gy)]
        return remote(b, b, send1.at[me], sem, at(x, 1 - c, z, y))

    local = [pltpu.make_async_copy(a, dst.at[mine, :, b], recv1.at[me]) for a, b in pieces(me)]

    def forward(k, m):
        p = (me - k + n) % n
        b = dst.at[row(p, x, y)]
        slot = (m - 1) * n + p
        return remote(b, b, send2.at[slot], recv2.at[slot], at(x ^ (m // 2), c, z, y ^ (m % 2)))

    def first():
        for copy in local:
            copy.start()
        for k in range(1, n):
            for copy in out(k):
                copy.start()

    def step(k):
        p = (me - k + n) % n
        whole(p, x, y, recv1.at[p]).wait_recv()
        for m in (3, 1, 2):
            forward(k, m).start()

    def last():
        for k in range(n):
            p = (me - k + n) % n
            for m in (1, 2, 3):
                slot = (m - 1) * n + p
                whole(p, x ^ (m // 2), y ^ (m % 2), recv2.at[slot]).wait_recv()
        for k in range(n):
            if k:
                p = (me + k) % n
                whole_send = remote(
                    dst.at[mine], dst.at[mine], send1.at[p], recv1.at[me], at(x, p % 2, p // 2, y)
                )
                whole_send.wait_send()
            for m in (1, 2, 3):
                forward(k, m).wait_send()

    return [first] + [functools.partial(step, k) for k in range(n)] + [last]


def sliced_sems(nz):
    n = 2 * nz
    return [pltpu.SemaphoreType.DMA((n,))] * 2 + [pltpu.SemaphoreType.DMA((3 * n,))] * 2


def group_gather(src, dst, send, recv, pos):
    x, c, z, y = pos
    g = x * 2 + y
    local = pltpu.make_async_copy(src, dst.at[g], recv.at[0])

    def out(m):
        return remote(src, dst.at[g], send.at[m], recv.at[m], at(x ^ (m // 2), c, z, y ^ (m % 2)))

    def first():
        local.start()
        for m in (3, 1, 2):
            out(m).start()

    def last():
        local.wait()
        for m in (1, 2, 3):
            there = dst.at[(x ^ (m // 2)) * 2 + (y ^ (m % 2))]
            remote(there, there, send.at[m], recv.at[m], at(x, 1 - c, z, y)).wait_recv()
            out(m).wait_send()

    return [first, last]


def head_runs(nz, cols):
    return lambda p: [
        (block_of(x, p % 2, p // 2, 0, nz) * HD, x * cols // 2, cols // 2) for x in range(2)
    ]


def qkv_cuts(nz, width, cols):
    runs = head_runs(nz, cols)
    return lambda p: [
        (pl.ds(j * width + there, size), pl.ds(j * cols + here, size)) for j in range(3) for there, here, size in runs(p)
    ]


def up_cuts(nz, unit):
    def cuts(p):
        z, c = p // 2, p % 2
        return [
            (pl.ds(((x * 2 + c) * 2 * nz + z * 2) * unit, 2 * unit), pl.ds(x * 2 * unit, 2 * unit))
            for x in range(2)
        ]

    return cuts


def fetch_kernel(
    nz, width, cols, unit, x_in, cot, w_qkv, w_up, w_down, vec, tab,
    x_all, cot_all, qkv_w, up_w, down_w, vecs, tab_out, *sems,
):
    pos = place()
    x, c, z, y = pos
    fsdp = 2 * nz
    devices = 4 * fsdp
    me = (x * 2 + c) * fsdp + z * 2 + y
    sems = list(sems)
    x_sems, cot_sems, qkv_sems, up_sems = sems[:2], sems[2:4], sems[4:8], sems[8:12]
    down_sems, vec_sems, tab_sems = sems[12:14], sems[14:16], sems[16:18]
    greet_all(devices, fsdp, me)

    def vec_copy(other):
        return remote(vec, vecs.at[me], vec_sems[0].at[other], vec_sems[1].at[me], (other // fsdp, other % fsdp))

    def each(fn):
        def body(k, _):
            fn((me + k) % devices)
            return 0

        lax.fori_loop(1, devices, body, 0)

    vec_local = pltpu.make_async_copy(vec, vecs.at[me], vec_sems[1].at[me])
    tab_local = pltpu.make_async_copy(tab, tab_out, tab_sems[1].at[0])
    tab_trade = remote(tab, tab_out, tab_sems[0].at[0], tab_sems[1].at[0], at(x, y, z, c))

    gx = line_gather(x_in, x_all, *x_sems, nz, True, pos)
    gc = line_gather(cot, cot_all, *cot_sems, nz, True, pos)
    cuts = qkv_cuts(nz, width, cols) if len(w_qkv.shape) == 2 else None
    gq = sliced_gather(w_qkv, qkv_w, cuts, qkv_sems, nz, pos)
    gu = sliced_gather(w_up, up_w, up_cuts(nz, unit), up_sems, nz, pos)
    gd = group_gather(w_down, down_w, *down_sems, pos)
    gx[0]()
    gq[0]()
    gx[1]()
    vec_local.start()
    each(lambda other: vec_copy(other).start())
    pl.when(c == y)(tab_local.start)
    pl.when(c != y)(tab_trade.start)
    gd[0]()
    gc[0]()
    gu[0]()
    for k in range(1, fsdp + 1):
        gq[k]()
    for stage in gx[2:]:
        stage()
    gc[1]()
    for k in range(1, fsdp + 1):
        gu[k]()
    for stage in gc[2:]:
        stage()
    gq[-1]()
    gu[-1]()
    gd[-1]()

    def vec_done(other):
        remote(vec, vecs.at[other], vec_sems[0].at[other], vec_sems[1].at[other], at(x, 1 - c, z, y)).wait_recv()
        vec_copy(other).wait_send()

    vec_local.wait()
    each(vec_done)
    tab_local.wait()
    pl.when(c != y)(tab_trade.wait_send)


def fetch(nz, x_in, cot, w_qkv, w_up, w_down, vec, tab, cid):
    rows, width = x_in.shape
    n = 2 * nz
    devices = 4 * n
    part, unit = w_up.shape[0], w_down.shape[0]
    cols = width // n
    shapes = [
        ((n, rows, width), BF),
        ((n, rows, width), BF),
        ((devices, part, 3 * cols), BF),
        ((devices, part, 4 * unit), BF),
        ((4, unit, width), BF),
        ((devices,) + vec.shape, F32),
        (tab.shape, jnp.int32),
    ]
    return pl.pallas_call(
        functools.partial(fetch_kernel, nz, width, cols, unit),
        out_shape=[jax.ShapeDtypeStruct(s, t) for s, t in shapes],
        in_specs=[HBM] * 7,
        out_specs=[HBM] * 7,
        scratch_shapes=gather_sems(nz) * 2
        + sliced_sems(nz) * 2
        + [pltpu.SemaphoreType.DMA((4,))] * 2
        + [pltpu.SemaphoreType.DMA((devices,))] * 2
        + [pltpu.SemaphoreType.DMA((1,))] * 2,
        compiler_params=params(cid),
        name="fetch",
    )(x_in, cot, w_qkv, w_up, w_down, vec, tab)


def exchange_kernel(nz, count, *refs):
    srcs, dsts, (send, recv) = refs[:count], refs[count : 2 * count], refs[2 * count :]
    pos = place()
    x, c, z, y = pos
    n = 2 * nz
    me = z * 2 + c
    greet(rank_partners(nz, pos))

    def move(i, p):
        return remote(srcs[i].at[p], dsts[i].at[me], send.at[i * n + p], recv.at[i * n + me], at(x, p % 2, p // 2, y))

    def come(i, p):
        there = dsts[i].at[p]
        return remote(there, there, send.at[i * n + me], recv.at[i * n + p], at(x, 1 - c, z, y))

    local = [pltpu.make_async_copy(s.at[me], d.at[me], recv.at[i * n + me]) for i, (s, d) in enumerate(zip(srcs, dsts))]
    for i in range(count):
        local[i].start()
        for k in range(1, n):
            move(i, (me + k) % n).start()
    for i in range(count):
        local[i].wait()
        for k in range(1, n):
            come(i, (me - k + n) % n).wait_recv()
            move(i, (me + k) % n).wait_send()


def exchange(arrays, nz, cid, name):
    n = 2 * nz
    return pl.pallas_call(
        functools.partial(exchange_kernel, nz, len(arrays)),
        out_shape=[jax.ShapeDtypeStruct(a.shape, a.dtype) for a in arrays],
        in_specs=[HBM] * len(arrays),
        out_specs=[HBM] * len(arrays),
        scratch_shapes=[pltpu.SemaphoreType.DMA((len(arrays) * n,))] * 2,
        compiler_params=params(cid),
        name=name,
    )(*arrays)


def hand_kernel(nz, kinds, *refs):
    count = len(kinds)
    srcs, dsts, (send, recv) = refs[:count], refs[count : 2 * count], refs[2 * count :]
    pos = place()
    x, c, z, y = pos
    n = 2 * nz
    greet(group_partners(pos))

    def copies(i, m):
        gx, gy = x ^ (m // 2), y ^ (m % 2)
        sem = i * 3 + m - 1
        target = at(gx, c, z, gy)
        if not kinds[i]:
            return [remote(srcs[i].at[gx * 2 + gy], dsts[i].at[m - 1], send.at[sem], recv.at[sem], target)]
        return [
            remote(
                srcs[i].at[block_of(gx, p % 2, p // 2, gy, nz)],
                dsts[i].at[m - 1, p],
                send.at[sem],
                recv.at[sem],
                target,
            )
            for p in range(n)
        ]

    for i in range(count):
        for m in (3, 1, 2):
            for copy in copies(i, m):
                copy.start()
    for i in range(count):
        for m in (1, 2, 3):
            sem = i * 3 + m - 1
            there = dsts[i].at[m - 1]
            whole = remote(there, there, send.at[sem], recv.at[sem], at(x, 1 - c, z, y))
            whole.wait_recv()
            whole.wait_send()


def hand(arrays, kinds, nz, cid):
    n = 2 * nz
    shapes = [(3, n) + a.shape[1:] if k else (3,) + a.shape[1:] for a, k in zip(arrays, kinds)]
    return pl.pallas_call(
        functools.partial(hand_kernel, nz, kinds),
        out_shape=[jax.ShapeDtypeStruct(s, a.dtype) for s, a in zip(shapes, arrays)],
        in_specs=[HBM] * len(arrays),
        out_specs=[HBM] * len(arrays),
        scratch_shapes=[pltpu.SemaphoreType.DMA((3 * len(arrays),))] * 2,
        compiler_params=params(cid),
        name="hand",
    )(*arrays)


def finish_kernel(nz, res, grad, small, res_out, grad_out, small_out, came, send, recv):
    pos = place()
    x, c, z, y = pos
    fsdp = 2 * nz
    devices = 4 * fsdp
    me = (x * 2 + c) * fsdp + z * 2 + y
    greet_all(devices, fsdp, me)

    def each(fn):
        def body(k, _):
            fn((me + k) % devices)
            return 0

        lax.fori_loop(1, devices, body, 0)

    def share(other):
        return remote(small.at[other], came.at[me], send.at[other], recv.at[me], (other // fsdp, other % fsdp))

    each(lambda other: share(other).start())
    homes = [(res, res_out, devices), (grad, grad_out, devices + 1)]
    for src, dst, sem in homes:
        pl.when(c == y)(pltpu.make_async_copy(src, dst, recv.at[sem]).start)
        pl.when(c != y)(remote(src, dst, send.at[sem], recv.at[sem], at(x, y, z, c)).start)

    def done(other):
        remote(small.at[me], came.at[other], send.at[other], recv.at[other], at(x, 1 - c, z, y)).wait_recv()
        share(other).wait_send()

    each(done)
    came[me] = small[me]
    small_out[...] = jnp.sum(came[...], axis=0)
    for src, dst, sem in homes:
        pltpu.make_async_copy(src, dst, recv.at[sem]).wait()
        pl.when(c != y)(remote(src, dst, send.at[sem], recv.at[sem], at(x, y, z, c)).wait_send)


def finish(res, grad, small, nz, cid):
    devices = small.shape[0]
    return pl.pallas_call(
        functools.partial(finish_kernel, nz),
        out_shape=[
            jax.ShapeDtypeStruct(res.shape, res.dtype),
            jax.ShapeDtypeStruct(grad.shape, grad.dtype),
            jax.ShapeDtypeStruct(small.shape[1:], F32),
        ],
        in_specs=[HBM, HBM, VM],
        out_specs=[HBM, HBM, VM],
        scratch_shapes=[pltpu.VMEM(small.shape, F32)] + [pltpu.SemaphoreType.DMA((devices + 2,))] * 2,
        compiler_params=params(cid, 32 * MIB),
        name="finish",
    )(res, grad, small)


def dot(a, b, dims):
    return lax.dot_general(a, b, (dims, ((), ())), preferred_element_type=F32)


NN = ((1,), (0,))
NT = ((1,), (1,))
TN = ((0,), (0,))


def attend_kernel(heads, slopes, far, joined_q, joined, out):
    cols = heads * HD
    gap = far[...]
    for h in range(heads):
        q = joined_q[:, h * HD : (h + 1) * HD]
        k = joined[:, cols + h * HD : cols + (h + 1) * HD]
        v = joined[:, 2 * cols + h * HD : 2 * cols + (h + 1) * HD]
        logits = dot(q, k, NT) * HD ** (-0.5) + slopes[h] * gap
        weights = jnp.exp(logits - jnp.max(logits, axis=1, keepdims=True))
        probs = weights * (1.0 / jnp.sum(weights, axis=1, keepdims=True))
        out[:, h * HD : (h + 1) * HD] = dot(probs.astype(BF), v, NN).astype(BF)


def attend(slopes, far, joined, heads):
    tree = far.shape[0]
    cols = heads * HD
    rows = min(256, tree)
    return pl.pallas_call(
        functools.partial(attend_kernel, heads),
        out_shape=jax.ShapeDtypeStruct((tree, cols), BF),
        grid=(tree // rows,),
        in_specs=[
            pl.BlockSpec(memory_space=pltpu.SMEM),
            pl.BlockSpec((rows, tree), lambda i: (i, 0)),
            pl.BlockSpec((rows, 3 * cols), lambda i: (i, 0)),
            pl.BlockSpec((tree, 3 * cols), lambda i: (0, 0)),
        ],
        out_specs=pl.BlockSpec((rows, cols), lambda i: (i, 0)),
        compiler_params=pltpu.CompilerParams(vmem_limit_bytes=56 * MIB),
        cost_estimate=pl.CostEstimate(
            flops=4 * heads * tree * tree * HD, bytes_accessed=4 * tree * tree, transcendentals=heads * tree * tree
        ),
        name="attend",
    )(slopes, far, joined, joined)


def attend_back_kernel(heads, slopes, far, joined_q, joined, grad, out_q, out_k, out_v, acc_k, acc_v):
    cols = heads * HD
    step = pl.program_id(0)

    @pl.when(step == 0)
    def _():
        acc_k[...] = jnp.zeros_like(acc_k)
        acc_v[...] = jnp.zeros_like(acc_v)

    gap = far[...]
    for h in range(heads):
        here = slice(h * HD, (h + 1) * HD)
        q = joined_q[:, here]
        k = joined[:, cols + h * HD : cols + (h + 1) * HD]
        v = joined[:, 2 * cols + h * HD : 2 * cols + (h + 1) * HD]
        g = grad[:, here]
        logits = dot(k, q, NT) * HD ** (-0.5) + slopes[h] * gap
        weights = jnp.exp(logits - jnp.max(logits, axis=0, keepdims=True))
        probs = weights * (1.0 / jnp.sum(weights, axis=0, keepdims=True))
        grad_probs = dot(v, g, NT)
        delta = jnp.sum(probs * grad_probs, axis=0, keepdims=True)
        grad_raw = (probs * (grad_probs - delta) * HD ** (-0.5)).astype(BF)
        acc_v[:, here] += dot(probs.astype(BF), g, NN)
        acc_k[:, here] += dot(grad_raw, q, NN)
        out_q[:, here] = dot(grad_raw, k, TN).astype(BF)

    @pl.when(step == pl.num_programs(0) - 1)
    def _():
        out_k[...] = acc_k[...].astype(BF)
        out_v[...] = acc_v[...].astype(BF)


def attend_back(slopes, far_t, joined, grad, heads):
    tree = far_t.shape[0]
    cols = heads * HD
    rows = min(256, tree)
    full = pl.BlockSpec((tree, cols), lambda i: (0, 0))
    part = pl.BlockSpec((rows, cols), lambda i: (i, 0))
    return pl.pallas_call(
        functools.partial(attend_back_kernel, heads),
        out_shape=[jax.ShapeDtypeStruct((tree, cols), BF)] * 3,
        grid=(tree // rows,),
        in_specs=[
            pl.BlockSpec(memory_space=pltpu.SMEM),
            pl.BlockSpec((tree, rows), lambda i: (0, i)),
            pl.BlockSpec((rows, 3 * cols), lambda i: (i, 0)),
            pl.BlockSpec((tree, 3 * cols), lambda i: (0, 0)),
            part,
        ],
        out_specs=[part, full, full],
        scratch_shapes=[pltpu.VMEM((tree, cols), F32)] * 2,
        compiler_params=pltpu.CompilerParams(vmem_limit_bytes=56 * MIB),
        cost_estimate=pl.CostEstimate(
            flops=10 * heads * tree * tree * HD, bytes_accessed=4 * tree * tree, transcendentals=heads * tree * tree
        ),
        name="attend_back",
    )(slopes, far_t, joined, joined, grad)


def norm_parts(values):
    center = values - jnp.mean(values, axis=-1, keepdims=True)
    inverse = lax.rsqrt(jnp.mean(center * center, axis=-1, keepdims=True) + EPSILON)
    return (center * inverse, inverse)


def norm_back(grad_normed, normed, inverse):
    mean_grad = jnp.mean(grad_normed, axis=-1, keepdims=True)
    mean_cross = jnp.mean(grad_normed * normed, axis=-1, keepdims=True)
    return inverse * (grad_normed - mean_grad - normed * mean_cross)


def tree_tables(parents, seg_blocks, valid):
    segments = parents.shape[0]
    seg_tokens = jnp.broadcast_to(seg_blocks[:, None], (seg_blocks.shape[0], BLK)).reshape(-1)
    labels = jnp.arange(segments, dtype=jnp.int32)
    member = (seg_tokens[:, None] == labels[None, :]).astype(jnp.int32)
    counted = member * valid[:, None]
    before = jnp.cumsum(counted, axis=0) - counted
    rank = jnp.sum(before * member, axis=1)
    seg_len = jnp.sum(counted, axis=0)
    picked = (parents[:, None] == labels[None, :]).astype(jnp.int32)
    grand = jnp.sum(picked * parents[None, :], axis=1)
    ancestor = ((labels[None, :] == parents[:, None]) | (labels[None, :] == grand[:, None])) & (
        labels[None, :] != labels[:, None]
    )
    offset = jnp.sum(ancestor.astype(jnp.int32) * seg_len[None, :], axis=1)
    position = jnp.sum(member * offset[None, :], axis=1) + rank
    return (seg_tokens, position, ancestor.astype(jnp.float32))


def allowed_mask(seg, index, valid, ancestor):
    labels = jnp.arange(ancestor.shape[0], dtype=jnp.int32)
    member = (seg[:, None] == labels[None, :]).astype(jnp.float32)
    reach = jnp.dot(jnp.dot(member, ancestor), member.T) > 0.5
    causal = (seg[:, None] == seg[None, :]) & (index[None, :] <= index[:, None])
    visible = (valid[None, :] == 1) | (index[None, :] == index[:, None])
    return (reach | causal) & visible


def gelu_exact(value):
    return jax.nn.gelu(value, approximate=False)


def mm(spec, a, b):
    return jnp.einsum(spec, a, b, preferred_element_type=F32)


def padded(flat, lanes):
    return jnp.pad(flat, [(0, 0)] * (flat.ndim - 1) + [(0, -flat.shape[-1] % lanes)])


def per_device(
    layer_in,
    cotangent,
    w_qkv,
    w_out,
    w_up,
    w_down,
    gain_attn,
    shift_attn,
    bias_query,
    bias_value,
    bias_out,
    gain_mlp,
    shift_mlp,
    bias_up,
    bias_down,
    parents,
    seg_blocks,
    token_valid,
):
    rows, width = layer_in.shape
    fsdp = lax.axis_size("fsdp")
    nz = fsdp // 2
    devices = 4 * fsdp
    x, c, z, y = place()
    rank = z * 2 + c
    heads = H // fsdp
    cols = heads * HD
    tree = token_valid.shape[1]
    part = w_qkv.shape[0]
    unit = w_down.shape[0]

    vec = jnp.concatenate(
        [gain_attn, shift_attn, bias_query, bias_value, bias_out, gain_mlp, shift_mlp, bias_down, bias_up]
    ).astype(F32)
    vec = padded(vec, 1024).reshape(-1, 128)
    tab = jnp.concatenate([token_valid[0], seg_blocks[0], parents[0]])
    tab = padded(tab, 1024).reshape(-1, 128)
    out_w = lax.all_gather(w_out, BOTH, axis=0, tiled=True)
    aligned = part == HD and cols % 256 == 0
    if not aligned:
        w_qkv = w_qkv.reshape(part, 3, fsdp, cols).transpose(2, 0, 1, 3).reshape(fsdp, part, 3 * cols)
    x_all, cot, qkv_w, up_w, down_w, vecs, tab = fetch(nz, layer_in, cotangent, w_qkv, w_up, w_down, vec, tab, 1)
    x_all, cot = x_all.reshape(tree, width), cot.reshape(tree, width)
    qkv_w = qkv_w.reshape(width, 3 * cols)
    up_w = up_w.reshape(width, 4 * unit)
    down_w = down_w.reshape(4 * unit, width)
    vecs = vecs.reshape(devices, -1)
    (gain_one, shift_one, query_bias, value_bias, out_bias, gain_two, shift_two, down_bias) = [
        vecs[:, i * part : (i + 1) * part].reshape(-1) for i in range(8)
    ]
    up_bias = vecs[:, 8 * part : 8 * part + unit].reshape(2, 2, nz, 2, unit)
    up_bias = lax.dynamic_slice(up_bias, (0, c, z, 0, 0), (2, 1, 1, 2, unit)).reshape(-1)

    def own_rows(v):
        return lax.dynamic_slice_in_dim(v, rank * rows, rows, 0)

    normed_all, _ = norm_parts(x_all.astype(F32))
    attn_in = (normed_all * gain_one + shift_one).astype(BF)
    inputs = own_rows(x_all).astype(F32)
    normed_one, inverse_one = norm_parts(inputs)

    if aligned:

        def own_cols(v):
            v = v.reshape(2, 2, nz, 2, HD)
            return lax.dynamic_slice(v, (0, c, z, 0, 0), (2, 1, 1, 2, HD)).reshape(-1)

        def spread(v):
            v = v.reshape(2, 1, 1, 2, HD)
            return lax.dynamic_update_slice(jnp.zeros((2, 2, nz, 2, HD), F32), v, (0, c, z, 0, 0))

        numbers = block_of(jnp.arange(2)[:, None], c, z, jnp.arange(2)[None, :], nz).reshape(-1)
    else:

        def own_cols(v):
            return lax.dynamic_slice_in_dim(v, rank * cols, cols, 0)

        def spread(v):
            return lax.dynamic_update_slice_in_dim(jnp.zeros((width,), F32), v, rank * cols, 0)

        numbers = rank * heads + jnp.arange(heads)

    joined_bias = jnp.concatenate([own_cols(query_bias), jnp.zeros((cols,), F32), own_cols(value_bias)])
    joined = (jnp.dot(attn_in, qkv_w, preferred_element_type=F32) + joined_bias).astype(BF)

    tab = tab.reshape(-1)
    blocks = seg_blocks.shape[1]
    valid = tab[:tree]
    seg, position, ancestor = tree_tables(
        tab[tree + blocks : tree + blocks + parents.shape[1]], tab[tree : tree + blocks], valid
    )
    index = jnp.arange(tree, dtype=jnp.int32)
    mask = allowed_mask(seg, index, valid, ancestor)
    far = jnp.where(mask, (position[None, :] - position[:, None]).astype(F32), MASKED)
    slopes = jnp.exp2(-8.0 * (numbers.astype(F32) + 1.0) / H)
    mixed = attend(slopes, far, joined, heads)

    (mixed_own,) = exchange([mixed.reshape(fsdp, rows, cols)], nz, 2, "mixed_to_tokens")
    if aligned:
        mixed_own = mixed_own.reshape(nz, 2, rows, 2, 2 * HD).transpose(2, 3, 1, 0, 4).reshape(rows, width)
    else:
        mixed_own = mixed_own.transpose(1, 0, 2).reshape(rows, width)
    branch = jnp.dot(mixed_own, out_w, preferred_element_type=F32) + out_bias
    middle = inputs + branch
    normed_two, inverse_two = norm_parts(middle)
    mlp_in = gather_tokens((normed_two * gain_two + shift_two).astype(BF), nz, 3).reshape(tree, width)
    hidden = jnp.dot(mlp_in, up_w, preferred_element_type=F32) + up_bias
    active_float, gelu_pull = jax.vjp(gelu_exact, hidden)
    active = active_float.astype(BF)
    grad_active = mm("td,fd->tf", cot, down_w)
    grad_hidden = gelu_pull(grad_active)[0].astype(BF)

    def scatter(v):
        return scatter_tokens(v.astype(BF).reshape(fsdp, rows, width), nz, 4)

    grad_mlp_in = scatter(mm("tf,df->td", grad_hidden, up_w))
    update = scatter(jnp.dot(active, down_w, preferred_element_type=F32)) + down_bias
    result = middle + update

    cot_own = own_rows(cot).astype(F32)
    grad_middle = cot_own + norm_back(grad_mlp_in * gain_two, normed_two, inverse_two)
    grad_branch = grad_middle.astype(BF)
    grad_mixed = mm("te,de->td", grad_branch, out_w).astype(BF)
    if aligned:
        branch_all = gather_tokens(grad_branch, nz, 3).reshape(tree, width)
        out_g = mm("td,te->de", mixed, branch_all).astype(BF).reshape(4, part, width)
    else:
        grad_out_w = lax.psum_scatter(
            mm("td,te->de", mixed_own, grad_branch).astype(BF), BOTH, scatter_dimension=0, tiled=True
        ).astype(F32)
    if aligned:
        grad_mixed = grad_mixed.reshape(rows, 2, 2, nz, 2 * HD).transpose(3, 2, 0, 1, 4).reshape(fsdp, rows, cols)
    else:
        grad_mixed = grad_mixed.reshape(rows, fsdp, cols).transpose(1, 0, 2)
    (grad_heads,) = exchange([grad_mixed], nz, 5, "grad_to_heads")
    grad_heads = grad_heads.reshape(tree, cols)
    grad_q, grad_k, grad_v = attend_back(slopes, far.T, joined, grad_heads, heads)
    grad_joined = jnp.concatenate([grad_q, grad_k, grad_v], axis=1)
    grad_attn_in = scatter(mm("te,de->td", grad_joined, qkv_w))
    grad_inputs = grad_middle + norm_back(grad_attn_in * gain_one, normed_one, inverse_one)

    down_g = mm("tf,td->fd", active, cot).astype(BF).reshape(4, unit, width)
    up_g = mm("td,tf->df", mlp_in, grad_hidden).astype(BF).reshape(devices, part, 4 * unit)
    qkv_g = mm("td,te->de", attn_in, grad_joined).astype(BF).reshape(devices, part, 3 * cols)
    flat = [down_g, out_g] if aligned else [down_g]
    *flat_c, up_c, qkv_c = hand(flat + [up_g, qkv_g], (False,) * len(flat) + (True, True), nz, 6)

    def mine(g, came):
        g = g.reshape((2, 2, nz, 2) + g.shape[1:])
        g = lax.dynamic_slice(g, (x, 0, 0, y, 0, 0), (1, 2, nz, 1) + g.shape[4:])
        g = g.reshape((2, nz) + g.shape[4:]).swapaxes(0, 1)
        return (g.reshape(came.shape[1:]).astype(F32) + jnp.sum(came.astype(F32), axis=0)).astype(BF)

    def mine_flat(g, came):
        return lax.dynamic_index_in_dim(g, x * 2 + y, 0, keepdims=False).astype(F32) + jnp.sum(came.astype(F32), axis=0)

    grad_down_w = mine_flat(down_g, flat_c[0])
    if aligned:
        grad_out_w = mine_flat(out_g, flat_c[1])
    up_s, qkv_s = mine(up_g, up_c), mine(qkv_g, qkv_c)

    up_s, qkv_s = exchange([up_s, qkv_s], nz, 7, "grads_to_owners")
    grad_up_w = up_s.reshape(nz, 2, part, 2, 2, unit).transpose(2, 3, 1, 0, 4, 5).reshape(part, -1).astype(F32)
    if aligned:
        grad_qkv_w = qkv_s.reshape(nz, 2, part, 3, 2, 2 * HD).transpose(2, 3, 4, 1, 0, 5)
    else:
        grad_qkv_w = qkv_s.reshape(fsdp, part, 3, cols).transpose(1, 2, 0, 3)
    grad_qkv_w = grad_qkv_w.reshape(part, -1).astype(F32)

    col = jnp.sum(grad_joined.astype(F32), axis=0)

    smalls = [
        jnp.sum(grad_attn_in * normed_one, axis=0),
        jnp.sum(grad_attn_in, axis=0),
        spread(col[:cols]),
        spread(col[2 * cols :]),
        jnp.sum(grad_branch.astype(F32), axis=0),
        jnp.sum(grad_mlp_in * normed_two, axis=0),
        jnp.sum(grad_mlp_in, axis=0),
        jnp.sum(cot_own, axis=0),
    ]
    grad_bias_up = jnp.sum(grad_hidden.astype(F32), axis=0).reshape(2, 1, 1, 2, unit)
    grad_bias_up = lax.dynamic_update_slice(jnp.zeros((2, 2, nz, 2, unit), F32), grad_bias_up, (0, c, z, 0, 0))
    squares = jnp.stack([jnp.sum(result * result), jnp.sum(branch * branch)])
    packed = jnp.concatenate(
        [v.reshape(devices, part) for v in smalls]
        + [grad_bias_up.reshape(devices, unit), jnp.broadcast_to(squares, (devices, 2))],
        axis=1,
    )
    packed = padded(packed, 1024).reshape(devices, -1, 128)
    layer_out, grad_x, packed = finish(result.astype(BF), grad_inputs.astype(BF), packed, nz, 8)
    packed = packed.reshape(-1)
    small = [packed[i * part : (i + 1) * part] for i in range(8)]
    up_at = 8 * part
    root_squares = jnp.sqrt(packed[up_at + unit : up_at + unit + 2] / (devices * rows * width))
    return (
        layer_out,
        grad_x,
        grad_qkv_w,
        grad_out_w,
        grad_up_w,
        grad_down_w,
        small[0],
        small[1],
        small[2],
        small[3],
        small[4],
        small[5],
        small[6],
        packed[up_at : up_at + unit],
        small[7],
        root_squares,
    )


def solution(mesh):
    matrix, vector, table = P(BOTH, None), P(BOTH), P("dp", None)
    return jax.shard_map(
        per_device,
        mesh=mesh,
        in_specs=(matrix,) * 6 + (vector,) * 9 + (table,) * 3,
        out_specs=(matrix,) * 6 + (vector,) * 9 + (P(),),
        check_vma=False,
    )
```

time: 1290 us -> 886 us (0.69)
  waiting for transfers between devices: 835 us -> 0.7 us
  Pallas kernels: 0 us -> 686 us
  blocking collectives: 154 us -> 0 us
  matrix products: 192 us -> 78.3 us
  other arithmetic: 25.9 us -> 47.8 us
  starting transfers between devices: 17.7 us -> 0.04 us
    pallas_call x0 -> x13, Pallas kernels: none -> 686 us  [the longest x1 172 us: fetch(): pl.pallas_call(functools.partial(fetch_kernel, nz, width, cols, unit), ou...]
    reduce_scatter x8 -> x0, waiting for transfers between devices: 417 us -> none  [the longest x3 235 us: scatter_tokens(): lax.psum_scatter(x.astype(BF), 'fsdp', scatter_dimension=0, tiled=True)]
    all_gather x6 -> x0, waiting for transfers between devices: 225 us -> none  [the longest x3 174 us: gather_tokens(): return lax.all_gather(x, 'fsdp', axis=0, tiled=True)]
    unnamed x17 -> x1, waiting for transfers between devices: 111 us -> 0.68 us
    dot_general x13 -> x8, matrix products: 148 us -> 53 us  [mm(): return jnp.einsum(spec, a, b, preferred_element_type=F32)]
    all_gather x1 -> x0, blocking collectives: 66.5 us -> none  [per_device(): vec = lax.all_gather(vec, BOTH, axis=0, tiled=False).astype(F32)]
    all_to_all x4 -> x0, waiting for transfers between devices: 52.4 us -> none  [the longest x1 33.8 us: to_rank(): lax.all_to_all(w, 'fsdp', split_axis=2, concat_axis=0, tiled=True)]
    all_to_all x2 -> x0, blocking collectives: 46 us -> none  [the longest x1 27.4 us: to_rank(): lax.all_to_all(w, 'fsdp', split_axis=2, concat_axis=0, tiled=True)]
  transfers between devices with their start and end apart: 20 -> 1, of which waited for: 15 -> 0; matrix products, arithmetic and copies ran while one was open for 18% -> 5% of each run, Pallas kernels for 0% -> 23%
where the time goes in v2:
time: 886 us; the launch traced here: 874 us
  Pallas kernels  686 us (77%)
  matrix products  78.3 us (9%)
  other arithmetic  47.8 us (5%)
  local copies, waits for them, and re-layouts  45.1 us (5%)
  between operations  15.3 us (2%)
    pallas_call x1, Pallas kernels, fetch(): pl.pallas_call(functools.partial(fetch_kernel, nz, width, cols, unit), ou...  172 us
    pallas_call x3, Pallas kernels, scatter_tokens(): pl.pallas_call(functools.partial(scatter_kernel, nz), out_shape=jax.Shape...  171 us
    pallas_call x1, Pallas kernels, hand(): pl.pallas_call(functools.partial(hand_kernel, nz, kinds), out_shape=[jax....  147 us
    pallas_call x2, Pallas kernels, gather_tokens(): pl.pallas_call(functools.partial(gather_kernel, nz), out_shape=jax.ShapeD...  85.1 us
    pallas_call x3, Pallas kernels, exchange(): pl.pallas_call(functools.partial(exchange_kernel, nz, len(arrays)), out_s...  62.5 us
    dot_general x8, matrix products, mm(): return jnp.einsum(spec, a, b, preferred_element_type=F32)  53 us
    pallas_call x1, Pallas kernels, attend_back(): pl.pallas_call(functools.partial(attend_back_kernel, heads), out_shape=[j...  23.6 us
  transfers between devices with their start and end apart: 1, of which 0 were waited for; matrix products, arithmetic and copies ran while one was open for 5% of the time, Pallas kernels for 23%

profile of v2, /device:TPU:0, one launch (start us, length us, event | category | flops | bytes accessed | tf_op | source)
XLA Modules:
  0.0 873.6 jit_solution(14008373514282496595)
XLA Ops:
  8.7 6.1 concatenate.15
  16.0 172.2 %fetch.1 = (bf16[8,128,2048]{2,1,0:T(8,128)(2,1)}, bf16[8,128,2048]{2,1,0:T(8,128)(2,1)}, bf16[32,64,768]{2,1,0:T(8,128)(2,1)}, bf16[32,64,1024]{2,1,0:T(8,128)(...) custom-call(bf16[128,2048]{1,0:T(8,128)(2,1)} %x_in.1, bf16[128,2048]{1,0:T(8,128)(2,1)} %cot.1, ...), custom_call_target="tpu_custom_call" | custom-call | tf_op jit(solution)/shard_map/fetch/pallas_call | solution.py:468
  193.5 3.7 reduce-window.6
  198.9 2.0 copy.60
  201.4 3.0 convert_reduce_fusion
  205.7 1.8 fusion.5
  207.5 6.3 convert_select_fusion
  213.8 4.5 add_convert_fusion.5.joined_q.joined
  218.3 14.5 %attend.1 = bf16[1024,256]{1,0:T(8,128)(2,1)} custom-call(f32[4]{0:T(128)} %reshape.423.slopes, f32[1024,1024]{1,0:T(8,128)} %get-tuple-element.86.far, bf16[1024,768]{1,0:T(8,128)(2,1)} %add_convert_fusion.5.joined_q.joined, bf16[1024,768]{1,0:T(8,128)(2,1)} %add_convert_fusion.5.joined_q.joined), custom_call_target="tpu_custom_call" | custom-call | flops 1073741824 | bytes 4194304 | tf_op jit(solution)/shard_map/attend/pallas_call | solution.py:654
  232.8 11.9 %mixed_to_tokens.1 = bf16[8,128,256]{2,1,0:T(8,128)(2,1)} custom-call(bf16[8,128,256]{2,1,0:T(8,128)(2,1)} %bitcast.150), custom_call_target="tpu_custom_call" | custom-call | tf_op jit(solution)/shard_map/mixed_to_tokens/pallas_call | solution.py:512
  248.0 5.6 fusion.57
  254.9 44.1 %gather_tokens.2 = bf16[8,128,2048]{2,1,0:T(8,128)(2,1)} custom-call(bf16[128,2048]{1,0:T(8,128)(2,1)} %add_convert_fusion.6.src), custom_call_target="tpu_custom_call" | custom-call | tf_op jit(solution)/shard_map/gather_tokens/pallas_call | solution.py:180
  299.0 8.0 fusion.61
  307.1 13.1 %convert_reduce_fusion.4 = (f32[1024]{0:T(1024)S(1)}, bf16[1024,1024]{0,1:T(8,128)(2,1)S(1)}, f32[1024,1024]{0,1:T(8,128)S(1)}) fusion(f32[1024,1024]{0,1:T(8,128)S(1)} %fusion.61, f32[1024]{0:T(1024)S(1)} %bitcast.164, bf16[1024,2048]{1,0:T(8,128)(2,1)S(1)} %bitcast.158, bf16[1024,2048]{1,0:T(8,128)(2,1)S(1)} %bitcast.170), kind=kOutput, calls=%fused_computation.19 | convolution fusion | flops 4373609472 | bytes 18882560 | tf_op jit(solution)/shard_map/td,fd->tf/dot_general | solution.py:777
  320.1 8.5 convolution_convert_fusion.3
  328.6 6.2 convolution_convert_fusion.2
  335.3 6.3 convolution_convert_fusion.4
  341.7 6.1 convolution_convert_fusion.1
  347.8 55.8 %scatter_tokens.3 = f32[128,2048]{1,0:T(8,128)} custom-call(bf16[8,128,2048]{2,1,0:T(8,128)(2,1)} %bitcast.139), custom_call_target="tpu_custom_call" | custom-call | tf_op jit(solution)/shard_map/scatter_tokens/pallas_call | solution.py:252
  403.6 58.6 %scatter_tokens.4 = f32[128,2048]{1,0:T(8,128)} custom-call(bf16[8,128,2048]{2,1,0:T(8,128)(2,1)} %bitcast.137), custom_call_target="tpu_custom_call" | custom-call | tf_op jit(solution)/shard_map/scatter_tokens/pallas_call | solution.py:252
  462.2 2.6 multiply_reduce_fusion.2
  464.8 2.5 convert_reduce_fusion.9
  467.3 41.0 %gather_tokens.3 = bf16[8,128,2048]{2,1,0:T(8,128)(2,1)} custom-call(bf16[128,2048]{1,0:T(8,128)(2,1)} %get-tuple-element.69.src), custom_call_target="tpu_custom_call" | custom-call | tf_op jit(solution)/shard_map/gather_tokens/pallas_call | solution.py:180
  508.3 6.3 convolution_convert_fusion.6
  516.5 12.5 %grad_to_heads.1 = bf16[8,128,256]{2,1,0:T(8,128)(2,1)} custom-call(bf16[8,128,256]{2,1,0:T(8,128)(2,1)} %reshape.399.refs_0_), custom_call_target="tpu_custom_call" | custom-call | tf_op jit(solution)/shard_map/grad_to_heads/pallas_call | solution.py:512
  529.0 23.6 %attend_back.1 = (bf16[1024,256]{1,0:T(8,128)(2,1)}, bf16[1024,256]{1,0:T(8,128)(2,1)}, bf16[1024,256]{1,0:T(8,128)(2,1)}) custom-call(f32[4]{0:T(128)} %reshape.423.slopes, f32[1024,1024]{1,0:T(8,128)} %get-tuple-element.85.far, bf16[1024,768]{1,0:T(8,128)(2,1)} %add_convert_fusion.5.joined_q.joined, bf16[1024,768]{1,0:T(8,128)(2,1)} %add_convert_fusion.5.joined_q.joined, ...), custom_call_target="tpu_custom_call" | custom-call | flops 2684354560 | bytes 4194304 | tf_op jit(solution)/shard_map/attend_back/pallas_call | solution.py:711
  555.9 5.0 convolution_convert_fusion
  561.2 57.0 %scatter_tokens.5 = f32[128,2048]{1,0:T(8,128)} custom-call(bf16[8,128,2048]{2,1,0:T(8,128)(2,1)} %bitcast.140), custom_call_target="tpu_custom_call" | custom-call | tf_op jit(solution)/shard_map/scatter_tokens/pallas_call | solution.py:252
  618.3 1.9 fusion.40
  620.9 1.4 pad_maximum_fusion.1
  622.5 2.0 fusion.39.grad
  624.5 9.8 %finish.1 = (bf16[128,2048]{1,0:T(8,128)(2,1)S(1)}, bf16[128,2048]{1,0:T(8,128)(2,1)S(1)}, f32[8,128]{1,0:T(8,128)S(1)}) custom-call(bf16[128,2048]{1,0:T(8,128)(2,1)S(1)} %get-tuple-element.75.res, bf16[128,2048]{1,0:T(8,128)(2,1)S(1)} %fusion.39.grad, f32[32,8,128]{2,1,0:T(8,128)S(1)} %bitcast.121), custom_call_target="tpu_custom_call" | custom-call | tf_op jit(solution)/shard_map/finish/pallas_call | solution.py:613
  636.0 2.3 convolution_convert_fusion.5
  638.2 5.6 fusion.25
  643.8 147.2 %hand.1 = (bf16[3,256,2048]{2,1,0:T(8,128)(2,1)}, bf16[3,64,2048]{2,1,0:T(8,128)(2,1)}, bf16[3,8,64,1024]{3,2,1,0:T(8,128)(2,1)}, bf16[3,8,64,768]{3,2,1,0:T(8,128)(2,1)}) custom-call(bf16[4,256,2048]{2,1,0:T(8,128)(2,1)} %bitcast.132, bf16[4,64,2048]{2,1,0:T(8,128)(2,1)} %bitcast.146, bf16[32,64,1024]{2,1,0:T(8,128)(2,1)} %bitcast.130, ...), custom_call_target="tpu_custom_call" | custom-call | tf_op jit(solution)/shard_map/hand/pallas_call | solution.py:564
  791.1 4.2 convert_reduce_fusion.1
  796.4 1.3 fusion.43
  797.6 1.5 fusion.42
  800.3 1.4 fusion.26.refs_0_
  801.7 38.1 %grads_to_owners.1 = (bf16[8,64,1024]{2,1,0:T(8,128)(2,1)}, bf16[8,64,768]{2,1,0:T(8,128)(2,1)}) custom-call(bf16[8,64,1024]{2,1,0:T(8,128)(2,1)} %fusion.26.refs_0_, bf16[8,64,768]{2,1,0:T(8,128)(2,1)} %fusion.27.refs_1_), custom_call_target="tpu_custom_call" | custom-call | tf_op jit(solution)/shard_map/grads_to_owners/pallas_call | solution.py:512
  839.8 4.1 reshape.433
  843.9 4.2 copy.71
  848.2 3.9 reshape.428
  852.2 3.6 convert_add_fusion
  855.7 1.8 convert_add_fusion.3
  857.5 2.0 reshape.432
  859.6 2.2 copy.70
  861.7 2.9 reshape.426
  (141 shorter events, 28.3 us)
Async XLA Ops:
  7.2 240.8 %all-gather.2.cloned.1.call-start = ((), (), s32[]{:S(2)}) async-start(), calls=%async_computation | async-start | bytes 8650752 | tf_op jit(solution)/shard_map/all_gather | solution.py:822
  197.9 3.4 copy-start.14
  200.9 3.6 copy-start
  207.5 6.3 copy-start.16
  299.0 8.0 copy-start.13
  299.0 8.0 copy-start.15
  320.1 8.5 copy-start.6
  403.6 58.6 %copy-start.4 = (f32[128,2048]{1,0:T(8,128)S(1)}, f32[128,2048]{1,0:T(8,128)}, u32[]{:S(2)}) copy-start(f32[128,2048]{1,0:T(8,128)} %scatter_tokens.3) | copy-start | bytes 3145732
  462.2 2.6 copy-start.2
  467.3 41.0 %copy-start.3 = (bf16[128,2048]{1,0:T(8,128)(2,1)S(1)}, bf16[128,2048]{1,0:T(8,128)(2,1)}, u32[]{:S(2)}) copy-start(bf16[128,2048]{1,0:T(8,128)(2,1)} %get-tuple-element.69.src) | copy-start | bytes 1572868
  529.0 26.9 %copy-start.17 = (bf16[32,64,768]{2,1,0:T(8,128)(2,1)S(1)}, bf16[32,64,768]{2,1,0:T(8,128)(2,1)}, u32[]{:S(2)}) copy-start(bf16[32,64,768]{2,1,0:T(8,128)(2,1)} %get-tuple-element.38) | copy-start | bytes 9437188
  555.9 5.1 copy-start.8
  618.3 17.7 %copy-start.12 = (bf16[1024,256]{1,0:T(8,128)(2,1)S(1)}, bf16[1024,256]{1,0:T(8,128)(2,1)}, u32[]{:S(2)}) copy-start(bf16[1024,256]{1,0:T(8,128)(2,1)} %attend.1) | copy-start | bytes 1572868
  622.4 13.6 %copy-start.5 = (bf16[8,128,2048]{2,1,0:T(8,128)(2,1)S(1)}, bf16[8,128,2048]{2,1,0:T(8,128)(2,1)}, u32[]{:S(2)}) copy-start(bf16[8,128,2048]{2,1,0:T(8,128)(2,1)} %gather_tokens.3) | copy-start | bytes 12582916
  624.4 13.8 %copy-start.1 = (bf16[8,128,2048]{2,1,0:T(8,128)(2,1)S(1)}, bf16[8,128,2048]{2,1,0:T(8,128)(2,1)}, u32[]{:S(2)}) copy-start(bf16[8,128,2048]{2,1,0:T(8,128)(2,1)} %get-tuple-element.35) | copy-start | bytes 12582916
  624.4 13.8 %copy-start.9 = (bf16[1024,768]{1,0:T(8,128)(2,1)S(1)}, bf16[1024,768]{1,0:T(8,128)(2,1)}, u32[]{:S(2)}) copy-start(bf16[1024,768]{1,0:T(8,128)(2,1)} %copy-done.8) | copy-start | bytes 4718596
  791.0 4.3 copy-start.10
  791.1 4.6 copy-start.7
  843.9 8.1 copy-start.11
Sparse Core Ops, SparseCore 0:
  11.0 141.6 all-gather.1

commit v3 on v2

--- a/solution.py
+++ b/solution.py
@@ -188,10 +188,8 @@
     )(a)
 
 
-def scatter_kernel(nz, p, out, acc, ups, dns, send, recv):
-    pos = place()
+def scatter_blocks(nz, pos, p, out, acc, ups, dns, send, recv):
     x, c, z, y = pos
-    greet(line_partners(nz, pos))
     sib = at(x, 1 - c, z, y)
     S, U, D = 0, nz, 2 * nz
 
@@ -247,6 +245,16 @@
         pl.when(z > t)(dn(t).wait_send)
 
 
+def scatter_scratch(nz, rows, width):
+    return [pltpu.VMEM((nz, rows, width), BF)] * 3 + [pltpu.SemaphoreType.DMA((3 * nz,))] * 2
+
+
+def scatter_kernel(nz, p, out, *scratch):
+    pos = place()
+    greet(line_partners(nz, pos))
+    scatter_blocks(nz, pos, p, out, *scratch)
+
+
 def scatter_tokens(p, nz, cid):
     blocks, rows, width = p.shape
     return pl.pallas_call(
@@ -254,31 +262,79 @@
         out_shape=jax.ShapeDtypeStruct((rows, width), F32),
         in_specs=[VM],
         out_specs=VM,
-        scratch_shapes=[pltpu.VMEM((nz, rows, width), BF)] * 3 + [pltpu.SemaphoreType.DMA((3 * nz,))] * 2,
+        scratch_shapes=scatter_scratch(nz, rows, width),
         compiler_params=params(cid, 60 * MIB),
         name="scatter_tokens",
     )(p)
 
 
+def scatter_and_hand_kernel(nz, kinds, runs, p, up_s, res, *refs):
+    count = len(kinds)
+    srcs, refs = refs[:count], refs[count:]
+    out, up_o, res_o, refs = *refs[:3], refs[3:]
+    dsts, refs = refs[:count], refs[count:]
+    scratch, hsems, esems, tsems = refs[:5], refs[5:7], refs[7:9], refs[9:11]
+    pos = place()
+    x, c, z, y = pos
+    greet(rank_partners(nz, pos) + group_partners(pos) + [(c != y, at(x, y, z, c))])
+    hs = hand_stages(srcs, dsts, kinds, *hsems, nz, pos)
+    es = exchange_stages(up_s, up_o, runs, *esems, nz, pos)
+    ts = trade_stages(res, res_o, *tsems, pos)
+    hs[0]()
+    es[0]()
+    ts[0]()
+    scatter_blocks(nz, pos, p, out, *scratch)
+    hs[1]()
+    es[1]()
+    ts[1]()
+
+
+def scatter_and_hand(p, up_s, runs, res, arrays, kinds, nz, cid):
+    blocks, rows, width = p.shape
+    n, part, share = up_s.shape
+    return pl.pallas_call(
+        functools.partial(scatter_and_hand_kernel, nz, kinds, runs),
+        out_shape=[
+            jax.ShapeDtypeStruct((rows, width), F32),
+            jax.ShapeDtypeStruct((part, n * share), BF),
+            jax.ShapeDtypeStruct(res.shape, BF),
+        ]
+        + hand_shapes(arrays, kinds, nz),
+        in_specs=[VM] + [HBM] * (2 + len(arrays)),
+        out_specs=[VM] + [HBM] * (2 + len(arrays)),
+        scratch_shapes=scatter_scratch(nz, rows, width) + hand_sems(kinds) + exchange_sems(runs, nz) + trade_sems(),
+        compiler_params=params(cid, 60 * MIB),
+        name="scatter_and_hand",
+    )(p, up_s, res, *arrays)
+
+
 def block_of(x, c, z, y, nz):
     return (x * 2 + c) * 2 * nz + z * 2 + y
 
 
-def sliced_gather(src, dst, cuts, sems, nz, pos):
+def halves(ref, rows):
+    half = rows // 2
+    if half % 16:
+        return {1: None, 2: ref}
+    return {1: ref.at[pl.ds(half, half)], 2: ref.at[pl.ds(0, half)]}
+
+
+def sliced_gather(src, dst, runs, sems, nz, pos):
     x, c, z, y = pos
     n = 2 * nz
     me = z * 2 + c
+    part = dst.shape[1]
     send1, recv1, send2, recv2 = sems
 
     def pieces(p):
-        if cuts is None:
+        if runs is None:
             return [(src.at[p], slice(None))]
-        return [(src.at[:, a], b) for a, b in cuts(p)]
+        return [(src.at[:, pl.ds(there, size)], pl.ds(here, size)) for there, here, size in runs(p)]
 
     def row(p, gx, gy):
-        return block_of(gx, p % 2, p // 2, gy, nz)
-
-    mine = row(me, x, y)
+        return dst.at[block_of(gx, p % 2, p // 2, gy, nz)]
+
+    mine = block_of(x, c, z, y, nz)
 
     def out(k):
         p = (me + k) % n
@@ -287,17 +343,28 @@
             for a, b in pieces(p)
         ]
 
-    def whole(p, gx, gy, sem):
-        b = dst.at[row(p, gx, gy)]
+    local = [pltpu.make_async_copy(a, dst.at[mine, :, b], recv1.at[me]) for a, b in pieces(me)]
+
+    def came(k):
+        return (me - k + n) % n
+
+    def arrival(b, sem):
         return remote(b, b, send1.at[me], sem, at(x, 1 - c, z, y))
 
-    local = [pltpu.make_async_copy(a, dst.at[mine, :, b], recv1.at[me]) for a, b in pieces(me)]
+    def neighbour(m):
+        return at(x ^ (m // 2), c, z, y ^ (m % 2))
 
     def forward(k, m):
-        p = (me - k + n) % n
-        b = dst.at[row(p, x, y)]
+        p = came(k)
+        b = row(p, x, y)
         slot = (m - 1) * n + p
-        return remote(b, b, send2.at[slot], recv2.at[slot], at(x ^ (m // 2), c, z, y ^ (m % 2)))
+        return remote(b, b, send2.at[slot], recv2.at[slot], neighbour(m))
+
+    def relay(k, m):
+        p = came(k)
+        b = halves(row(p, x ^ (m // 2), y ^ (m % 2)), part)[m]
+        slot = (1 + m) * n + p
+        return b is not None and remote(b, b, send2.at[slot], recv2.at[slot], neighbour(3 - m))
 
     def first():
         for copy in local:
@@ -307,56 +374,208 @@
                 copy.start()
 
     def step(k):
-        p = (me - k + n) % n
-        whole(p, x, y, recv1.at[p]).wait_recv()
-        for m in (3, 1, 2):
+        p = came(k)
+        arrival(row(p, x, y), recv1.at[p]).wait_recv()
+        for m in (1, 2):
             forward(k, m).start()
+
+    def pass_on(k):
+        p = came(k)
+        for m in (1, 2):
+            arrival(row(p, x ^ (m // 2), y ^ (m % 2)), recv2.at[(m - 1) * n + p]).wait_recv()
+            if relay(k, m):
+                relay(k, m).start()
 
     def last():
         for k in range(n):
-            p = (me - k + n) % n
-            for m in (1, 2, 3):
-                slot = (m - 1) * n + p
-                whole(p, x ^ (m // 2), y ^ (m % 2), recv2.at[slot]).wait_recv()
+            p = came(k)
+            parts = halves(row(p, 1 - x, 1 - y), part)
+            for m in (1, 2):
+                if parts[m] is not None:
+                    arrival(parts[m], recv2.at[(1 + m) * n + p]).wait_recv()
         for k in range(n):
             if k:
                 p = (me + k) % n
-                whole_send = remote(
-                    dst.at[mine], dst.at[mine], send1.at[p], recv1.at[me], at(x, p % 2, p // 2, y)
-                )
-                whole_send.wait_send()
-            for m in (1, 2, 3):
+                b = dst.at[mine]
+                remote(b, b, send1.at[p], recv1.at[me], at(x, p % 2, p // 2, y)).wait_send()
+            for m in (1, 2):
                 forward(k, m).wait_send()
-
-    return [first] + [functools.partial(step, k) for k in range(n)] + [last]
+                if relay(k, m):
+                    relay(k, m).wait_send()
+
+    stages = [functools.partial(step, k) for k in range(n)] + [functools.partial(pass_on, k) for k in range(n)]
+    return [first] + stages + [last]
 
 
 def sliced_sems(nz):
     n = 2 * nz
-    return [pltpu.SemaphoreType.DMA((n,))] * 2 + [pltpu.SemaphoreType.DMA((3 * n,))] * 2
+    return [pltpu.SemaphoreType.DMA((n,))] * 2 + [pltpu.SemaphoreType.DMA((4 * n,))] * 2
 
 
 def group_gather(src, dst, send, recv, pos):
     x, c, z, y = pos
-    g = x * 2 + y
-    local = pltpu.make_async_copy(src, dst.at[g], recv.at[0])
+    rows = src.shape[0]
+    local = pltpu.make_async_copy(src, dst.at[x * 2 + y], recv.at[0])
+
+    def there(m):
+        return dst.at[(x ^ (m // 2)) * 2 + (y ^ (m % 2))]
+
+    def neighbour(m):
+        return at(x ^ (m // 2), c, z, y ^ (m % 2))
 
     def out(m):
-        return remote(src, dst.at[g], send.at[m], recv.at[m], at(x ^ (m // 2), c, z, y ^ (m % 2)))
+        return remote(src, dst.at[x * 2 + y], send.at[m], recv.at[m], neighbour(m))
+
+    def relay(m):
+        b = halves(there(m), rows)[m]
+        return b is not None and remote(b, b, send.at[2 + m], recv.at[2 + m], neighbour(3 - m))
+
+    def arrival(b, sem):
+        return remote(b, b, send.at[0], sem, at(x, 1 - c, z, y))
 
     def first():
         local.start()
-        for m in (3, 1, 2):
+        for m in (1, 2):
             out(m).start()
+
+    def pass_on():
+        for m in (1, 2):
+            arrival(there(m), recv.at[m]).wait_recv()
+            if relay(m):
+                relay(m).start()
 
     def last():
         local.wait()
-        for m in (1, 2, 3):
-            there = dst.at[(x ^ (m // 2)) * 2 + (y ^ (m % 2))]
-            remote(there, there, send.at[m], recv.at[m], at(x, 1 - c, z, y)).wait_recv()
+        parts = halves(there(3), rows)
+        for m in (1, 2):
+            if parts[m] is not None:
+                arrival(parts[m], recv.at[2 + m]).wait_recv()
             out(m).wait_send()
-
-    return [first, last]
+            if relay(m):
+                relay(m).wait_send()
+
+    return [first, pass_on, last]
+
+
+def full_gather(src, dst, send, recv, nz, pos):
+    x, c, z, y = pos
+    rows = src.shape[0]
+    sib = at(x, 1 - c, z, y)
+    mine = dst.at[block_of(x, c, z, y, nz)]
+
+    def row(core, k, m):
+        return dst.at[block_of(x ^ (m // 2), core, z + k, y ^ (m % 2), nz)]
+
+    def neighbour(m):
+        return at(x ^ (m // 2), c, z, y ^ (m % 2))
+
+    def arrival(b, sem):
+        return remote(b, b, send.at[0], recv.at[sem], sib)
+
+    def along(k, sign):
+        b = row(c, k, 0)
+        return remote(
+            b if k else src, b, send.at[(0 if sign > 0 else nz) + z + k], recv.at[z + k], at(x, c, z + sign, y)
+        )
+
+    def forward(k, m):
+        b = row(c, k, 0)
+        return remote(b if k else src, b, send.at[(1 + m) * nz + z + k], recv.at[m * nz + z + k], neighbour(m))
+
+    def relay(k, m):
+        b = halves(row(c, k, m), rows)[m]
+        if b is None:
+            return None
+        return remote(b, b, send.at[(3 + m) * nz + z + k], recv.at[(2 + m) * nz + z + k], neighbour(3 - m))
+
+    def side(k, m):
+        b = row(c, k, m)
+        return remote(b if k or m else src, b, send.at[(6 + m) * nz + z + k], recv.at[(5 + m) * nz + z + k], sib)
+
+    local = pltpu.make_async_copy(src, mine, recv.at[z])
+
+    def first():
+        local.start()
+        pl.when(z < nz - 1)(along(0, 1).start)
+        pl.when(z > 0)(along(0, -1).start)
+        for m in (1, 2):
+            forward(0, m).start()
+        side(0, 0).start()
+
+    def both(k, fn):
+        @pl.when(z >= k)
+        def _():
+            fn(-k)
+
+        if k:
+
+            @pl.when(z + k < nz)
+            def _():
+                fn(k)
+
+    def step(k):
+        def one(k):
+            arrival(row(c, k, 0), z + k).wait_recv()
+            if k > 0:
+                pl.when(z > 0)(along(k, -1).start)
+            else:
+                pl.when(z < nz - 1)(along(k, 1).start)
+            for m in (1, 2):
+                forward(k, m).start()
+            side(k, 0).start()
+
+        both(k, one)
+
+    def pass_on(k):
+        def one(k):
+            for m in (1, 2):
+                arrival(row(c, k, m), m * nz + z + k).wait_recv()
+                if relay(k, m) is not None:
+                    relay(k, m).start()
+                side(k, m).start()
+
+        both(k, one)
+
+    def diagonal(k):
+        def one(k):
+            parts = halves(row(c, k, 3), rows)
+            for m in (1, 2):
+                if parts[m] is not None:
+                    arrival(parts[m], (2 + m) * nz + z + k).wait_recv()
+            side(k, 3).start()
+
+        both(k, one)
+
+    def last():
+        local.wait()
+
+        def one(k):
+            for m in range(4):
+                arrival(row(1 - c, k, m), (5 + m) * nz + z + k).wait_recv()
+                side(k, m).wait_send()
+            if k >= 0:
+                pl.when(z > 0)(along(k, -1).wait_send)
+            if k <= 0:
+                pl.when(z < nz - 1)(along(k, 1).wait_send)
+            for m in (1, 2):
+                forward(k, m).wait_send()
+                if relay(k, m) is not None:
+                    relay(k, m).wait_send()
+
+        for k in range(nz):
+            both(k, one)
+
+    return (
+        [first]
+        + [functools.partial(step, k) for k in range(1, nz)]
+        + [functools.partial(pass_on, k) for k in range(nz)]
+        + [functools.partial(diagonal, k) for k in range(nz)]
+        + [last]
+    )
+
+
+def full_sems(nz):
+    return [pltpu.SemaphoreType.DMA((10 * nz,)), pltpu.SemaphoreType.DMA((9 * nz,))]
 
 
 def head_runs(nz, cols):
@@ -365,36 +584,24 @@
     ]
 
 
-def qkv_cuts(nz, width, cols):
+def up_runs(nz, unit):
+    return lambda p: [(block_of(x, p % 2, p // 2, 0, nz) * unit, x * 2 * unit, 2 * unit) for x in range(2)]
+
+
+def qkv_runs(nz, width, cols):
     runs = head_runs(nz, cols)
-    return lambda p: [
-        (pl.ds(j * width + there, size), pl.ds(j * cols + here, size)) for j in range(3) for there, here, size in runs(p)
-    ]
-
-
-def up_cuts(nz, unit):
-    def cuts(p):
-        z, c = p // 2, p % 2
-        return [
-            (pl.ds(((x * 2 + c) * 2 * nz + z * 2) * unit, 2 * unit), pl.ds(x * 2 * unit, 2 * unit))
-            for x in range(2)
-        ]
-
-    return cuts
+    return lambda p: [(j * width + there, j * cols + here, size) for j in range(3) for there, here, size in runs(p)]
 
 
 def fetch_kernel(
-    nz, width, cols, unit, x_in, cot, w_qkv, w_up, w_down, vec, tab,
-    x_all, cot_all, qkv_w, up_w, down_w, vecs, tab_out, *sems,
+    nz, width, cols, x_in, w_qkv, w_down, vec, tab, x_all, qkv_w, down_w, vecs, tab_out, *sems
 ):
     pos = place()
     x, c, z, y = pos
     fsdp = 2 * nz
     devices = 4 * fsdp
     me = (x * 2 + c) * fsdp + z * 2 + y
-    sems = list(sems)
-    x_sems, cot_sems, qkv_sems, up_sems = sems[:2], sems[2:4], sems[4:8], sems[8:12]
-    down_sems, vec_sems, tab_sems = sems[12:14], sems[14:16], sems[16:18]
+    x_sems, qkv_sems, vec_sems, tab_sems, down_sems = sems[:2], sems[2:6], sems[6:8], sems[8:10], sems[10:]
     greet_all(devices, fsdp, me)
 
     def vec_copy(other):
@@ -412,11 +619,8 @@
     tab_trade = remote(tab, tab_out, tab_sems[0].at[0], tab_sems[1].at[0], at(x, y, z, c))
 
     gx = line_gather(x_in, x_all, *x_sems, nz, True, pos)
-    gc = line_gather(cot, cot_all, *cot_sems, nz, True, pos)
-    cuts = qkv_cuts(nz, width, cols) if len(w_qkv.shape) == 2 else None
-    gq = sliced_gather(w_qkv, qkv_w, cuts, qkv_sems, nz, pos)
-    gu = sliced_gather(w_up, up_w, up_cuts(nz, unit), up_sems, nz, pos)
-    gd = group_gather(w_down, down_w, *down_sems, pos)
+    runs = qkv_runs(nz, width, cols) if len(w_qkv.shape) == 2 else None
+    gq = sliced_gather(w_qkv, qkv_w, runs, qkv_sems, nz, pos)
     gx[0]()
     gq[0]()
     gx[1]()
@@ -424,21 +628,18 @@
     each(lambda other: vec_copy(other).start())
     pl.when(c == y)(tab_local.start)
     pl.when(c != y)(tab_trade.start)
+    gd = group_gather(w_down, down_w, *down_sems, pos)
+    for stage in gq[1 : fsdp + 1]:
+        stage()
+    gx[2]()
     gd[0]()
-    gc[0]()
-    gu[0]()
-    for k in range(1, fsdp + 1):
-        gq[k]()
-    for stage in gx[2:]:
+    for stage in gx[3:-1]:
         stage()
-    gc[1]()
-    for k in range(1, fsdp + 1):
-        gu[k]()
-    for stage in gc[2:]:
+    for stage in gq[fsdp + 1 :]:
         stage()
-    gq[-1]()
-    gu[-1]()
-    gd[-1]()
+    gx[-1]()
+    for stage in gd[1:]:
+        stage()
 
     def vec_done(other):
         remote(vec, vecs.at[other], vec_sems[0].at[other], vec_sems[1].at[other], at(x, 1 - c, z, y)).wait_recv()
@@ -450,83 +651,37 @@
     pl.when(c != y)(tab_trade.wait_send)
 
 
-def fetch(nz, x_in, cot, w_qkv, w_up, w_down, vec, tab, cid):
+def fetch(nz, x_in, w_qkv, w_down, part, vec, tab, cid):
     rows, width = x_in.shape
     n = 2 * nz
     devices = 4 * n
-    part, unit = w_up.shape[0], w_down.shape[0]
     cols = width // n
     shapes = [
         ((n, rows, width), BF),
-        ((n, rows, width), BF),
         ((devices, part, 3 * cols), BF),
-        ((devices, part, 4 * unit), BF),
-        ((4, unit, width), BF),
+        ((4,) + w_down.shape, BF),
         ((devices,) + vec.shape, F32),
         (tab.shape, jnp.int32),
     ]
     return pl.pallas_call(
-        functools.partial(fetch_kernel, nz, width, cols, unit),
+        functools.partial(fetch_kernel, nz, width, cols),
         out_shape=[jax.ShapeDtypeStruct(s, t) for s, t in shapes],
-        in_specs=[HBM] * 7,
-        out_specs=[HBM] * 7,
-        scratch_shapes=gather_sems(nz) * 2
-        + sliced_sems(nz) * 2
-        + [pltpu.SemaphoreType.DMA((4,))] * 2
+        in_specs=[HBM] * 5,
+        out_specs=[HBM] * 5,
+        scratch_shapes=gather_sems(nz)
+        + sliced_sems(nz)
         + [pltpu.SemaphoreType.DMA((devices,))] * 2
-        + [pltpu.SemaphoreType.DMA((1,))] * 2,
+        + [pltpu.SemaphoreType.DMA((1,))] * 2
+        + [pltpu.SemaphoreType.DMA((5,))] * 2,
         compiler_params=params(cid),
         name="fetch",
-    )(x_in, cot, w_qkv, w_up, w_down, vec, tab)
-
-
-def exchange_kernel(nz, count, *refs):
-    srcs, dsts, (send, recv) = refs[:count], refs[count : 2 * count], refs[2 * count :]
-    pos = place()
+    )(x_in, w_qkv, w_down, vec, tab)
+
+
+def hand_stages(srcs, dsts, kinds, send, recv, nz, pos):
     x, c, z, y = pos
     n = 2 * nz
-    me = z * 2 + c
-    greet(rank_partners(nz, pos))
-
-    def move(i, p):
-        return remote(srcs[i].at[p], dsts[i].at[me], send.at[i * n + p], recv.at[i * n + me], at(x, p % 2, p // 2, y))
-
-    def come(i, p):
-        there = dsts[i].at[p]
-        return remote(there, there, send.at[i * n + me], recv.at[i * n + p], at(x, 1 - c, z, y))
-
-    local = [pltpu.make_async_copy(s.at[me], d.at[me], recv.at[i * n + me]) for i, (s, d) in enumerate(zip(srcs, dsts))]
-    for i in range(count):
-        local[i].start()
-        for k in range(1, n):
-            move(i, (me + k) % n).start()
-    for i in range(count):
-        local[i].wait()
-        for k in range(1, n):
-            come(i, (me - k + n) % n).wait_recv()
-            move(i, (me + k) % n).wait_send()
-
-
-def exchange(arrays, nz, cid, name):
-    n = 2 * nz
-    return pl.pallas_call(
-        functools.partial(exchange_kernel, nz, len(arrays)),
-        out_shape=[jax.ShapeDtypeStruct(a.shape, a.dtype) for a in arrays],
-        in_specs=[HBM] * len(arrays),
-        out_specs=[HBM] * len(arrays),
-        scratch_shapes=[pltpu.SemaphoreType.DMA((len(arrays) * n,))] * 2,
-        compiler_params=params(cid),
-        name=name,
-    )(*arrays)
-
-
-def hand_kernel(nz, kinds, *refs):
     count = len(kinds)
-    srcs, dsts, (send, recv) = refs[:count], refs[count : 2 * count], refs[2 * count :]
-    pos = place()
-    x, c, z, y = pos
-    n = 2 * nz
-    greet(group_partners(pos))
 
     def copies(i, m):
         gx, gy = x ^ (m // 2), y ^ (m % 2)
@@ -545,39 +700,132 @@
             for p in range(n)
         ]
 
-    for i in range(count):
-        for m in (3, 1, 2):
-            for copy in copies(i, m):
+    def first():
+        for i in range(count):
+            for m in (3, 1, 2):
+                for copy in copies(i, m):
+                    copy.start()
+
+    def last():
+        for i in range(count):
+            for m in (1, 2, 3):
+                sem = i * 3 + m - 1
+                there = dsts[i].at[m - 1]
+                whole = remote(there, there, send.at[sem], recv.at[sem], at(x, 1 - c, z, y))
+                whole.wait_recv()
+                whole.wait_send()
+
+    return [first, last]
+
+
+def hand_shapes(arrays, kinds, nz):
+    return [
+        jax.ShapeDtypeStruct((3, 2 * nz) + a.shape[1:] if k else (3,) + a.shape[1:], a.dtype)
+        for a, k in zip(arrays, kinds)
+    ]
+
+
+def hand_sems(kinds):
+    return [pltpu.SemaphoreType.DMA((3 * len(kinds),))] * 2
+
+
+def exchange_stages(src, dst, runs, send, recv, nz, pos):
+    x, c, z, y = pos
+    n = 2 * nz
+    me = z * 2 + c
+
+    def give(to, p):
+        if runs is None:
+            return [(src.at[to], dst.at[p])]
+        return [(src.at[to, :, pl.ds(here, size)], dst.at[:, pl.ds(there, size)]) for there, here, size in runs(p)]
+
+    width = len(give(0, 0))
+
+    def move(p):
+        return [
+            remote(a, b, send.at[p * width + i], recv.at[me * width + i], at(x, p % 2, p // 2, y))
+            for i, (a, b) in enumerate(give(p, me))
+        ]
+
+    def come(p):
+        return [
+            remote(b, b, send.at[me * width + i], recv.at[p * width + i], at(x, 1 - c, z, y))
+            for i, (_, b) in enumerate(give(me, p))
+        ]
+
+    local = [pltpu.make_async_copy(a, b, recv.at[me * width + i]) for i, (a, b) in enumerate(give(me, me))]
+
+    def first():
+        for copy in local:
+            copy.start()
+        for k in range(1, n):
+            for copy in move((me + k) % n):
                 copy.start()
-    for i in range(count):
-        for m in (1, 2, 3):
-            sem = i * 3 + m - 1
-            there = dsts[i].at[m - 1]
-            whole = remote(there, there, send.at[sem], recv.at[sem], at(x, 1 - c, z, y))
-            whole.wait_recv()
-            whole.wait_send()
-
-
-def hand(arrays, kinds, nz, cid):
-    n = 2 * nz
-    shapes = [(3, n) + a.shape[1:] if k else (3,) + a.shape[1:] for a, k in zip(arrays, kinds)]
+
+    def last():
+        for copy in local:
+            copy.wait()
+        for k in range(1, n):
+            for copy in come((me - k + n) % n):
+                copy.wait_recv()
+            for copy in move((me + k) % n):
+                copy.wait_send()
+
+    return [first, last]
+
+
+def exchange_sems(runs, nz):
+    width = 1 if runs is None else len(runs(0))
+    return [pltpu.SemaphoreType.DMA((width * 2 * nz,))] * 2
+
+
+def exchange_kernel(nz, src, dst, send, recv):
+    pos = place()
+    greet(rank_partners(nz, pos))
+    for stage in exchange_stages(src, dst, None, send, recv, nz, pos):
+        stage()
+
+
+def exchange(a, nz, cid, name):
     return pl.pallas_call(
-        functools.partial(hand_kernel, nz, kinds),
-        out_shape=[jax.ShapeDtypeStruct(s, a.dtype) for s, a in zip(shapes, arrays)],
-        in_specs=[HBM] * len(arrays),
-        out_specs=[HBM] * len(arrays),
-        scratch_shapes=[pltpu.SemaphoreType.DMA((3 * len(arrays),))] * 2,
+        functools.partial(exchange_kernel, nz),
+        out_shape=jax.ShapeDtypeStruct(a.shape, a.dtype),
+        in_specs=[HBM],
+        out_specs=HBM,
+        scratch_shapes=exchange_sems(None, nz),
         compiler_params=params(cid),
-        name="hand",
-    )(*arrays)
-
-
-def finish_kernel(nz, res, grad, small, res_out, grad_out, small_out, came, send, recv):
+        name=name,
+    )(a)
+
+
+def trade_stages(src, dst, send, recv, pos):
+    x, c, z, y = pos
+    local = pltpu.make_async_copy(src, dst, recv.at[0])
+    trade = remote(src, dst, send.at[0], recv.at[0], at(x, y, z, c))
+
+    def first():
+        pl.when(c == y)(local.start)
+        pl.when(c != y)(trade.start)
+
+    def last():
+        local.wait()
+        pl.when(c != y)(trade.wait_send)
+
+    return [first, last]
+
+
+def trade_sems():
+    return [pltpu.SemaphoreType.DMA((1,))] * 2
+
+
+def finish_kernel(nz, runs, grad, small, qkv_s, grad_out, small_out, qkv_o, came, send, recv, *sems):
     pos = place()
     x, c, z, y = pos
     fsdp = 2 * nz
     devices = 4 * fsdp
     me = (x * 2 + c) * fsdp + z * 2 + y
+    es = exchange_stages(qkv_s, qkv_o, runs, *sems[:2], nz, pos)
+    ts = trade_stages(grad, grad_out, *sems[2:], pos)
     greet_all(devices, fsdp, me)
 
     def each(fn):
@@ -590,11 +838,9 @@
     def share(other):
         return remote(small.at[other], came.at[me], send.at[other], recv.at[me], (other // fsdp, other % fsdp))
 
+    es[0]()
+    ts[0]()
     each(lambda other: share(other).start())
-    homes = [(res, res_out, devices), (grad, grad_out, devices + 1)]
-    for src, dst, sem in homes:
-        pl.when(c == y)(pltpu.make_async_copy(src, dst, recv.at[sem]).start)
-        pl.when(c != y)(remote(src, dst, send.at[sem], recv.at[sem], at(x, y, z, c)).start)
 
     def done(other):
         remote(small.at[me], came.at[other], send.at[other], recv.at[other], at(x, 1 - c, z, y)).wait_recv()
@@ -603,26 +849,29 @@
     each(done)
     came[me] = small[me]
     small_out[...] = jnp.sum(came[...], axis=0)
-    for src, dst, sem in homes:
-        pltpu.make_async_copy(src, dst, recv.at[sem]).wait()
-        pl.when(c != y)(remote(src, dst, send.at[sem], recv.at[sem], at(x, y, z, c)).wait_send)
-
-
-def finish(res, grad, small, nz, cid):
+    ts[1]()
+    es[1]()
+
+
+def finish(grad, small, qkv_s, runs, nz, cid):
     devices = small.shape[0]
+    out_shape = qkv_s.shape if runs is None else (qkv_s.shape[1], qkv_s.shape[0] * qkv_s.shape[2])
     return pl.pallas_call(
-        functools.partial(finish_kernel, nz),
+        functools.partial(finish_kernel, nz, runs),
         out_shape=[
-            jax.ShapeDtypeStruct(res.shape, res.dtype),
             jax.ShapeDtypeStruct(grad.shape, grad.dtype),
             jax.ShapeDtypeStruct(small.shape[1:], F32),
+            jax.ShapeDtypeStruct(out_shape, BF),
         ],
-        in_specs=[HBM, HBM, VM],
-        out_specs=[HBM, HBM, VM],
-        scratch_shapes=[pltpu.VMEM(small.shape, F32)] + [pltpu.SemaphoreType.DMA((devices + 2,))] * 2,
+        in_specs=[HBM, VM, HBM],
+        out_specs=[HBM, VM, HBM],
+        scratch_shapes=[pltpu.VMEM(small.shape, F32)]
+        + [pltpu.SemaphoreType.DMA((devices,))] * 2
+        + exchange_sems(runs, nz)
+        + trade_sems(),
         compiler_params=params(cid, 32 * MIB),
         name="finish",
-    )(res, grad, small)
+    )(grad, small, qkv_s)
 
 
 def dot(a, b, dims):
@@ -634,8 +883,36 @@
 TN = ((0,), (0,))
 
 
-def attend_kernel(heads, slopes, far, joined_q, joined, out):
+def attend_kernel(
+    heads, nz, unit, slopes, far, joined_q, joined, cot, w_up, w_out, out, cot_all, up_w, out_w, *sems
+):
     cols = heads * HD
+    step, steps = pl.program_id(0), pl.num_programs(0)
+    pos = place()
+    n = 2 * nz
+    gc = line_gather(cot, cot_all, *sems[:2], nz, True, pos)
+    gu = sliced_gather(w_up, up_w, up_runs(nz, unit), sems[2:6], nz, pos)
+    go = full_gather(w_out, out_w, *sems[6:8], nz, pos)
+
+    @pl.when(step == 0)
+    def _():
+        x, c, z, y = pos
+        greet(rank_partners(nz, pos) + group_partners(pos) + [(c != y, at(x, y, z, c))])
+        gc[0]()
+        gu[0]()
+        go[0]()
+
+    @pl.when(step == 1)
+    def _():
+        for stage in go[1:nz]:
+            stage()
+
+    @pl.when(step == 2)
+    def _():
+        for stage in gu[1 : n + 1]:
+            stage()
+        gc[1]()
+
     gap = far[...]
     for h in range(heads):
         q = joined_q[:, h * HD : (h + 1) * HD]
@@ -646,38 +923,76 @@
         probs = weights * (1.0 / jnp.sum(weights, axis=1, keepdims=True))
         out[:, h * HD : (h + 1) * HD] = dot(probs.astype(BF), v, NN).astype(BF)
 
-
-def attend(slopes, far, joined, heads):
+    @pl.when(step == steps - 1)
+    def _():
+        for stage in go[nz : 2 * nz]:
+            stage()
+        ahead, later = gc[2:-1], gu[n + 1 : -1]
+        for i, stage in enumerate(ahead):
+            stage()
+            for other in later[i * n // len(ahead) : (i + 1) * n // len(ahead)]:
+                other()
+        for stage in go[2 * nz :]:
+            stage()
+        gc[-1]()
+        gu[-1]()
+
+
+def attend(slopes, far, joined, cot, w_up, w_out, unit, heads, nz, cid):
     tree = far.shape[0]
     cols = heads * HD
-    rows = min(256, tree)
+    rows = min(256, max(128, 2**18 // tree))
+    block, width = cot.shape
+    part = w_up.shape[0]
+    n = 2 * nz
+    shapes = [(tree, cols), (n, block, width), (4 * n, part, 4 * unit), (4 * n, part, width)]
     return pl.pallas_call(
-        functools.partial(attend_kernel, heads),
-        out_shape=jax.ShapeDtypeStruct((tree, cols), BF),
+        functools.partial(attend_kernel, heads, nz, unit),
+        out_shape=[jax.ShapeDtypeStruct(s, BF) for s in shapes],
         grid=(tree // rows,),
         in_specs=[
             pl.BlockSpec(memory_space=pltpu.SMEM),
             pl.BlockSpec((rows, tree), lambda i: (i, 0)),
             pl.BlockSpec((rows, 3 * cols), lambda i: (i, 0)),
             pl.BlockSpec((tree, 3 * cols), lambda i: (0, 0)),
+            HBM,
+            HBM,
+            HBM,
         ],
-        out_specs=pl.BlockSpec((rows, cols), lambda i: (i, 0)),
-        compiler_params=pltpu.CompilerParams(vmem_limit_bytes=56 * MIB),
-        cost_estimate=pl.CostEstimate(
-            flops=4 * heads * tree * tree * HD, bytes_accessed=4 * tree * tree, transcendentals=heads * tree * tree
-        ),
+        out_specs=[pl.BlockSpec((rows, cols), lambda i: (i, 0)), HBM, HBM, HBM],
+        scratch_shapes=gather_sems(nz) + sliced_sems(nz) + full_sems(nz),
+        compiler_params=params(cid, 56 * MIB),
         name="attend",
-    )(slopes, far, joined, joined)
-
-
-def attend_back_kernel(heads, slopes, far, joined_q, joined, grad, out_q, out_k, out_v, acc_k, acc_v):
+    )(slopes, far, joined, joined, cot, w_up, w_out)
+
+
+def attend_back_kernel(heads, nz, kinds, slopes, far, joined_q, joined, grad, branch, part_sums, *refs):
+    count = len(kinds)
+    srcs, refs = refs[:count], refs[count:]
+    out_q, out_k, out_v, branch_all, update, refs = *refs[:5], refs[5:]
+    dsts, refs = refs[:count], refs[count:]
+    acc_k, acc_v, p, refs = *refs[:3], refs[3:]
+    scratch, gsems, hsems, psem = refs[:5], refs[5:7], refs[7:9], refs[9]
     cols = heads * HD
     step = pl.program_id(0)
+    pos = place()
+    gb = line_gather(branch, branch_all, *gsems, nz, False, pos)
+    hs = hand_stages(srcs, dsts, kinds, *hsems, nz, pos)
+    load = pltpu.make_async_copy(part_sums, p, psem.at[0])
 
     @pl.when(step == 0)
     def _():
         acc_k[...] = jnp.zeros_like(acc_k)
         acc_v[...] = jnp.zeros_like(acc_v)
+        greet(line_partners(nz, pos) + group_partners(pos))
+        hs[0]()
+        gb[0]()
+        gb[1]()
+        load.start()
+
+    @pl.when(step == 3)
+    def _():
+        gb[2]()
 
     gap = far[...]
     for h in range(heads):
@@ -700,17 +1015,25 @@
     def _():
         out_k[...] = acc_k[...].astype(BF)
         out_v[...] = acc_v[...].astype(BF)
-
-
-def attend_back(slopes, far_t, joined, grad, heads):
+        for stage in gb[3:]:
+            stage()
+        load.wait()
+        scatter_blocks(nz, pos, p, update, *scratch)
+        hs[1]()
+
+
+def attend_back(slopes, far_t, joined, grad, branch, part_sums, arrays, kinds, heads, nz, cid):
     tree = far_t.shape[0]
     cols = heads * HD
-    rows = min(256, tree)
+    rows = min(256, max(128, 2**18 // tree))
+    block, width = branch.shape
     full = pl.BlockSpec((tree, cols), lambda i: (0, 0))
     part = pl.BlockSpec((rows, cols), lambda i: (i, 0))
     return pl.pallas_call(
-        functools.partial(attend_back_kernel, heads),
-        out_shape=[jax.ShapeDtypeStruct((tree, cols), BF)] * 3,
+        functools.partial(attend_back_kernel, heads, nz, kinds),
+        out_shape=[jax.ShapeDtypeStruct((tree, cols), BF)] * 3
+        + [jax.ShapeDtypeStruct((2 * nz, block, width), BF), jax.ShapeDtypeStruct((block, width), F32)]
+        + hand_shapes(arrays, kinds, nz),
         grid=(tree // rows,),
         in_specs=[
             pl.BlockSpec(memory_space=pltpu.SMEM),
@@ -718,15 +1041,20 @@
             pl.BlockSpec((rows, 3 * cols), lambda i: (i, 0)),
             pl.BlockSpec((tree, 3 * cols), lambda i: (0, 0)),
             part,
-        ],
-        out_specs=[part, full, full],
-        scratch_shapes=[pltpu.VMEM((tree, cols), F32)] * 2,
-        compiler_params=pltpu.CompilerParams(vmem_limit_bytes=56 * MIB),
-        cost_estimate=pl.CostEstimate(
-            flops=10 * heads * tree * tree * HD, bytes_accessed=4 * tree * tree, transcendentals=heads * tree * tree
-        ),
+            HBM,
+            HBM,
+        ]
+        + [HBM] * len(arrays),
+        out_specs=[part, full, full, HBM, pl.BlockSpec((block, width), lambda i: (0, 0))] + [HBM] * len(arrays),
+        scratch_shapes=[pltpu.VMEM((tree, cols), F32)] * 2
+        + [pltpu.VMEM((2 * nz, block, width), BF)]
+        + scatter_scratch(nz, block, width)
+        + gather_sems(nz)
+        + hand_sems(kinds)
+        + [pltpu.SemaphoreType.DMA((1,))],
+        compiler_params=params(cid, 62 * MIB),
         name="attend_back",
-    )(slopes, far_t, joined, joined, grad)
+    )(slopes, far_t, joined, joined, grad, branch, part_sums, *arrays)
 
 
 def norm_parts(values):
@@ -810,7 +1138,7 @@
     heads = H // fsdp
     cols = heads * HD
     tree = token_valid.shape[1]
-    part = w_qkv.shape[0]
+    part = w_up.shape[0]
     unit = w_down.shape[0]
 
     vec = jnp.concatenate(
@@ -819,15 +1147,13 @@
     vec = padded(vec, 1024).reshape(-1, 128)
     tab = jnp.concatenate([token_valid[0], seg_blocks[0], parents[0]])
     tab = padded(tab, 1024).reshape(-1, 128)
-    out_w = lax.all_gather(w_out, BOTH, axis=0, tiled=True)
     aligned = part == HD and cols % 256 == 0
     if not aligned:
         w_qkv = w_qkv.reshape(part, 3, fsdp, cols).transpose(2, 0, 1, 3).reshape(fsdp, part, 3 * cols)
-    x_all, cot, qkv_w, up_w, down_w, vecs, tab = fetch(nz, layer_in, cotangent, w_qkv, w_up, w_down, vec, tab, 1)
-    x_all, cot = x_all.reshape(tree, width), cot.reshape(tree, width)
+    x_all, qkv_w, down_w, vecs, tab = fetch(nz, layer_in, w_qkv, w_down, part, vec, tab, 1)
+    down_w = down_w.reshape(4 * unit, width)
+    x_all = x_all.reshape(tree, width)
     qkv_w = qkv_w.reshape(width, 3 * cols)
-    up_w = up_w.reshape(width, 4 * unit)
-    down_w = down_w.reshape(4 * unit, width)
     vecs = vecs.reshape(devices, -1)
     (gain_one, shift_one, query_bias, value_bias, out_bias, gain_two, shift_two, down_bias) = [
         vecs[:, i * part : (i + 1) * part].reshape(-1) for i in range(8)
@@ -877,9 +1203,12 @@
     mask = allowed_mask(seg, index, valid, ancestor)
     far = jnp.where(mask, (position[None, :] - position[:, None]).astype(F32), MASKED)
     slopes = jnp.exp2(-8.0 * (numbers.astype(F32) + 1.0) / H)
-    mixed = attend(slopes, far, joined, heads)
-
-    (mixed_own,) = exchange([mixed.reshape(fsdp, rows, cols)], nz, 2, "mixed_to_tokens")
+    mixed, cot, up_w, out_w = attend(slopes, far, joined, cotangent, w_up, w_out, unit, heads, nz, 9)
+    out_w = out_w.reshape(width, width)
+    cot = cot.reshape(tree, width)
+    up_w = up_w.reshape(width, 4 * unit)
+
+    mixed_own = exchange(mixed.reshape(fsdp, rows, cols), nz, 2, "mixed_to_tokens")
     if aligned:
         mixed_own = mixed_own.reshape(nz, 2, rows, 2, 2 * HD).transpose(2, 3, 1, 0, 4).reshape(rows, width)
     else:
@@ -898,17 +1227,15 @@
         return scatter_tokens(v.astype(BF).reshape(fsdp, rows, width), nz, 4)
 
     grad_mlp_in = scatter(mm("tf,df->td", grad_hidden, up_w))
-    update = scatter(jnp.dot(active, down_w, preferred_element_type=F32)) + down_bias
-    result = middle + update
+    update = jnp.dot(active, down_w, preferred_element_type=F32).astype(BF).reshape(fsdp, rows, width)
+    down_g = mm("tf,td->fd", active, cot).astype(BF).reshape(4, unit, width)
+    up_g = mm("td,tf->df", mlp_in, grad_hidden).astype(BF).reshape(devices, part, 4 * unit)
 
     cot_own = own_rows(cot).astype(F32)
     grad_middle = cot_own + norm_back(grad_mlp_in * gain_two, normed_two, inverse_two)
     grad_branch = grad_middle.astype(BF)
     grad_mixed = mm("te,de->td", grad_branch, out_w).astype(BF)
-    if aligned:
-        branch_all = gather_tokens(grad_branch, nz, 3).reshape(tree, width)
-        out_g = mm("td,te->de", mixed, branch_all).astype(BF).reshape(4, part, width)
-    else:
+    if not aligned:
         grad_out_w = lax.psum_scatter(
             mm("td,te->de", mixed_own, grad_branch).astype(BF), BOTH, scatter_dimension=0, tiled=True
         ).astype(F32)
@@ -916,18 +1243,13 @@
         grad_mixed = grad_mixed.reshape(rows, 2, 2, nz, 2 * HD).transpose(3, 2, 0, 1, 4).reshape(fsdp, rows, cols)
     else:
         grad_mixed = grad_mixed.reshape(rows, fsdp, cols).transpose(1, 0, 2)
-    (grad_heads,) = exchange([grad_mixed], nz, 5, "grad_to_heads")
+    grad_heads = exchange(grad_mixed, nz, 5, "grad_to_heads")
     grad_heads = grad_heads.reshape(tree, cols)
-    grad_q, grad_k, grad_v = attend_back(slopes, far.T, joined, grad_heads, heads)
+    grad_q, grad_k, grad_v, branch_all, update, down_c, up_c = attend_back(
+        slopes, far.T, joined, grad_heads, grad_branch, update, [down_g, up_g], (False, True), heads, nz, 6
+    )
+    result = middle + update + down_bias
     grad_joined = jnp.concatenate([grad_q, grad_k, grad_v], axis=1)
-    grad_attn_in = scatter(mm("te,de->td", grad_joined, qkv_w))
-    grad_inputs = grad_middle + norm_back(grad_attn_in * gain_one, normed_one, inverse_one)
-
-    down_g = mm("tf,td->fd", active, cot).astype(BF).reshape(4, unit, width)
-    up_g = mm("td,tf->df", mlp_in, grad_hidden).astype(BF).reshape(devices, part, 4 * unit)
-    qkv_g = mm("td,te->de", attn_in, grad_joined).astype(BF).reshape(devices, part, 3 * cols)
-    flat = [down_g, out_g] if aligned else [down_g]
-    *flat_c, up_c, qkv_c = hand(flat + [up_g, qkv_g], (False,) * len(flat) + (True, True), nz, 6)
 
     def mine(g, came):
         g = g.reshape((2, 2, nz, 2) + g.shape[1:])
@@ -938,18 +1260,20 @@
     def mine_flat(g, came):
         return lax.dynamic_index_in_dim(g, x * 2 + y, 0, keepdims=False).astype(F32) + jnp.sum(came.astype(F32), axis=0)
 
-    grad_down_w = mine_flat(down_g, flat_c[0])
+    grad_down_w = mine_flat(down_g, down_c)
+    qkv_g = mm("td,te->de", attn_in, grad_joined).astype(BF).reshape(devices, part, 3 * cols)
+    flat = []
     if aligned:
-        grad_out_w = mine_flat(out_g, flat_c[1])
-    up_s, qkv_s = mine(up_g, up_c), mine(qkv_g, qkv_c)
-
-    up_s, qkv_s = exchange([up_s, qkv_s], nz, 7, "grads_to_owners")
-    grad_up_w = up_s.reshape(nz, 2, part, 2, 2, unit).transpose(2, 3, 1, 0, 4, 5).reshape(part, -1).astype(F32)
+        flat = [mm("td,te->de", mixed, branch_all.reshape(tree, width)).astype(BF).reshape(4, part, width)]
+    kinds = (True,) + (False,) * len(flat)
+    grad_attn_in = mm("te,de->td", grad_joined, qkv_w).astype(BF).reshape(fsdp, rows, width)
+    grad_attn_in, grad_up_w, layer_out, qkv_c, *out_c = scatter_and_hand(
+        grad_attn_in, mine(up_g, up_c), up_runs(nz, unit), result.astype(BF), [qkv_g] + flat, kinds, nz, 10
+    )
+    grad_up_w = grad_up_w.astype(F32)
     if aligned:
-        grad_qkv_w = qkv_s.reshape(nz, 2, part, 3, 2, 2 * HD).transpose(2, 3, 4, 1, 0, 5)
-    else:
-        grad_qkv_w = qkv_s.reshape(fsdp, part, 3, cols).transpose(1, 2, 0, 3)
-    grad_qkv_w = grad_qkv_w.reshape(part, -1).astype(F32)
+        grad_out_w = mine_flat(flat[0], out_c[0])
+    grad_inputs = grad_middle + norm_back(grad_attn_in * gain_one, normed_one, inverse_one)
 
     col = jnp.sum(grad_joined.astype(F32), axis=0)
 
@@ -972,7 +1296,11 @@
         axis=1,
     )
     packed = padded(packed, 1024).reshape(devices, -1, 128)
-    layer_out, grad_x, packed = finish(result.astype(BF), grad_inputs.astype(BF), packed, nz, 8)
+    runs = qkv_runs(nz, width, cols) if aligned else None
+    grad_x, packed, grad_qkv_w = finish(grad_inputs.astype(BF), packed, mine(qkv_g, qkv_c), runs, nz, 8)
+    if not aligned:
+        grad_qkv_w = grad_qkv_w.reshape(fsdp, part, 3, cols).transpose(1, 2, 0, 3).reshape(part, -1)
+    grad_qkv_w = grad_qkv_w.astype(F32)
     packed = packed.reshape(-1)
     small = [packed[i * part : (i + 1) * part] for i in range(8)]
     up_at = 8 * part

time: 886 us -> 704 us (0.79)
  Pallas kernels: 686 us -> 521 us
  local copies, waits for them, and re-layouts: 45.1 us -> 24.7 us
  matrix products: 78.3 us -> 93.1 us
  between operations: 15.3 us -> 1.66 us
    pallas_call x3 -> x1, Pallas kernels: 171 us -> 55.8 us  [scatter_tokens(): pl.pallas_call(functools.partial(scatter_kernel, nz), out_shape=jax.Shape...]
    pallas_call x2 -> x1, Pallas kernels: 85.1 us -> 45.6 us  [gather_tokens(): pl.pallas_call(functools.partial(gather_kernel, nz), out_shape=jax.ShapeD...]
    convert_element_type x6 -> x0, local copies, waits for them, and re-layouts: 19.3 us -> none  [the longest x3 12.2 us: per_device(): up_s.reshape(nz, 2, part, 2, 2, unit).transpose(2, 3, 1, 0, 4, 5)]
    pallas_call x8 -> x7, Pallas kernels: 430 us -> 420 us  [the longest x1 105 us: attend_back(): pl.pallas_call(functools.partial(attend_back_kernel, heads, nz, kinds), o...]
    dot_general x8, matrix products: 53 us -> 62.5 us  [mm(): return jnp.einsum(spec, a, b, preferred_element_type=F32)]
  transfers between devices with their start and end apart: 1 -> 0, of which waited for: 0 -> 0; matrix products, arithmetic and copies ran while one was open for 5% -> 0% of each run, Pallas kernels for 23% -> 0%
where the time goes in v3:
time: 704 us; the launch traced here: 695 us
  Pallas kernels  521 us (74%)
  matrix products  93.1 us (13%)
  other arithmetic  54.5 us (8%)
  local copies, waits for them, and re-layouts  24.7 us (4%)
    pallas_call x1, Pallas kernels, attend_back(): pl.pallas_call(functools.partial(attend_back_kernel, heads, nz, kinds), o...  105 us
    pallas_call x1, Pallas kernels, attend(): pl.pallas_call(functools.partial(attend_kernel, heads, nz, unit), out_sha...  102 us
    pallas_call x1, Pallas kernels, fetch(): pl.pallas_call(functools.partial(fetch_kernel, nz, width, cols), out_shap...  88.7 us
    pallas_call x1, Pallas kernels, scatter_and_hand(): pl.pallas_call(functools.partial(scatter_and_hand_kernel, nz, kinds, runs...  72.7 us
    dot_general x8, matrix products, mm(): return jnp.einsum(spec, a, b, preferred_element_type=F32)  62.5 us
    pallas_call x1, Pallas kernels, scatter_tokens(): pl.pallas_call(functools.partial(scatter_kernel, nz), out_shape=jax.Shape...  55.8 us
    pallas_call x1, Pallas kernels, gather_tokens(): pl.pallas_call(functools.partial(gather_kernel, nz), out_shape=jax.ShapeD...  45.6 us
    pallas_call x1, Pallas kernels, finish(): pl.pallas_call(functools.partial(finish_kernel, nz, runs), out_shape=[jax...  27.4 us

profile of v3, /device:TPU:0, one launch (start us, length us, event | category | flops | bytes accessed | tf_op | source)
XLA Modules:
  0.0 695.3 jit_solution(1886383088212934225)
XLA Ops:
  1.4 6.1 concatenate.15
  9.4 88.7 %fetch.1 = (bf16[8,128,2048]{2,1,0:T(8,128)(2,1)}, bf16[32,64,768]{2,1,0:T(8,128)(2,1)}, bf16[4,256,2048]{2,1,0:T(8,128)(2,1)}, f32[32,8,128]{2,1,0:T(8,128)}, s32[16,128]{1,0:T(8,128)}) custom-call(bf16[128,2048]{1,0:T(8,128)(2,1)} %x_in.1, bf16[64,6144]{1,0:T(8,128)(2,1)} %w_qkv.1, bf16[256,2048]{1,0:T(8,128)(2,1)} %w_down.1, ...), custom_call_target="tpu_custom_call" | custom-call | tf_op jit(solution)/shard_map/fetch/pallas_call | solution.py:666
  100.8 2.0 copy.58
  103.2 3.7 reduce-window.6
  107.8 6.3 convert_select_fusion
  114.3 3.0 convert_reduce_fusion
  117.8 1.2 fusion.2
  119.0 3.1 fusion.5
  122.3 7.7 %add_convert_fusion.5.joined_q.joined = bf16[1024,768]{1,0:T(8,128)(2,1)} fusion(bf16[1024,2048]{1,0:T(8,128)(2,1)} %bitcast.136, bf16[2048,768]{1,0:T(8,128)(2,1)} %bitcast.173, f32[768]{0:T(1024)S(1)} %pad_maximum_fusion), kind=kOutput, calls=%fused_computation.56 | convolution fusion | flops 3222798336 | bytes 8915968 | tf_op jit(solution)/shard_map/dot_general | solution.py:1194
  130.1 1.2 convert_reduce_fusion.7
  131.3 102.4 %attend.1 = (bf16[1024,256]{1,0:T(8,128)(2,1)}, bf16[8,128,2048]{2,1,0:T(8,128)(2,1)}, bf16[32,64,1024]{2,1,0:T(8,128)(2,1)}, bf16[32,64,2048]{2,1,0:T(8,128)(2,1)}) custom-call(f32[4]{0:T(128)} %reshape.413.slopes, f32[1024,1024]{1,0:T(8,128)} %get-tuple-element.95.far, bf16[1024,768]{1,0:T(8,128)(2,1)} %add_convert_fusion.5.joined_q.joined, ...), custom_call_target="tpu_custom_call" | custom-call | tf_op jit(solution)/shard_map/attend/pallas_call | solution.py:949
  233.7 12.1 %mixed_to_tokens.1 = bf16[8,128,256]{2,1,0:T(8,128)(2,1)} custom-call(bf16[8,128,256]{2,1,0:T(8,128)(2,1)} %bitcast.149), custom_call_target="tpu_custom_call" | custom-call | tf_op jit(solution)/shard_map/mixed_to_tokens/pallas_call | solution.py:790
  245.8 1.2 reshape.381
  247.4 5.6 fusion.57
  254.5 45.6 %gather_tokens.1 = bf16[8,128,2048]{2,1,0:T(8,128)(2,1)} custom-call(bf16[128,2048]{1,0:T(8,128)(2,1)} %add_convert_fusion.6.src), custom_call_target="tpu_custom_call" | custom-call | tf_op jit(solution)/shard_map/gather_tokens/pallas_call | solution.py:180
  300.1 10.1 %fusion.61 = f32[1024,1024]{0,1:T(8,128)} fusion(bf16[1024,2048]{1,0:T(8,128)(2,1)} %bitcast.138, bf16[2048,1024]{1,0:T(8,128)(2,1)} %bitcast.171), kind=kOutput, calls=%fused_computation.160 | convolution fusion | flops 4294967296 | bytes 12582912 | tf_op jit(solution)/shard_map/dot_general | solution.py:1220
  310.2 18.8 %convert_reduce_fusion.4 = (f32[1024]{0:T(1024)S(1)}, bf16[1024,1024]{0,1:T(8,128)(2,1)S(1)}, f32[1024,1024]{0,1:T(8,128)}) fusion(f32[1024,1024]{0,1:T(8,128)} %fusion.61, f32[1024]{0:T(1024)S(1)} %bitcast.162, bf16[1024,2048]{1,0:T(8,128)(2,1)} %bitcast.155, bf16[1024,2048]{1,0:T(8,128)(2,1)} %bitcast.168), kind=kOutput, calls=%fused_computation.15 | convolution fusion | flops 4373609472 | bytes 18882560 | tf_op jit(solution)/shard_map/td,fd->tf/dot_general | solution.py:1105
  329.0 6.2 convolution_convert_fusion.4
  335.2 55.8 %scatter_tokens.1 = f32[128,2048]{1,0:T(8,128)} custom-call(bf16[8,128,2048]{2,1,0:T(8,128)(2,1)} %bitcast.137), custom_call_target="tpu_custom_call" | custom-call | tf_op jit(solution)/shard_map/scatter_tokens/pallas_call | solution.py:260
  390.9 1.7 multiply_reduce_fusion.2
  392.6 3.0 convert_reduce_fusion.9
  395.6 6.4 convolution_convert_fusion.6
  402.8 1.1 reshape.390.src
  404.0 11.9 %grad_to_heads.1 = bf16[8,128,256]{2,1,0:T(8,128)(2,1)} custom-call(bf16[8,128,256]{2,1,0:T(8,128)(2,1)} %reshape.390.src), custom_call_target="tpu_custom_call" | custom-call | tf_op jit(solution)/shard_map/grad_to_heads/pallas_call | solution.py:790
  415.9 4.1 multiply_convert_fusion
  420.5 6.2 convolution_convert_fusion.3
  426.8 6.1 convolution_convert_fusion.2
  432.9 6.4 convolution_convert_fusion.1
  439.3 104.8 %attend_back.1 = (bf16[1024,256]{1,0:T(8,128)(2,1)}, bf16[1024,256]{1,0:T(8,128)(2,1)}, bf16[1024,256]{1,0:T(8,128)(2,1)}, bf16[8,128,2048]{2,1,0:T(8,128)(2,1)}...) custom-call(f32[4]{0:T(128)} %reshape.413.slopes, ...), custom_call_target="tpu_custom_call" | custom-call | tf_op jit(solution)/shard_map/attend_back/pallas_call | solution.py:1032
  546.3 1.1 constant_dynamic-update-slice_fusion
  547.4 7.7 %convolution_convert_fusion = bf16[1024,2048]{1,0:T(8,128)(2,1)} fusion(bf16[1024,768]{1,0:T(8,128)(2,1)S(1)} %constant_dynamic-update-slice_fusion, bf16[2048,768]{1,0:T(8,128)(2,1)} %bitcast.174), kind=kOutput, calls=%fused_computation.49 | convolution fusion | flops 3223322624 | bytes 8912896 | tf_op jit(solution)/shard_map/te,de->td/dot_general | solution.py:1105
  555.1 2.0 convert_reduce_fusion.2
  557.1 1.6 fusion.42
  559.0 1.4 fusion.26.up_s
  560.5 1.6 multiply_reduce_fusion.1
  562.1 8.7 %fusion.25 = bf16[2048,768]{1,0:T(8,128)(2,1)} fusion(bf16[1024,768]{1,0:T(8,128)(2,1)} %copy-done.7, bf16[1024,2048]{1,0:T(8,128)(2,1)} %bitcast.127, f32[2048]{0:T(1024)S(1)} %add.236, f32[2048]{0:T(1024)S(1)} %mul.243, f32[1024]{0:T(1024)S(1)} %get-tuple-element.111, f32[1024]{0:T(1024)S(1)} %get-tuple-element.109), kind=kOutput, calls=%fused_computation.54 | convolution fusion | flops 3235381248 | bytes 8937472 | tf_op jit(solution)/shard_map/td,te->de/dot_general | solution.py:1105
  570.8 2.2 convolution_convert_fusion.5
  573.1 72.7 %scatter_and_hand.1 = (f32[128,2048]{1,0:T(8,128)}, bf16[64,8192]{1,0:T(8,128)(2,1)}, bf16[128,2048]{1,0:T(8,128)(2,1)}, bf16[3,8,64,768]{3,2,1,0:T(8,128)(2,1)}, bf16[3,64,2048]{2,1,0:T(8,128)(2,1)}) custom-call(bf16[8,128,2048]{2,1,0:T(8,128)(2,1)} %bitcast.140, bf16[8,64,1024]{2,1,0:T(8,128)(2,1)} %fusion.26.up_s, ...), custom_call_target="tpu_custom_call" | custom-call | tf_op jit(solution)/shard_map/scatter_and_hand/pallas_call | solution.py:295
  645.8 1.9 fusion.40
  647.8 1.8 fusion.39.grad
  650.6 1.4 pad_maximum_fusion.1
  652.1 2.2 convert_reduce_fusion.3
  654.3 1.3 fusion.43
  655.9 27.4 %finish.1 = (bf16[128,2048]{1,0:T(8,128)(2,1)S(1)}, f32[8,128]{1,0:T(8,128)S(1)}, bf16[64,6144]{1,0:T(8,128)(2,1)S(1)}) custom-call(bf16[128,2048]{1,0:T(8,128)(2,1)S(1)} %fusion.39.grad, f32[32,8,128]{2,1,0:T(8,128)S(1)} %bitcast.120, bf16[8,64,768]{2,1,0:T(8,128)(2,1)S(1)} %fusion.27.qkv_s), custom_call_target="tpu_custom_call" | custom-call | tf_op jit(solution)/shard_map/finish/pallas_call | solution.py:859
  683.3 1.2 convert_element_type.196
  684.7 1.9 convert_add_fusion.3
  686.6 1.5 convert_element_type.200
  688.7 2.8 convert_add_fusion
  (139 shorter events, 18.9 us)
Async XLA Ops:
  99.8 2.9 copy-start.16
  107.8 6.3 copy-start.14
  114.3 3.5 copy-start
  310.2 18.8 %copy-start.19 = (bf16[32,64,1024]{2,1,0:T(8,128)(2,1)S(1)}, bf16[32,64,1024]{2,1,0:T(8,128)(2,1)}, u32[]{:S(2)}) copy-start(bf16[32,64,1024]{2,1,0:T(8,128)(2,1)} %get-tuple-element.47) | copy-start | bytes 12582916
  329.0 6.2 copy-start.20
  395.6 6.5 copy-start.2
  415.9 4.6 copy-start.17
  420.5 6.2 copy-start.15
  426.8 6.1 copy-start.3
  426.8 6.1 copy-start.21
  547.3 7.8 %copy-start.7 = (bf16[1024,768]{1,0:T(8,128)(2,1)}, bf16[1024,768]{1,0:T(8,128)(2,1)S(1)}, u32[]{:S(2)}) copy-start(bf16[1024,768]{1,0:T(8,128)(2,1)S(1)} %constant_dynamic-update-slice_fusion) | copy-start | bytes 4718596
  547.4 7.8 %copy-start.6 = (bf16[3,8,64,1024]{3,2,1,0:T(8,128)(2,1)S(1)}, bf16[3,8,64,1024]{3,2,1,0:T(8,128)(2,1)}, u32[]{:S(2)}) copy-start(bf16[3,8,64,1024]{3,2,1,0:T(8,128)(2,1)} %get-tuple-element.52) | copy-start | bytes 9437188
  557.1 1.9 copy-start.1
  557.1 3.4 copy-start.10
  562.1 8.7 %copy-start.12 = (bf16[1024,256]{1,0:T(8,128)(2,1)S(1)}, bf16[1024,256]{1,0:T(8,128)(2,1)}, u32[]{:S(2)}) copy-start(bf16[1024,256]{1,0:T(8,128)(2,1)} %get-tuple-element.45) | copy-start | bytes 1572868
  562.1 8.7 %copy-start.18 = (bf16[8,128,2048]{2,1,0:T(8,128)(2,1)S(1)}, bf16[8,128,2048]{2,1,0:T(8,128)(2,1)}, u32[]{:S(2)}) copy-start(bf16[8,128,2048]{2,1,0:T(8,128)(2,1)} %get-tuple-element.54) | copy-start | bytes 12582916
  573.1 74.7 %copy-start.4 = (f32[128,2048]{1,0:T(8,128)S(1)}, f32[128,2048]{1,0:T(8,128)}, u32[]{:S(2)}) copy-start(f32[128,2048]{1,0:T(8,128)} %get-tuple-element.79) | copy-start | bytes 3145732
  645.8 4.0 copy-start.8
  655.6 28.9 %copy-start.11 = (bf16[3,64,2048]{2,1,0:T(8,128)(2,1)S(1)}, bf16[3,64,2048]{2,1,0:T(8,128)(2,1)}, u32[]{:S(2)}) copy-start(bf16[3,64,2048]{2,1,0:T(8,128)(2,1)} %get-tuple-element.60) | copy-start | bytes 2359300
  655.9 30.8 %copy-start.9 = (bf16[64,8192]{1,0:T(8,128)(2,1)S(1)}, bf16[64,8192]{1,0:T(8,128)(2,1)}, u32[]{:S(2)}) copy-start(bf16[64,8192]{1,0:T(8,128)(2,1)} %get-tuple-element.61) | copy-start | bytes 3145732
  684.7 3.4 copy-start.5
  688.1 5.1 copy-start.13

commit v4 on v3

--- a/solution.py
+++ b/solution.py
@@ -1,4 +1,5 @@
 import functools
+import math
 
 import jax
 import jax.numpy as jnp
@@ -881,6 +882,260 @@
 NN = ((1,), (0,))
 NT = ((1,), (1,))
 TN = ((0,), (0,))
+
+
+def gelu_and_slope(value):
+    normal = 0.5 + 0.5 * lax.erf(value * math.sqrt(0.5))
+    density = jnp.exp(-0.5 * value * value) * (1.0 / math.sqrt(2.0 * math.pi))
+    return value * normal, normal + value * density
+
+
+def mlp_kernel(
+    nz, own, cot_in, up_in, down_in, bias, out, upd_out, up_out, down_out, bias_g,
+    mlp, cot, up_w, down_w, p, upd, up_g, down_g, active, gh, acc, ups, dns, gsend, grecv, ssend, srecv, lsem,
+):
+    pos = place()
+    x, c, z, y = pos
+    blocks, rows, width = mlp.shape
+    units = active.shape[1]
+    pair = 2 * rows
+    me = z * 2 + c
+    sib = at(x, 1 - c, z, y)
+    up_dev, dn_dev = at(x, c, z + 1, y), at(x, c, z - 1, y)
+    UP, DN, SU, SD = 0, nz, 2 * nz, 3 * nz
+    S, U, D = 0, nz, 2 * nz
+
+    def f(v):
+        return v.astype(F32)
+
+    loads = [
+        pltpu.make_async_copy(a, b, lsem.at[i])
+        for i, (a, b) in enumerate([(cot_in, cot), (down_in, down_w), (up_in, up_w)])
+    ]
+    stores = [
+        pltpu.make_async_copy(a, b, lsem.at[3 + i])
+        for i, (a, b) in enumerate([(upd, upd_out), (up_g, up_out), (down_g, down_out)])
+    ]
+
+    def block(b, sem, target):
+        return remote(mlp.at[b], mlp.at[b], gsend.at[sem], grecv.at[sem], target)
+
+    def up(d):
+        return block((z - d) * 2 + c, UP + d, up_dev)
+
+    def dn(d):
+        return block((z + d) * 2 + c, DN + d, dn_dev)
+
+    def side(d, below):
+        return block(jnp.where(below, z - d, z + d) * 2 + c, jnp.where(below, SU, SD) + d, sib)
+
+    def turn(i):
+        both = jnp.minimum(z, nz - 1 - z)
+        two = i <= 2 * both
+        d = jnp.where(two, (i + 1) // 2, i - both)
+        below = jnp.where(two, i % 2 == 1, z > nz - 1 - z)
+        return d, below
+
+    def arrive(i):
+        if i == 0:
+            block(z * 2 + 1 - c, SU, sib).wait_recv()
+            return z
+        d, below = turn(i)
+        zi = jnp.where(below, z - d, z + d)
+        block(zi * 2 + c, jnp.where(below, UP, DN) + d - 1, sib).wait_recv()
+        pl.when(below & (z < nz - 1))(lambda: up(d).start())
+        pl.when(jnp.logical_not(below) & (z > 0))(lambda: dn(d).start())
+        side(d, below).start()
+        block(zi * 2 + 1 - c, jnp.where(below, SU, SD) + d, sib).wait_recv()
+        return zi
+
+    def swap(t):
+        return remote(p.at[t * 2 + 1 - c], acc.at[t], ssend.at[S + t], srecv.at[S + t], sib)
+
+    def rise(t):
+        return remote(acc.at[t], ups.at[t], ssend.at[U + t], srecv.at[U + t], up_dev)
+
+    def fall(t):
+        return remote(acc.at[t], dns.at[t], ssend.at[D + t], srecv.at[D + t], dn_dev)
+
+    def event(t, upward):
+        swap(t).wait_recv()
+        acc[t] = (f(acc[t]) + f(p[t * 2 + c])).astype(BF)
+        move, came = (rise, ups) if upward else (fall, dns)
+
+        @pl.when(z > 0 if upward else z < nz - 1)
+        def _():
+            move(t).wait_recv()
+            acc[t] = (f(acc[t]) + f(came[t])).astype(BF)
+
+        move(t).start()
+
+    def events(s):
+        for t in range(nz):
+            zz = s - t
+            if 0 <= zz < t:
+                pl.when(z == zz)(functools.partial(event, t, True))
+            zz = 2 * (nz - 1) - s - t
+            if t < zz < nz:
+                pl.when(z == zz)(functools.partial(event, t, False))
+
+    def at_rows(ref, zi):
+        return ref[pl.ds(zi * 2, 2)].reshape(pair, width)
+
+    def hidden_part(zi, early):
+        here = pl.ds(pl.multiple_of(zi * pair, pair), pair)
+
+        def tile(j, _):
+            u = pl.ds(pl.multiple_of(j * 256, 256), 256)
+            value = dot(at_rows(mlp, zi), up_w[:, u], NN) + bias[:, u]
+            grad = dot(at_rows(cot, zi), down_w[u, :], NT)
+            act, slope = gelu_and_slope(value)
+            low = (grad * slope).astype(BF)
+            active[here, u] = act.astype(BF)
+            gh[here, u] = low
+            bias_g[:, u] += jnp.sum(f(low), axis=0, keepdims=True)
+            return 0
+
+        lax.fori_loop(0, units // 256, tile, 0)
+
+        def back(j, _):
+            w = pl.ds(pl.multiple_of(j * 512, 512), 512)
+            p[pl.ds(zi * 2, 2), :, w] = dot(gh[here, :], up_w[w, :], NT).astype(BF).reshape(2, rows, 512)
+            return 0
+
+        lax.fori_loop(0, width // 512, back, 0)
+
+    def forward_part(zi):
+        here = pl.ds(pl.multiple_of(zi * pair, pair), pair)
+
+        def tile(j, _):
+            w = pl.ds(pl.multiple_of(j * 512, 512), 512)
+            upd[pl.ds(zi * 2, 2), :, w] = dot(active[here, :], down_w[:, w], NN).astype(BF).reshape(2, rows, 512)
+            return 0
+
+        lax.fori_loop(0, width // 512, tile, 0)
+
+    def up_grads(first, count):
+        def tile(j, _):
+            w = pl.ds(pl.multiple_of(j * 256, 256), 256)
+            up_g[w, :] = dot(mlp[:, :, w].reshape(blocks * rows, 256), gh[...], TN).astype(BF)
+            return 0
+
+        lax.fori_loop(first, first + count, tile, 0)
+
+    def down_grads():
+        def tile(j, _):
+            u = pl.ds(pl.multiple_of(j * 256, 256), 256)
+            down_g[u, :] = dot(active[:, u], cot[...].reshape(blocks * rows, width), TN).astype(BF)
+            return 0
+
+        lax.fori_loop(0, units // 256, tile, 0)
+
+    mlp[me] = own[...]
+    greet(line_partners(nz, pos))
+    pl.when(z < nz - 1)(up(0).start)
+    pl.when(z > 0)(dn(0).start)
+    side(0, z >= 0).start()
+    for copy in loads:
+        copy.start()
+    bias_g[...] = jnp.zeros_like(bias_g)
+    for copy in loads:
+        copy.wait()
+    slots = 2 * nz - 1
+    tiles = width // 256
+    for s in range(slots):
+        if s < nz:
+            zi = arrive(s)
+            hidden_part(zi, s)
+            swap(zi).start()
+        events(s)
+        if s < nz:
+            forward_part(zi)
+        if s == nz - 1:
+            stores[0].start()
+            down_grads()
+            stores[2].start()
+        elif s == nz:
+            up_grads(0, tiles // 2)
+        elif s == nz + 1:
+            up_grads(tiles // 2, tiles - tiles // 2)
+            stores[1].start()
+    swap(z).wait_recv()
+    out[...] = f(acc[z]) + f(p[z * 2 + c])
+
+    @pl.when(z > 0)
+    def _():
+        rise(z).wait_recv()
+        out[...] += f(ups[z])
+
+    @pl.when(z < nz - 1)
+    def _():
+        fall(z).wait_recv()
+        out[...] += f(dns[z])
+
+    for copy in stores:
+        copy.wait()
+    side(0, z >= 0).wait_send()
+    pl.when(z < nz - 1)(up(0).wait_send)
+    pl.when(z > 0)(dn(0).wait_send)
+    for k in range(1, nz):
+
+        @pl.when(z >= k)
+        def _():
+            pl.when(z < nz - 1)(up(k).wait_send)
+            side(k, z >= 0).wait_send()
+
+        @pl.when(z + k < nz)
+        def _():
+            pl.when(z > 0)(dn(k).wait_send)
+            side(k, z < 0).wait_send()
+
+    for t in range(nz):
+        swap(t).wait_send()
+        pl.when(z < t)(rise(t).wait_send)
+        pl.when(z > t)(fall(t).wait_send)
+
+
+def mlp_bytes(nz, rows, width, units):
+    tree = 2 * nz * rows
+    return 2 * (4 * tree * width + 4 * units * width + 2 * tree * units + 3 * nz * rows * width) + 8 * rows * width
+
+
+def mlp_call(own, cot, up_w, down_w, bias, nz, cid):
+    rows, width = own.shape
+    units = down_w.shape[0]
+    n = 2 * nz
+    shape = jax.ShapeDtypeStruct
+    return pl.pallas_call(
+        functools.partial(mlp_kernel, nz),
+        out_shape=[
+            shape((rows, width), F32),
+            shape((n, rows, width), BF),
+            shape((width, units), BF),
+            shape((units, width), BF),
+            shape((1, units), F32),
+        ],
+        in_specs=[VM, HBM, HBM, HBM, VM],
+        out_specs=[VM, HBM, HBM, HBM, VM],
+        scratch_shapes=[
+            pltpu.VMEM((n, rows, width), BF),
+            pltpu.VMEM((n, rows, width), BF),
+            pltpu.VMEM((width, units), BF),
+            pltpu.VMEM((units, width), BF),
+            pltpu.VMEM((n, rows, width), BF),
+            pltpu.VMEM((n, rows, width), BF),
+            pltpu.VMEM((width, units), BF),
+            pltpu.VMEM((units, width), BF),
+            pltpu.VMEM((n * rows, units), BF),
+            pltpu.VMEM((n * rows, units), BF),
+        ]
+        + [pltpu.VMEM((nz, rows, width), BF)] * 3
+        + gather_sems(nz)
+        + [pltpu.SemaphoreType.DMA((3 * nz,))] * 2
+        + [pltpu.SemaphoreType.DMA((6,))],
+        compiler_params=params(cid, 62 * MIB),
+        name="mlp",
+    )(own, cot, up_w, down_w, bias)
 
 
 def attend_kernel(
@@ -1216,20 +1471,28 @@
     branch = jnp.dot(mixed_own, out_w, preferred_element_type=F32) + out_bias
     middle = inputs + branch
     normed_two, inverse_two = norm_parts(middle)
-    mlp_in = gather_tokens((normed_two * gain_two + shift_two).astype(BF), nz, 3).reshape(tree, width)
-    hidden = jnp.dot(mlp_in, up_w, preferred_element_type=F32) + up_bias
-    active_float, gelu_pull = jax.vjp(gelu_exact, hidden)
-    active = active_float.astype(BF)
-    grad_active = mm("td,fd->tf", cot, down_w)
-    grad_hidden = gelu_pull(grad_active)[0].astype(BF)
-
-    def scatter(v):
-        return scatter_tokens(v.astype(BF).reshape(fsdp, rows, width), nz, 4)
-
-    grad_mlp_in = scatter(mm("tf,df->td", grad_hidden, up_w))
-    update = jnp.dot(active, down_w, preferred_element_type=F32).astype(BF).reshape(fsdp, rows, width)
-    down_g = mm("tf,td->fd", active, cot).astype(BF).reshape(4, unit, width)
-    up_g = mm("td,tf->df", mlp_in, grad_hidden).astype(BF).reshape(devices, part, 4 * unit)
+    mlp_own = (normed_two * gain_two + shift_two).astype(BF)
+    cot_blocks = cot.reshape(fsdp, rows, width)
+    if mlp_bytes(nz, rows, width, 4 * unit) < 50 * MIB:
+        grad_mlp_in, update, up_g, down_g, grad_bias_up = mlp_call(
+            mlp_own, cot_blocks, up_w, down_w, up_bias[None], nz, 3
+        )
+        grad_bias_up = grad_bias_up[0]
+    else:
+        mlp_in = gather_tokens(mlp_own, nz, 3).reshape(tree, width)
+        hidden = jnp.dot(mlp_in, up_w, preferred_element_type=F32) + up_bias
+        active_float, gelu_pull = jax.vjp(gelu_exact, hidden)
+        active = active_float.astype(BF)
+        grad_active = mm("td,fd->tf", cot, down_w)
+        grad_hidden = gelu_pull(grad_active)[0].astype(BF)
+        grad_mlp_in = mm("tf,df->td", grad_hidden, up_w).astype(BF).reshape(fsdp, rows, width)
+        grad_mlp_in = scatter_tokens(grad_mlp_in, nz, 4)
+        update = jnp.dot(active, down_w, preferred_element_type=F32).astype(BF).reshape(fsdp, rows, width)
+        down_g = mm("tf,td->fd", active, cot).astype(BF)
+        up_g = mm("td,tf->df", mlp_in, grad_hidden).astype(BF)
+        grad_bias_up = jnp.sum(grad_hidden.astype(F32), axis=0)
+    down_g = down_g.reshape(4, unit, width)
+    up_g = up_g.reshape(devices, part, 4 * unit)
 
     cot_own = own_rows(cot).astype(F32)
     grad_middle = cot_own + norm_back(grad_mlp_in * gain_two, normed_two, inverse_two)
@@ -1287,7 +1550,7 @@
         jnp.sum(grad_mlp_in, axis=0),
         jnp.sum(cot_own, axis=0),
     ]
-    grad_bias_up = jnp.sum(grad_hidden.astype(F32), axis=0).reshape(2, 1, 1, 2, unit)
+    grad_bias_up = grad_bias_up.reshape(2, 1, 1, 2, unit)
     grad_bias_up = lax.dynamic_update_slice(jnp.zeros((2, 2, nz, 2, unit), F32), grad_bias_up, (0, c, z, 0, 0))
     squares = jnp.stack([jnp.sum(result * result), jnp.sum(branch * branch)])
     packed = jnp.concatenate(

time: 704 us -> 645 us (0.916)
  matrix products: 93.1 us -> 39.3 us
    dot_general x8 -> x4, matrix products: 62.5 us -> 25 us  [mm(): return jnp.einsum(spec, a, b, preferred_element_type=F32)]
    dot_general x2 -> x0, matrix products: 16.3 us -> none  [the longest x1 10.1 us: per_device(): hidden = jnp.dot(mlp_in, up_w, preferred_element_type=F32) + up_bias]
    pallas_call x2 -> x1, Pallas kernels: 101 us -> 93.5 us  [mlp_call(): pl.pallas_call(functools.partial(mlp_kernel, nz), out_shape=[shape((rows,...]
where the time goes in v4:
time: 645 us; the launch traced here: 636 us
  Pallas kernels  519 us (80%)
  other arithmetic  51.2 us (8%)
  matrix products  39.3 us (6%)
  local copies, waits for them, and re-layouts  25.4 us (4%)
    pallas_call x1, Pallas kernels, attend_back(): pl.pallas_call(functools.partial(attend_back_kernel, heads, nz, kinds), o...  105 us
    pallas_call x1, Pallas kernels, attend(): pl.pallas_call(functools.partial(attend_kernel, heads, nz, unit), out_sha...  102 us
    pallas_call x1, Pallas kernels, mlp_call(): pl.pallas_call(functools.partial(mlp_kernel, nz), out_shape=[shape((rows,...  93.5 us
    pallas_call x1, Pallas kernels, fetch(): pl.pallas_call(functools.partial(fetch_kernel, nz, width, cols), out_shap...  88.7 us
    pallas_call x1, Pallas kernels, scatter_and_hand(): pl.pallas_call(functools.partial(scatter_and_hand_kernel, nz, kinds, runs...  72.7 us
    pallas_call x2, Pallas kernels, exchange(): pl.pallas_call(functools.partial(exchange_kernel, nz), out_shape=jax.Shap...  29.4 us
    pallas_call x1, Pallas kernels, finish(): pl.pallas_call(functools.partial(finish_kernel, nz, runs), out_shape=[jax...  27.4 us
    dot_general x4, matrix products, mm(): return jnp.einsum(spec, a, b, preferred_element_type=F32)  25 us

profile of v4, /device:TPU:0, one launch (start us, length us, event | category | flops | bytes accessed | tf_op | source)
XLA Modules:
  0.0 636.3 jit_solution(9462818985947627150)
XLA Ops:
  1.4 6.1 concatenate.15
  8.0 0.8 concatenate.16
  9.4 88.7 %fetch.1 = (bf16[8,128,2048]{2,1,0:T(8,128)(2,1)}, bf16[32,64,768]{2,1,0:T(8,128)(2,1)}, bf16[4,256,2048]{2,1,0:T(8,128)(2,1)}, f32[32,8,128]{2,1,0:T(8,128)}, s32[16,128]{1,0:T(8,128)}) custom-call(bf16[128,2048]{1,0:T(8,128)(2,1)} %x_in.1, bf16[64,6144]{1,0:T(8,128)(2,1)} %w_qkv.1, bf16[256,2048]{1,0:T(8,128)(2,1)} %w_down.1, ...), custom_call_target="tpu_custom_call" | custom-call | tf_op jit(solution)/shard_map/fetch/pallas_call | solution.py:667
  98.9 0.8 slice.133
  99.8 1.0 broadcast_compare_fusion
  100.8 2.0 copy.54
  103.2 3.7 reduce-window.6
  107.8 6.4 %convert_select_fusion = (f32[1024,1024]{1,0:T(8,128)}, f32[1024,1024]{1,0:T(8,128)}) fusion(pred[1024,1024]{1,0:T(8,128)(4,1)S(1)} %copy.54, s32[1024]{0:T(1024)S(1)} %add.223, s32[1024]{0:T(1024)S(1)} %eq.111, pred[1024]{0:T(1024)(128)(4,1)S(1)} %broadcast_compare_fusion.1, pred[1024,1024]{0,1:T(8,128)(4,1)S(1)} %broadcast_compare_fusion), kind=kLoop, calls=%fused_computation.17 | loop fusion | flops 20971520 | bytes 10494976 | tf_op jit(solution)/shard_map/jit(_where)/select_n | solution.py:1459
  114.5 3.0 convert_reduce_fusion
  117.9 1.2 fusion.2
  119.2 3.1 fusion.5
  122.5 7.7 %add_convert_fusion.4.joined_q.joined = bf16[1024,768]{1,0:T(8,128)(2,1)} fusion(bf16[1024,2048]{1,0:T(8,128)(2,1)} %bitcast.121, bf16[2048,768]{1,0:T(8,128)(2,1)} %bitcast.147, f32[768]{0:T(1024)S(1)} %pad_maximum_fusion), kind=kOutput, calls=%fused_computation.34 | convolution fusion | flops 3222798336 | bytes 8915968 | tf_op jit(solution)/shard_map/dot_general | solution.py:1449
  130.2 1.2 convert_reduce_fusion.6
  131.5 102.2 %attend.1 = (bf16[1024,256]{1,0:T(8,128)(2,1)}, bf16[8,128,2048]{2,1,0:T(8,128)(2,1)}, bf16[32,64,1024]{2,1,0:T(8,128)(2,1)}, bf16[32,64,2048]{2,1,0:T(8,128)(2,1)}) custom-call(f32[4]{0:T(128)} %reshape.396.slopes, f32[1024,1024]{1,0:T(8,128)} %get-tuple-element.102.far, bf16[1024,768]{1,0:T(8,128)(2,1)} %add_convert_fusion.4.joined_q.joined, ...), custom_call_target="tpu_custom_call" | custom-call | tf_op jit(solution)/shard_map/attend/pallas_call | solution.py:1204
  233.7 12.1 %mixed_to_tokens.1 = bf16[8,128,256]{2,1,0:T(8,128)(2,1)} custom-call(bf16[8,128,256]{2,1,0:T(8,128)(2,1)} %bitcast.132), custom_call_target="tpu_custom_call" | custom-call | tf_op jit(solution)/shard_map/mixed_to_tokens/pallas_call | solution.py:791
  245.8 1.2 reshape.368
  247.4 5.6 fusion.50
  253.5 1.1 add_convert_fusion.5.own
  255.2 93.5 %mlp.1 = (f32[128,2048]{1,0:T(8,128)}, bf16[8,128,2048]{2,1,0:T(8,128)(2,1)}, bf16[2048,1024]{1,0:T(8,128)(2,1)}, bf16[1024,2048]{1,0:T(8,128)(2,1)}, f32[1,1024]{1,0:T(1,128)}) custom-call(bf16[128,2048]{1,0:T(8,128)(2,1)} %add_convert_fusion.5.own, bf16[8,128,2048]{2,1,0:T(8,128)(2,1)} %get-tuple-element.49.cot_in, bf16[2048,1024]{1,0:T(8,128)(2,1)} %bitcast.124, ...), custom_call_target="tpu_custom_call" | custom-call | tf_op jit(solution)/shard_map/mlp/pallas_call | solution.py:1109
  348.7 1.7 multiply_reduce_fusion.2
  350.3 3.0 convert_reduce_fusion.8
  353.3 6.4 %convolution_convert_fusion.2 = bf16[128,2048]{1,0:T(8,128)(2,1)S(1)} fusion(bf16[128,2048]{1,0:T(8,128)(2,1)S(1)} %get-tuple-element.85.branch, bf16[2048,2048]{1,0:T(8,128)(2,1)} %bitcast.108), kind=kOutput, calls=%fused_computation.37 | convolution fusion | flops 1074003968 | bytes 9437184 | tf_op jit(solution)/shard_map/te,de->td/dot_general | solution.py:1360
  360.6 1.1 reshape.375.src
  361.7 17.3 %grad_to_heads.1 = bf16[8,128,256]{2,1,0:T(8,128)(2,1)} custom-call(bf16[8,128,256]{2,1,0:T(8,128)(2,1)} %reshape.375.src), custom_call_target="tpu_custom_call" | custom-call | tf_op jit(solution)/shard_map/grad_to_heads/pallas_call | solution.py:791
  379.0 105.3 %attend_back.1 = (bf16[1024,256]{1,0:T(8,128)(2,1)}, bf16[1024,256]{1,0:T(8,128)(2,1)}, bf16[1024,256]{1,0:T(8,128)(2,1)}, bf16[8,128,2048]{2,1,0:T(8,128)(2,1)}...) custom-call(f32[4]{0:T(128)} %reshape.396.slopes, ...), custom_call_target="tpu_custom_call" | custom-call | tf_op jit(solution)/shard_map/attend_back/pallas_call | solution.py:1287
  484.3 1.1 constant_dynamic-update-slice_fusion.2
  485.4 1.1 constant_dynamic-update-slice_fusion.1
  486.5 1.1 constant_dynamic-update-slice_fusion
  487.6 7.6 %convolution_convert_fusion = bf16[1024,2048]{1,0:T(8,128)(2,1)} fusion(bf16[1024,768]{1,0:T(8,128)(2,1)S(1)} %constant_dynamic-update-slice_fusion, bf16[2048,768]{1,0:T(8,128)(2,1)} %bitcast.148), kind=kOutput, calls=%fused_computation.31 | convolution fusion | flops 3223322624 | bytes 8912896 | tf_op jit(solution)/shard_map/te,de->td/dot_general | solution.py:1360
  495.2 2.0 convert_reduce_fusion.2
  497.2 1.6 fusion.36
  499.1 1.4 fusion.20.up_s
  500.6 1.6 multiply_reduce_fusion.1
  502.2 8.7 %fusion.19 = bf16[2048,768]{1,0:T(8,128)(2,1)} fusion(bf16[1024,768]{1,0:T(8,128)(2,1)} %copy-done.6, bf16[1024,2048]{1,0:T(8,128)(2,1)} %bitcast.111, f32[2048]{0:T(1024)S(1)} %add.226, f32[2048]{0:T(1024)S(1)} %mul.213, f32[1024]{0:T(1024)S(1)} %get-tuple-element.118, f32[1024]{0:T(1024)S(1)} %get-tuple-element.116), kind=kOutput, calls=%fused_computation.32 | convolution fusion | flops 3235381248 | bytes 8937472 | tf_op jit(solution)/shard_map/td,te->de/dot_general | solution.py:1360
  510.9 2.3 convolution_convert_fusion.1
  513.2 72.7 %scatter_and_hand.1 = (f32[128,2048]{1,0:T(8,128)}, bf16[64,8192]{1,0:T(8,128)(2,1)}, bf16[128,2048]{1,0:T(8,128)(2,1)}, bf16[3,8,64,768]{3,2,1,0:T(8,128)(2,1)}, bf16[3,64,2048]{2,1,0:T(8,128)(2,1)}) custom-call(bf16[8,128,2048]{2,1,0:T(8,128)(2,1)} %bitcast.123, bf16[8,64,1024]{2,1,0:T(8,128)(2,1)} %fusion.20.up_s, ...), custom_call_target="tpu_custom_call" | custom-call | tf_op jit(solution)/shard_map/scatter_and_hand/pallas_call | solution.py:296
  585.9 1.9 fusion.34
  587.9 1.8 fusion.33.grad
  591.9 1.4 pad_maximum_fusion.1
  593.4 2.2 convert_reduce_fusion.3
  595.6 1.3 fusion.37
  597.2 27.4 %finish.1 = (bf16[128,2048]{1,0:T(8,128)(2,1)S(1)}, f32[8,128]{1,0:T(8,128)S(1)}, bf16[64,6144]{1,0:T(8,128)(2,1)S(1)}) custom-call(bf16[128,2048]{1,0:T(8,128)(2,1)S(1)} %fusion.33.grad, f32[32,8,128]{2,1,0:T(8,128)S(1)} %bitcast.104, bf16[8,64,768]{2,1,0:T(8,128)(2,1)S(1)} %fusion.21.qkv_s), custom_call_target="tpu_custom_call" | custom-call | tf_op jit(solution)/shard_map/finish/pallas_call | solution.py:860
  624.6 1.2 convert_element_type.168
  626.0 1.9 convert_add_fusion.3
  627.9 1.5 convert_element_type.172
  630.1 2.8 convert_add_fusion
  634.5 0.8 copy.83
  635.3 0.8 copy.84
  (123 shorter events, 12.9 us)
Async XLA Ops:
  99.8 2.9 copy-start.14
  107.8 6.4 %copy-start.13 = (f32[32,8,128]{2,1,0:T(8,128)S(1)}, f32[32,8,128]{2,1,0:T(8,128)}, u32[]{:S(2)}) copy-start(f32[32,8,128]{2,1,0:T(8,128)} %get-tuple-element.47) | copy-start | bytes 393220
  114.5 3.5 copy-start
  353.3 6.5 %copy-start.2 = (bf16[128,2048]{1,0:T(8,128)(2,1)}, bf16[128,2048]{1,0:T(8,128)(2,1)S(1)}, u32[]{:S(2)}) copy-start(bf16[128,2048]{1,0:T(8,128)(2,1)S(1)} %get-tuple-element.85.branch) | copy-start | bytes 1572868
  487.5 7.6 %copy-start.6 = (bf16[1024,768]{1,0:T(8,128)(2,1)}, bf16[1024,768]{1,0:T(8,128)(2,1)S(1)}, u32[]{:S(2)}) copy-start(bf16[1024,768]{1,0:T(8,128)(2,1)S(1)} %constant_dynamic-update-slice_fusion) | copy-start | bytes 4718596
  487.6 7.6 %copy-start.5 = (bf16[3,8,64,1024]{3,2,1,0:T(8,128)(2,1)S(1)}, bf16[3,8,64,1024]{3,2,1,0:T(8,128)(2,1)}, u32[]{:S(2)}) copy-start(bf16[3,8,64,1024]{3,2,1,0:T(8,128)(2,1)} %get-tuple-element.61) | copy-start | bytes 9437188
  497.2 1.9 copy-start.1
  497.2 3.4 copy-start.9
  502.2 8.7 %copy-start.11 = (bf16[1024,256]{1,0:T(8,128)(2,1)S(1)}, bf16[1024,256]{1,0:T(8,128)(2,1)}, u32[]{:S(2)}) copy-start(bf16[1024,256]{1,0:T(8,128)(2,1)} %get-tuple-element.50) | copy-start | bytes 1572868
  502.2 8.7 %copy-start.16 = (bf16[8,128,2048]{2,1,0:T(8,128)(2,1)S(1)}, bf16[8,128,2048]{2,1,0:T(8,128)(2,1)}, u32[]{:S(2)}) copy-start(bf16[8,128,2048]{2,1,0:T(8,128)(2,1)} %get-tuple-element.63) | copy-start | bytes 12582916
  513.2 74.7 %copy-start.3 = (f32[128,2048]{1,0:T(8,128)S(1)}, f32[128,2048]{1,0:T(8,128)}, u32[]{:S(2)}) copy-start(f32[128,2048]{1,0:T(8,128)} %get-tuple-element.86) | copy-start | bytes 3145732
  585.9 4.0 copy-start.7
  585.9 5.2 copy-start.15
  596.9 28.9 %copy-start.10 = (bf16[3,64,2048]{2,1,0:T(8,128)(2,1)S(1)}, bf16[3,64,2048]{2,1,0:T(8,128)(2,1)}, u32[]{:S(2)}) copy-start(bf16[3,64,2048]{2,1,0:T(8,128)(2,1)} %get-tuple-element.70) | copy-start | bytes 2359300
  597.2 30.8 %copy-start.8 = (bf16[64,8192]{1,0:T(8,128)(2,1)S(1)}, bf16[64,8192]{1,0:T(8,128)(2,1)}, u32[]{:S(2)}) copy-start(bf16[64,8192]{1,0:T(8,128)(2,1)} %get-tuple-element.71) | copy-start | bytes 3145732
  626.0 3.4 copy-start.4
  629.4 5.1 copy-start.12

commit v5 on v4

--- a/solution.py
+++ b/solution.py
@@ -819,14 +819,19 @@
     return [pltpu.SemaphoreType.DMA((1,))] * 2
 
 
-def finish_kernel(nz, runs, grad, small, qkv_s, grad_out, small_out, qkv_o, came, send, recv, *sems):
+def finish_kernel(nz, runs, has, *refs):
+    grad, small, *refs = refs
+    qkv_s = refs.pop(0) if has else None
+    grad_out, small_out, *refs = refs
+    qkv_o = refs.pop(0) if has else None
+    came, send, recv, *sems = refs
     pos = place()
     x, c, z, y = pos
     fsdp = 2 * nz
     devices = 4 * fsdp
     me = (x * 2 + c) * fsdp + z * 2 + y
-    es = exchange_stages(qkv_s, qkv_o, runs, *sems[:2], nz, pos)
-    ts = trade_stages(grad, grad_out, *sems[2:], pos)
+    es = exchange_stages(qkv_s, qkv_o, runs, *sems[2:], nz, pos) if has else [lambda: None] * 2
+    ts = trade_stages(grad, grad_out, *sems[:2], pos)
     greet_all(devices, fsdp, me)
 
     def each(fn):
@@ -856,23 +861,23 @@
 
 def finish(grad, small, qkv_s, runs, nz, cid):
     devices = small.shape[0]
-    out_shape = qkv_s.shape if runs is None else (qkv_s.shape[1], qkv_s.shape[0] * qkv_s.shape[2])
+    has = qkv_s is not None
+    shapes = [jax.ShapeDtypeStruct(grad.shape, grad.dtype), jax.ShapeDtypeStruct(small.shape[1:], F32)]
+    if has:
+        out_shape = qkv_s.shape if runs is None else (qkv_s.shape[1], qkv_s.shape[0] * qkv_s.shape[2])
+        shapes.append(jax.ShapeDtypeStruct(out_shape, BF))
     return pl.pallas_call(
-        functools.partial(finish_kernel, nz, runs),
-        out_shape=[
-            jax.ShapeDtypeStruct(grad.shape, grad.dtype),
-            jax.ShapeDtypeStruct(small.shape[1:], F32),
-            jax.ShapeDtypeStruct(out_shape, BF),
-        ],
-        in_specs=[HBM, VM, HBM],
-        out_specs=[HBM, VM, HBM],
+        functools.partial(finish_kernel, nz, runs, has),
+        out_shape=shapes,
+        in_specs=[HBM, VM] + [HBM] * has,
+        out_specs=[HBM, VM] + [HBM] * has,
         scratch_shapes=[pltpu.VMEM(small.shape, F32)]
         + [pltpu.SemaphoreType.DMA((devices,))] * 2
-        + exchange_sems(runs, nz)
-        + trade_sems(),
+        + trade_sems()
+        + (exchange_sems(runs, nz) if has else []),
         compiler_params=params(cid, 32 * MIB),
         name="finish",
-    )(grad, small, qkv_s)
+    )(*((grad, small, qkv_s) if has else (grad, small)))
 
 
 def dot(a, b, dims):
@@ -882,6 +887,411 @@
 NN = ((1,), (0,))
 NT = ((1,), (1,))
 TN = ((0,), (0,))
+
+
+def scatter_parts(nz, pos, own, other, acc, came, send, recv):
+    x, c, z, y = pos
+    S, U, D = 0, nz, 2 * nz
+    sib = at(x, 1 - c, z, y)
+
+    def f(v):
+        return v.astype(F32)
+
+    def swap(t):
+        return remote(other(t), acc.at[t], send.at[S + t], recv.at[S + t], sib)
+
+    def rise(t):
+        return remote(acc.at[t], came.at[t], send.at[U + t], recv.at[U + t], at(x, c, z + 1, y))
+
+    def fall(t):
+        slot = jnp.where(z - 1 == t, nz, t)
+        return remote(acc.at[t], came.at[slot], send.at[D + t], recv.at[D + t], at(x, c, z - 1, y))
+
+    def arrival(slot, sem):
+        return remote(came.at[slot], came.at[slot], send.at[S], recv.at[sem], sib)
+
+    def event(t, upward):
+        swap(t).wait_recv()
+
+        @pl.when(z > 0 if upward else z < nz - 1)
+        def _():
+            arrival(t, (U if upward else D) + t).wait_recv()
+            acc[t] = (f(acc[t]) + f(own(t)) + f(came[t])).astype(BF)
+
+        @pl.when(z == 0 if upward else z == nz - 1)
+        def _():
+            acc[t] = (f(acc[t]) + f(own(t))).astype(BF)
+
+        (rise if upward else fall)(t).start()
+
+    def events(s):
+        for t in range(nz):
+            zz = s - t
+            if 0 <= zz < t:
+                pl.when(z == zz)(functools.partial(event, t, True))
+            zz = 2 * (nz - 1) - s - t
+            if t < zz < nz:
+                pl.when(z == zz)(functools.partial(event, t, False))
+
+    def total(out):
+        swap(z).wait_recv()
+        out[...] = f(acc[z]) + f(own(z))
+
+        @pl.when(z > 0)
+        def _():
+            arrival(z, U + z).wait_recv()
+            out[...] += f(came[z])
+
+        @pl.when(z < nz - 1)
+        def _():
+            arrival(nz, D + z).wait_recv()
+            out[...] += f(came[nz])
+
+    def done():
+        for t in range(nz):
+            swap(t).wait_send()
+            pl.when(z < t)(lambda t=t: rise(t).wait_send())
+            pl.when(z > t)(lambda t=t: fall(t).wait_send())
+
+    return swap, events, total, done
+
+
+def reduce_parts(src, mine, near, far, send, recv, lsem, pos):
+    x, c, z, y = pos
+    half = src.shape[1] // 2
+
+    def f(v):
+        return v.astype(F32)
+
+    def share(gx, gy, lower):
+        return src.at[gx * 2 + gy, pl.ds(lower * half, half)]
+
+    parts = [(x, y, 0), (x, y, 1), (x, 1 - y, 0), (1 - x, y, 1)]
+    loads = [pltpu.make_async_copy(share(*p), mine.at[i], lsem.at[i]) for i, p in enumerate(parts)]
+    along_x, along_y = at(1 - x, c, z, y), at(x, c, z, 1 - y)
+
+    def out(i):
+        a, b, target = [
+            (share(1 - x, y, 0), near.at[0, 0], along_x),
+            (share(1 - x, 1 - y, 0), near.at[0, 1], along_x),
+            (share(x, 1 - y, 1), near.at[1, 0], along_y),
+            (share(1 - x, 1 - y, 1), near.at[1, 1], along_y),
+        ][i]
+        return remote(a, b, send.at[i], recv.at[i], target)
+
+    def on(i):
+        return remote(near.at[i, 1], far.at[i], send.at[4 + i], recv.at[4 + i], [along_y, along_x][i])
+
+    def first():
+        for i in (1, 3, 0, 2):
+            out(i).start()
+        for copy in loads:
+            copy.start()
+
+    def second():
+        for copy in loads:
+            copy.wait()
+        for i in range(2):
+            out(2 * i + 1).wait_recv()
+            near[i, 1] = (f(near[i, 1]) + f(mine[2 + i])).astype(BF)
+            on(i).start()
+
+    def total(put):
+        for i in range(2):
+            out(2 * i).wait_recv()
+            on(i).wait_recv()
+            put(i, f(mine[i]) + f(near[i, 0]) + f(far[i]))
+
+    def done():
+        for i in range(4):
+            out(i).wait_send()
+        for i in range(2):
+            on(i).wait_send()
+
+    return first, second, total, done
+
+
+def reduce_scratch(rows, width):
+    half = rows // 2
+    return [
+        pltpu.VMEM((4, half, width), BF),
+        pltpu.VMEM((2, 2, half, width), BF),
+        pltpu.VMEM((2, half, width), BF),
+        pltpu.SemaphoreType.DMA((6,)),
+        pltpu.SemaphoreType.DMA((6,)),
+        pltpu.SemaphoreType.DMA((4,)),
+    ]
+
+
+def tail_kernel(
+    heads, nz, runs_up, runs_qkv, slopes, far_in, grad_in, joined, a1_in, mixed, qkv_in, branch, upd_in, up_src, down_src,
+    base, grad_out, down_o, out_o, col_o, square_o, up_o, qkv_o, branch_all, layer_o, grad_s, *refs,
+):
+    refs = list(refs)
+
+    def take(n):
+        got = refs[:n]
+        del refs[:n]
+        return got
+
+    gap_s, tokens, qkv_w, grad_joined, acc_k, acc_v = take(6)
+    upd_own, upd_acc, upd_came, upd_send, upd_recv = take(5)
+    att_p, att_acc, att_came, att_send, att_recv = take(5)
+    up_refs, down_refs, qkv_refs, out_refs = take(6), take(6), take(6), take(6)
+    up_sum, qkv_sum, qkv_g, out_g, res, res_low = take(6)
+    gsems, esems, esems_up, esems_qkv, tsems = take(2), take(2), take(2), take(2), take(2)
+    gap_sem, load_sem = take(2)
+
+    pos = place()
+    x, c, z, y = pos
+    n = 2 * nz
+    tree, cols = mixed.shape
+    rows, width = branch.shape
+    part = up_sum.shape[1]
+    rank = z * 2 + c
+    step = gap_s.shape[2]
+
+    es = exchange_stages(grad_in, grad_s, None, *esems, nz, pos)
+    gb = line_gather(branch, branch_all, *gsems, nz, False, pos)
+    up1, up2, up_total, up_done = reduce_parts(up_src, *up_refs, pos)
+    down1, down2, down_total, down_done = reduce_parts(down_src, *down_refs, pos)
+    qkv1, qkv2, qkv_total, qkv_done = reduce_parts(qkv_g, *qkv_refs, pos)
+    out1, out2, out_total, out_done = reduce_parts(out_g, *out_refs, pos)
+    upd_swap, upd_events, upd_total, upd_done = scatter_parts(
+        nz, pos, lambda t: upd_own[t], lambda t: upd_in.at[t * 2 + 1 - c], upd_acc, upd_came, upd_send, upd_recv
+    )
+    att_swap, att_events, att_total, att_done = scatter_parts(
+        nz, pos, lambda t: att_p[t * 2 + c], lambda t: att_p.at[t * 2 + 1 - c], att_acc, att_came, att_send, att_recv
+    )
+    ex_up = exchange_stages(up_sum, up_o, runs_up, *esems_up, nz, pos)
+    ex_qkv = exchange_stages(qkv_sum, qkv_o, runs_qkv, *esems_qkv, nz, pos)
+    home = trade_stages(res_low, layer_o, *tsems, pos)
+    loads = [pltpu.make_async_copy(upd_in.at[t * 2 + c], upd_own.at[t], load_sem.at[t]) for t in range(nz)]
+    load_w = pltpu.make_async_copy(qkv_in, qkv_w, load_sem.at[nz])
+    load_a = pltpu.make_async_copy(a1_in, tokens, load_sem.at[nz + 1])
+    load_b = pltpu.make_async_copy(branch_all, tokens, load_sem.at[nz + 2])
+
+    def gap_load(i, slot):
+        return pltpu.make_async_copy(
+            far_in.at[:, pl.ds(pl.multiple_of(i * step, step), step)], gap_s.at[slot], gap_sem.at[slot]
+        )
+
+    greet(rank_partners(nz, pos) + group_partners(pos) + [(c != y, at(x, y, z, c))])
+    es[0]()
+    up1()
+    gb[0]()
+    gb[1]()
+    for t in list(range(nz - 1, 0, -1)) + [0]:
+        upd_swap(t).start()
+    gap_load(0, 0).start()
+    for copy in loads + [load_w, load_a]:
+        copy.start()
+    acc_k[...] = jnp.zeros_like(acc_k)
+    acc_v[...] = jnp.zeros_like(acc_v)
+    for copy in loads:
+        copy.wait()
+    es[1]()
+
+    steps = tree // step
+
+    def attend_step(i, _):
+        slot = i % 2
+        gap_load(i, slot).wait()
+        pl.when(i + 1 < steps)(lambda: gap_load(i + 1, 1 - slot).start())
+        gap = gap_s[slot]
+        here = pl.ds(pl.multiple_of(i * step, step), step)
+        per = step // rows
+        grads = grad_s[pl.ds(i * per, per)].reshape(step, cols)
+        for h in range(heads):
+            lane = slice(h * HD, (h + 1) * HD)
+            q = joined[here, lane]
+            k = joined[:, cols + h * HD : cols + (h + 1) * HD]
+            v = joined[:, 2 * cols + h * HD : 2 * cols + (h + 1) * HD]
+            g = grads[:, lane]
+            logits = dot(k, q, NT) * HD ** (-0.5) + slopes[h] * gap
+            weights = jnp.exp(logits - jnp.max(logits, axis=0, keepdims=True))
+            probs = weights * (1.0 / jnp.sum(weights, axis=0, keepdims=True))
+            grad_probs = dot(v, g, NT)
+            delta = jnp.sum(probs * grad_probs, axis=0, keepdims=True)
+            grad_raw = (probs * (grad_probs - delta) * HD ** (-0.5)).astype(BF)
+            acc_v[:, lane] += dot(probs.astype(BF), g, NN)
+            acc_k[:, lane] += dot(grad_raw, q, NN)
+            grad_joined[here, lane] = dot(grad_raw, k, TN).astype(BF)
+
+        def later(k, fns):
+            @pl.when(i == k)
+            def _():
+                for fn in fns:
+                    fn()
+
+        later(0, [down1, lambda: upd_events(0)])
+        later(1, [gb[2], lambda: upd_events(1)])
+        later(2, [up2] + gb[3:4] + [lambda: upd_events(2)])
+        later(3, gb[4:5] + [lambda: upd_events(3)])
+        return 0
+
+    lax.fori_loop(0, steps, attend_step, 0)
+    grad_joined[:, cols : 2 * cols] = acc_k[...].astype(BF)
+    grad_joined[:, 2 * cols :] = acc_v[...].astype(BF)
+    load_w.wait()
+
+    def back(t, _):
+        here = pl.ds(pl.multiple_of(t * 2 * rows, 2 * rows), 2 * rows)
+
+        def tile(j, _):
+            w = pl.ds(pl.multiple_of(j * 512, 512), 512)
+            att_p[pl.ds(t * 2, 2), :, w] = dot(grad_joined[here, :], qkv_w[w, :], NT).astype(BF).reshape(2, rows, 512)
+            return 0
+
+        lax.fori_loop(0, width // 512, tile, 0)
+        att_swap(t).start()
+        return 0
+
+    lax.fori_loop(0, nz, back, 0)
+    col_o[...] = jnp.sum(grad_joined[...].astype(F32), axis=0, keepdims=True)
+    load_a.wait()
+    blocks = 256 // part
+
+    def qkv_tile(j, _):
+        w = pl.ds(pl.multiple_of(j * 256, 256), 256)
+        value = dot(tokens[:, :, w].reshape(tree, 256), grad_joined[...], TN).astype(BF)
+        for i in range(blocks):
+            r = j * blocks + i
+            d, f = r // n, r % n
+            p = f // 2 * 2 + d % 2
+            qkv_g[d // 2 * 2 + f % 2, pl.ds(pl.multiple_of(p * part, part), part), :] = value[i * part : (i + 1) * part]
+        return 0
+
+    att_events(0)
+    lax.fori_loop(0, width // 256, qkv_tile, 0)
+    qkv1()
+    upd_events(4)
+    att_events(1)
+    down2()
+    for stage in gb[5:]:
+        stage()
+    load_b.start()
+    load_b.wait()
+
+    def out_tile(j, _):
+        w = pl.ds(pl.multiple_of(j * 512, 512), 512)
+        value = dot(mixed[...], tokens[:, :, w].reshape(tree, 512), TN).astype(BF)
+        out_g[:, :, w] = value.reshape(4, cols // 4, 512)
+        return 0
+
+    lax.fori_loop(0, width // 512, out_tile, 0)
+    out1()
+    upd_events(5)
+    att_events(2)
+
+    def put_ranks(dest):
+        def put(lower, value):
+            dest[pl.ds(lower * nz, nz)] = value.astype(BF).reshape(nz, part, -1)
+
+        return put
+
+    up_total(put_ranks(up_sum))
+    ex_up[0]()
+    upd_events(6)
+    upd_total(res)
+    res[...] += base[...]
+    res_low[...] = res[...].astype(BF)
+    home[0]()
+    square_o[...] = jnp.sum(res[...] * res[...], axis=0, keepdims=True)
+    att_events(3)
+    qkv2()
+    att_events(4)
+    out2()
+
+    def put_down(lower, value):
+        half = value.shape[0]
+        down_o[pl.ds(lower * half, half), :] = value
+
+    down_total(put_down)
+    att_events(5)
+    att_events(6)
+    att_total(grad_out)
+    ex_up[1]()
+
+    def put_out(lower, value):
+        half = value.shape[0]
+        out_o[pl.ds(lower * half, half), :] = value
+
+    out_total(put_out)
+    qkv_total(put_ranks(qkv_sum))
+    ex_qkv[0]()
+    home[1]()
+    ex_qkv[1]()
+    for fn in (up_done, down_done, qkv_done, out_done, upd_done, att_done):
+        fn()
+
+
+def tail_call(slopes, far_t, grad, joined, a1, mixed, qkv_w, branch, upd, up_g, down_g, base, runs, heads, nz, cid):
+    tree, cols = mixed.shape
+    rows, width = branch.shape
+    n = 2 * nz
+    part = width // (4 * n)
+    unit = down_g.shape[1]
+    step = 256
+    runs_up, runs_qkv = runs
+    shape = jax.ShapeDtypeStruct
+
+    def scatter_refs(own):
+        return [
+            pltpu.VMEM((own, rows, width), BF),
+            pltpu.VMEM((nz, rows, width), BF),
+            pltpu.VMEM((nz + 1, rows, width), BF),
+            pltpu.SemaphoreType.DMA((3 * nz,)),
+            pltpu.SemaphoreType.DMA((3 * nz,)),
+        ]
+
+    return pl.pallas_call(
+        functools.partial(tail_kernel, heads, nz, runs_up, runs_qkv),
+        out_shape=[
+            shape((rows, width), F32),
+            shape((unit, width), F32),
+            shape((part, width), F32),
+            shape((1, 3 * cols), F32),
+            shape((1, width), F32),
+            shape((part, 4 * n * unit), BF),
+            shape((part, 3 * width), BF),
+            shape((n, rows, width), BF),
+            shape((rows, width), BF),
+        ],
+        in_specs=[pl.BlockSpec(memory_space=pltpu.SMEM), HBM, HBM, VM, HBM, VM, HBM, HBM, HBM, HBM, HBM, VM],
+        out_specs=[VM] * 5 + [HBM] * 4,
+        scratch_shapes=[
+            pltpu.VMEM((n, rows, cols), BF),
+            pltpu.VMEM((2, tree, step), F32),
+            pltpu.VMEM((n, rows, width), BF),
+            pltpu.VMEM((width, 3 * cols), BF),
+            pltpu.VMEM((tree, 3 * cols), BF),
+            pltpu.VMEM((tree, cols), F32),
+            pltpu.VMEM((tree, cols), F32),
+        ]
+        + scatter_refs(nz)
+        + scatter_refs(n)
+        + reduce_scratch(n * part, 4 * unit)
+        + reduce_scratch(unit, width)
+        + reduce_scratch(n * part, 3 * cols)
+        + reduce_scratch(part, width)
+        + [
+            pltpu.VMEM((n, part, 4 * unit), BF),
+            pltpu.VMEM((n, part, 3 * cols), BF),
+            pltpu.VMEM((4, n * part, 3 * cols), BF),
+            pltpu.VMEM((4, part, width), BF),
+            pltpu.VMEM((rows, width), F32),
+            pltpu.VMEM((rows, width), BF),
+        ]
+        + gather_sems(nz)
+        + exchange_sems(None, nz)
+        + exchange_sems(runs_up, nz)
+        + exchange_sems(runs_qkv, nz)
+        + trade_sems()
+        + [pltpu.SemaphoreType.DMA((2,)), pltpu.SemaphoreType.DMA((nz + 3,))],
+        compiler_params=params(cid, 63 * MIB),
+        name="tail",
+    )(slopes, far_t, grad, joined, a1, mixed, qkv_w, branch, upd, up_g, down_g, base)
 
 
 def gelu_and_slope(value):
@@ -912,10 +1322,25 @@
         pltpu.make_async_copy(a, b, lsem.at[i])
         for i, (a, b) in enumerate([(cot_in, cot), (down_in, down_w), (up_in, up_w)])
     ]
+    part = up_out.shape[1] // blocks
+
+    def rank_rows(r):
+        d, f = r // blocks, r % blocks
+        return up_out.at[d // 2 * 2 + f % 2, pl.ds((f // 2 * 2 + d % 2) * part, part)]
+
     stores = [
-        pltpu.make_async_copy(a, b, lsem.at[3 + i])
-        for i, (a, b) in enumerate([(upd, upd_out), (up_g, up_out), (down_g, down_out)])
+        [pltpu.make_async_copy(upd, upd_out, lsem.at[3])],
+        [
+            pltpu.make_async_copy(up_g.at[pl.ds(r * part, part)], rank_rows(r), lsem.at[5 + r])
+            for r in range(4 * blocks)
+        ],
+        [pltpu.make_async_copy(down_g, down_out, lsem.at[4])],
     ]
+
+    def store(i):
+        for copy in stores[i]:
+            copy.start()
+
 
     def block(b, sem, target):
         return remote(mlp.at[b], mlp.at[b], gsend.at[sem], grecv.at[sem], target)
@@ -1052,14 +1477,14 @@
         if s < nz:
             forward_part(zi)
         if s == nz - 1:
-            stores[0].start()
+            store(0)
             down_grads()
-            stores[2].start()
+            store(2)
         elif s == nz:
             up_grads(0, tiles // 2)
         elif s == nz + 1:
             up_grads(tiles // 2, tiles - tiles // 2)
-            stores[1].start()
+            store(1)
     swap(z).wait_recv()
     out[...] = f(acc[z]) + f(p[z * 2 + c])
 
@@ -1073,8 +1498,9 @@
         fall(z).wait_recv()
         out[...] += f(dns[z])
 
-    for copy in stores:
-        copy.wait()
+    for copies in stores:
+        for copy in copies:
+            copy.wait()
     side(0, z >= 0).wait_send()
     pl.when(z < nz - 1)(up(0).wait_send)
     pl.when(z > 0)(dn(0).wait_send)
@@ -1111,7 +1537,7 @@
         out_shape=[
             shape((rows, width), F32),
             shape((n, rows, width), BF),
-            shape((width, units), BF),
+            shape((4, width // 4, units), BF),
             shape((units, width), BF),
             shape((1, units), F32),
         ],
@@ -1132,7 +1558,7 @@
         + [pltpu.VMEM((nz, rows, width), BF)] * 3
         + gather_sems(nz)
         + [pltpu.SemaphoreType.DMA((3 * nz,))] * 2
-        + [pltpu.SemaphoreType.DMA((6,))],
+        + [pltpu.SemaphoreType.DMA((5 + 4 * n,))],
         compiler_params=params(cid, 62 * MIB),
         name="mlp",
     )(own, cot, up_w, down_w, bias)
@@ -1473,7 +1899,8 @@
     normed_two, inverse_two = norm_parts(middle)
     mlp_own = (normed_two * gain_two + shift_two).astype(BF)
     cot_blocks = cot.reshape(fsdp, rows, width)
-    if mlp_bytes(nz, rows, width, 4 * unit) < 50 * MIB:
+    fused = aligned and nz == 4 and mlp_bytes(nz, rows, width, 4 * unit) < 50 * MIB
+    if fused:
         grad_mlp_in, update, up_g, down_g, grad_bias_up = mlp_call(
             mlp_own, cot_blocks, up_w, down_w, up_bias[None], nz, 3
         )
@@ -1492,8 +1919,6 @@
         up_g = mm("td,tf->df", mlp_in, grad_hidden).astype(BF)
         grad_bias_up = jnp.sum(grad_hidden.astype(F32), axis=0)
     down_g = down_g.reshape(4, unit, width)
-    up_g = up_g.reshape(devices, part, 4 * unit)
-
     cot_own = own_rows(cot).astype(F32)
     grad_middle = cot_own + norm_back(grad_mlp_in * gain_two, normed_two, inverse_two)
     grad_branch = grad_middle.astype(BF)
@@ -1506,39 +1931,48 @@
         grad_mixed = grad_mixed.reshape(rows, 2, 2, nz, 2 * HD).transpose(3, 2, 0, 1, 4).reshape(fsdp, rows, cols)
     else:
         grad_mixed = grad_mixed.reshape(rows, fsdp, cols).transpose(1, 0, 2)
-    grad_heads = exchange(grad_mixed, nz, 5, "grad_to_heads")
-    grad_heads = grad_heads.reshape(tree, cols)
-    grad_q, grad_k, grad_v, branch_all, update, down_c, up_c = attend_back(
-        slopes, far.T, joined, grad_heads, grad_branch, update, [down_g, up_g], (False, True), heads, nz, 6
-    )
-    result = middle + update + down_bias
-    grad_joined = jnp.concatenate([grad_q, grad_k, grad_v], axis=1)
-
-    def mine(g, came):
-        g = g.reshape((2, 2, nz, 2) + g.shape[1:])
-        g = lax.dynamic_slice(g, (x, 0, 0, y, 0, 0), (1, 2, nz, 1) + g.shape[4:])
-        g = g.reshape((2, nz) + g.shape[4:]).swapaxes(0, 1)
-        return (g.reshape(came.shape[1:]).astype(F32) + jnp.sum(came.astype(F32), axis=0)).astype(BF)
-
-    def mine_flat(g, came):
-        return lax.dynamic_index_in_dim(g, x * 2 + y, 0, keepdims=False).astype(F32) + jnp.sum(came.astype(F32), axis=0)
-
-    grad_down_w = mine_flat(down_g, down_c)
-    qkv_g = mm("td,te->de", attn_in, grad_joined).astype(BF).reshape(devices, part, 3 * cols)
-    flat = []
-    if aligned:
-        flat = [mm("td,te->de", mixed, branch_all.reshape(tree, width)).astype(BF).reshape(4, part, width)]
-    kinds = (True,) + (False,) * len(flat)
-    grad_attn_in = mm("te,de->td", grad_joined, qkv_w).astype(BF).reshape(fsdp, rows, width)
-    grad_attn_in, grad_up_w, layer_out, qkv_c, *out_c = scatter_and_hand(
-        grad_attn_in, mine(up_g, up_c), up_runs(nz, unit), result.astype(BF), [qkv_g] + flat, kinds, nz, 10
-    )
+    if fused:
+        runs = up_runs(nz, unit), qkv_runs(nz, width, cols)
+        grad_attn_in, grad_down_w, grad_out_w, col, square, grad_up_w, grad_qkv_w, _, layer_out = tail_call(
+            slopes, far.T, grad_mixed, joined, attn_in.reshape(fsdp, rows, width), mixed, qkv_w, grad_branch,
+            update, up_g, down_g, middle + down_bias, runs, heads, nz, 6,
+        )
+        col, square = col[0], jnp.sum(square)
+    else:
+        up_g = up_g.reshape(devices, part, 4 * unit)
+        grad_heads = exchange(grad_mixed, nz, 5, "grad_to_heads")
+        grad_heads = grad_heads.reshape(tree, cols)
+        grad_q, grad_k, grad_v, branch_all, update, down_c, up_c = attend_back(
+            slopes, far.T, joined, grad_heads, grad_branch, update, [down_g, up_g], (False, True), heads, nz, 6
+        )
+        result = middle + update + down_bias
+        grad_joined = jnp.concatenate([grad_q, grad_k, grad_v], axis=1)
+
+        def mine(g, came):
+            g = g.reshape((2, 2, nz, 2) + g.shape[1:])
+            g = lax.dynamic_slice(g, (x, 0, 0, y, 0, 0), (1, 2, nz, 1) + g.shape[4:])
+            g = g.reshape((2, nz) + g.shape[4:]).swapaxes(0, 1)
+            return (g.reshape(came.shape[1:]).astype(F32) + jnp.sum(came.astype(F32), axis=0)).astype(BF)
+
+        def mine_flat(g, came):
+            return lax.dynamic_index_in_dim(g, x * 2 + y, 0, keepdims=False).astype(F32) + jnp.sum(came.astype(F32), axis=0)
+
+        grad_down_w = mine_flat(down_g, down_c)
+        qkv_g = mm("td,te->de", attn_in, grad_joined).astype(BF).reshape(devices, part, 3 * cols)
+        flat = []
+        if aligned:
+            flat = [mm("td,te->de", mixed, branch_all.reshape(tree, width)).astype(BF).reshape(4, part, width)]
+        kinds = (True,) + (False,) * len(flat)
+        grad_attn_in = mm("te,de->td", grad_joined, qkv_w).astype(BF).reshape(fsdp, rows, width)
+        grad_attn_in, grad_up_w, layer_out, qkv_c, *out_c = scatter_and_hand(
+            grad_attn_in, mine(up_g, up_c), up_runs(nz, unit), result.astype(BF), [qkv_g] + flat, kinds, nz, 10
+        )
+        grad_up_w = grad_up_w.astype(F32)
+        if aligned:
+            grad_out_w = mine_flat(flat[0], out_c[0])
+        col, square = jnp.sum(grad_joined.astype(F32), axis=0), jnp.sum(result * result)
     grad_up_w = grad_up_w.astype(F32)
-    if aligned:
-        grad_out_w = mine_flat(flat[0], out_c[0])
     grad_inputs = grad_middle + norm_back(grad_attn_in * gain_one, normed_one, inverse_one)
-
-    col = jnp.sum(grad_joined.astype(F32), axis=0)
 
     smalls = [
         jnp.sum(grad_attn_in * normed_one, axis=0),
@@ -1552,15 +1986,18 @@
     ]
     grad_bias_up = grad_bias_up.reshape(2, 1, 1, 2, unit)
     grad_bias_up = lax.dynamic_update_slice(jnp.zeros((2, 2, nz, 2, unit), F32), grad_bias_up, (0, c, z, 0, 0))
-    squares = jnp.stack([jnp.sum(result * result), jnp.sum(branch * branch)])
+    squares = jnp.stack([square, jnp.sum(branch * branch)])
     packed = jnp.concatenate(
         [v.reshape(devices, part) for v in smalls]
         + [grad_bias_up.reshape(devices, unit), jnp.broadcast_to(squares, (devices, 2))],
         axis=1,
     )
     packed = padded(packed, 1024).reshape(devices, -1, 128)
-    runs = qkv_runs(nz, width, cols) if aligned else None
-    grad_x, packed, grad_qkv_w = finish(grad_inputs.astype(BF), packed, mine(qkv_g, qkv_c), runs, nz, 8)
+    if fused:
+        grad_x, packed = finish(grad_inputs.astype(BF), packed, None, None, nz, 8)
+    else:
+        runs = qkv_runs(nz, width, cols) if aligned else None
+        grad_x, packed, grad_qkv_w = finish(grad_inputs.astype(BF), packed, mine(qkv_g, qkv_c), runs, nz, 8)
     if not aligned:
         grad_qkv_w = grad_qkv_w.reshape(fsdp, part, 3, cols).transpose(1, 2, 0, 3).reshape(part, -1)
     grad_qkv_w = grad_qkv_w.astype(F32)

time: 645 us -> 574 us (0.89)
  Pallas kernels: 519 us -> 484 us
  matrix products: 39.3 us -> 20.5 us
  other arithmetic: 51.2 us -> 35.9 us
    pallas_call x3 -> x2, Pallas kernels: 205 us -> 187 us  [the longest x1 171 us: tail_call(): pl.pallas_call(functools.partial(tail_kernel, heads, nz, runs_up, runs_qk...]
    dot_general x4 -> x1, matrix products: 25 us -> 6.44 us  [mm(): return jnp.einsum(spec, a, b, preferred_element_type=F32)]
    pallas_call x2 -> x1, Pallas kernels: 29.4 us -> 12.1 us  [exchange(): pl.pallas_call(functools.partial(exchange_kernel, nz), out_shape=jax.Shap...]
where the time goes in v5:
time: 574 us; the launch traced here: 566 us
  Pallas kernels  484 us (84%)
  other arithmetic  35.9 us (6%)
  local copies, waits for them, and re-layouts  24 us (4%)
  matrix products  20.5 us (4%)
    pallas_call x1, Pallas kernels, tail_call(): pl.pallas_call(functools.partial(tail_kernel, heads, nz, runs_up, runs_qk...  171 us
    pallas_call x1, Pallas kernels, attend(): pl.pallas_call(functools.partial(attend_kernel, heads, nz, unit), out_sha...  102 us
    pallas_call x1, Pallas kernels, mlp_call(): pl.pallas_call(functools.partial(mlp_kernel, nz), out_shape=[shape((rows,...  93.8 us
    pallas_call x1, Pallas kernels, fetch(): pl.pallas_call(functools.partial(fetch_kernel, nz, width, cols), out_shap...  88.7 us
    pallas_call x1, Pallas kernels, finish(): pl.pallas_call(functools.partial(finish_kernel, nz, runs, has), out_shape...  15.7 us
    pallas_call x1, Pallas kernels, exchange(): pl.pallas_call(functools.partial(exchange_kernel, nz), out_shape=jax.Shap...  12.1 us

profile of v5, /device:TPU:0, one launch (start us, length us, event | category | flops | bytes accessed | tf_op | source)
XLA Modules:
  0.0 565.6 jit_solution(8836521825531148704)
XLA Ops:
  0.8 0.6 reshape.356.slopes
  1.4 6.1 %concatenate.12 = bf16[768]{0:T(1024)(128)(2,1)S(1)} concatenate(bf16[64]{0:T(256)(128)(2,1)} %param.24, bf16[64]{0:T(256)(128)(2,1)} %param.25, bf16[64]{0:T(256)(128)(2,1)} %param.26, bf16[64]{0:T(256)(128)(2,1)} %param.27, bf16[64]{0:T(256)(128)(2,1)} %param.28, bf16[64]{0:T(256)(128)(2,1)} %param.29, bf16[64]{0:T(256)(128)(2,1)} %param.30, bf16[64]{0:T(256)(128)(2,1)} %param.32, ...), dimensions={0} | concatenate | bytes 3072 | tf_op jit(solution)/shard_map/concatenate | solution.py:1825
  7.4 0.6 bitcast_convert_fusion.vec
  8.0 0.8 concatenate.13
  8.8 0.6 pad_bitcast_fusion.1.tab
  9.4 88.7 %fetch.1 = (bf16[8,128,2048]{2,1,0:T(8,128)(2,1)}, bf16[32,64,768]{2,1,0:T(8,128)(2,1)}, bf16[4,256,2048]{2,1,0:T(8,128)(2,1)}, f32[32,8,128]{2,1,0:T(8,128)}, s32[16,128]{1,0:T(8,128)}) custom-call(bf16[128,2048]{1,0:T(8,128)(2,1)} %x_in.1, bf16[64,6144]{1,0:T(8,128)(2,1)} %w_qkv.1, bf16[256,2048]{1,0:T(8,128)(2,1)} %w_down.1, ...), custom_call_target="tpu_custom_call" | custom-call | tf_op jit(solution)/shard_map/fetch/pallas_call | solution.py:667
  98.1 0.7 slice.118
  98.9 0.8 slice.119
  99.8 1.0 broadcast_compare_fusion
  100.8 2.0 copy.54
  103.2 3.7 reduce-window.6
  107.8 6.3 %convert_select_fusion = (f32[1024,1024]{1,0:T(8,128)}, f32[1024,1024]{1,0:T(8,128)}) fusion(pred[1024,1024]{1,0:T(8,128)(4,1)S(1)} %copy.54, s32[1024]{0:T(1024)S(1)} %add.181, s32[1024]{0:T(1024)S(1)} %eq.110, pred[1024]{0:T(1024)(128)(4,1)S(1)} %broadcast_compare_fusion.1, pred[1024,1024]{0,1:T(8,128)(4,1)S(1)} %broadcast_compare_fusion), kind=kLoop, calls=%fused_computation.8 | loop fusion | flops 20971520 | bytes 10494976 | tf_op jit(solution)/shard_map/jit(_where)/select_n | solution.py:1885
  114.3 1.2 convert_reduce_fusion.1
  115.7 3.0 convert_reduce_fusion
  118.7 0.5 copy-done
  119.1 1.2 fusion.2
  120.4 3.1 fusion.5.a1_in
  123.7 6.7 %add_convert_fusion.joined_q.joined = bf16[1024,768]{1,0:T(8,128)(2,1)} fusion(bf16[1024,2048]{1,0:T(8,128)(2,1)} %bitcast.72, bf16[2048,768]{1,0:T(8,128)(2,1)S(1)} %bitcast.79, f32[768]{0:T(1024)S(1)} %pad_maximum_fusion), kind=kOutput, calls=%fused_computation.22 | convolution fusion | flops 3222798336 | bytes 8915968 | tf_op jit(solution)/shard_map/dot_general | solution.py:1875
  130.4 102.5 %attend.1 = (bf16[1024,256]{1,0:T(8,128)(2,1)}, bf16[8,128,2048]{2,1,0:T(8,128)(2,1)}, bf16[32,64,1024]{2,1,0:T(8,128)(2,1)}, bf16[32,64,2048]{2,1,0:T(8,128)(2,1)}) custom-call(f32[4]{0:T(128)} %reshape.356.slopes, f32[1024,1024]{1,0:T(8,128)} %get-tuple-element.92.far, bf16[1024,768]{1,0:T(8,128)(2,1)} %add_convert_fusion.joined_q.joined, ...), custom_call_target="tpu_custom_call" | custom-call | tf_op jit(solution)/shard_map/attend/pallas_call | solution.py:1630
  232.9 12.1 %mixed_to_tokens.1 = bf16[8,128,256]{2,1,0:T(8,128)(2,1)} custom-call(bf16[8,128,256]{2,1,0:T(8,128)(2,1)} %bitcast.81), custom_call_target="tpu_custom_call" | custom-call | tf_op jit(solution)/shard_map/mixed_to_tokens/pallas_call | solution.py:791
  244.9 1.2 reshape.334
  246.1 0.5 copy.55
  246.6 6.4 %broadcast_add_fusion = (f32[128,2048]{1,0:T(8,128)}, f32[128,2048]{1,0:T(8,128)S(1)}, f32[128]{0:T(128)S(1)}, f32[]{:T(128)}) fusion(f32[2048]{0:T(1024)S(1)} %add.202, bf16[1024,2048]{1,0:T(8,128)(2,1)} %bitcast.69, s32[]{:T(128)S(6)} %select_n.43, f32[128]{0:T(128)S(1)} %broadcast_multiply_fusion.3, f32[2048]{0:T(1024)S(1)} %add.193, ...), kind=kOutput, calls=%fused_computation.54 | convolution fusion | flops 1076100992 | bytes 11551752 | tf_op jit(solution)/shard_map/dot_general | solution.py:1897
  253.5 1.1 add_convert_fusion.1.own
  254.6 0.6 broadcast_in_dim_reshape.2.bias
  255.2 93.8 %mlp.1 = (f32[128,2048]{1,0:T(8,128)}, bf16[8,128,2048]{2,1,0:T(8,128)(2,1)}, bf16[4,512,1024]{2,1,0:T(8,128)(2,1)}, bf16[1024,2048]{1,0:T(8,128)(2,1)}, f32[1,1024]{1,0:T(1,128)}) custom-call(bf16[128,2048]{1,0:T(8,128)(2,1)} %add_convert_fusion.1.own, bf16[8,128,2048]{2,1,0:T(8,128)(2,1)} %get-tuple-element.44.cot_in, bf16[2048,1024]{1,0:T(8,128)(2,1)} %bitcast.75, ...), custom_call_target="tpu_custom_call" | custom-call | tf_op jit(solution)/shard_map/mlp/pallas_call | solution.py:1535
  349.1 1.7 multiply_reduce_fusion.1
  350.7 3.0 convert_reduce_fusion.3
  353.7 6.4 %convolution_convert_fusion = bf16[128,2048]{1,0:T(8,128)(2,1)S(1)} fusion(bf16[128,2048]{1,0:T(8,128)(2,1)S(1)} %get-tuple-element.77.branch, bf16[2048,2048]{1,0:T(8,128)(2,1)} %bitcast.67), kind=kOutput, calls=%fused_computation.24 | convolution fusion | flops 1074003968 | bytes 9437184 | tf_op jit(solution)/shard_map/te,de->td/dot_general | solution.py:1786
  360.5 0.4 copy.66
  361.0 1.1 reshape.341.grad_in
  362.1 171.0 %tail.1 = (f32[128,2048]{1,0:T(8,128)}, f32[256,2048]{1,0:T(8,128)}, f32[64,2048]{1,0:T(8,128)}, f32[1,768]{1,0:T(1,128)}, f32[1,2048]{1,0:T(1,128)}, /*index=5*...) custom-call(f32[4]{0:T(128)} %reshape.356.slopes, ...), custom_call_target="tpu_custom_call" | custom-call | tf_op jit(solution)/shard_map/tail/pallas_call | solution.py:1248
  533.1 2.0 fusion.26
  535.1 2.1 fusion.25.refs_0_
  537.9 0.5 broadcast.259
  538.4 0.7 reduce.13
  539.2 0.6 reduce_sum.228
  539.8 1.4 pad_maximum_fusion.1
  541.3 15.7 %finish.1 = (bf16[128,2048]{1,0:T(8,128)(2,1)S(1)}, f32[8,128]{1,0:T(8,128)S(1)}) custom-call(bf16[128,2048]{1,0:T(8,128)(2,1)S(1)} %fusion.25.refs_0_, f32[32,8,128]{2,1,0:T(8,128)S(1)} %bitcast.63), custom_call_target="tpu_custom_call" | custom-call | tf_op jit(solution)/shard_map/finish/pallas_call | solution.py:869
  557.1 1.2 convert_element_type.78
  558.3 1.5 convert_element_type.79
  559.8 0.6 fusion.38
  560.4 0.6 slice_bitcast_fusion
  560.9 0.5 multiply_sqrt_fusion
  561.5 0.8 copy.77
  562.2 0.8 copy.78
  563.0 0.8 copy.79
  563.8 1.3 copy.80
  (99 shorter events, 4.1 us)
Async XLA Ops:
  99.8 2.9 copy-start.9
  107.8 6.3 %copy-start.8 = (f32[32,8,128]{2,1,0:T(8,128)S(1)}, f32[32,8,128]{2,1,0:T(8,128)}, u32[]{:S(2)}) copy-start(f32[32,8,128]{2,1,0:T(8,128)} %get-tuple-element.42) | copy-start | bytes 393220
  115.7 3.5 copy-start
  120.4 3.3 copy-start.2
  353.7 6.5 %copy-start.1 = (bf16[128,2048]{1,0:T(8,128)(2,1)}, bf16[128,2048]{1,0:T(8,128)(2,1)S(1)}, u32[]{:S(2)}) copy-start(bf16[128,2048]{1,0:T(8,128)(2,1)S(1)} %get-tuple-element.77.branch) | copy-start | bytes 1572868
  533.1 4.3 copy-start.12
  533.1 5.3 copy-start.11
  533.1 6.1 %copy-start.10 = (f32[1,2048]{1,0:T(1,128)S(1)}, f32[1,2048]{1,0:T(1,128)}, u32[]{:S(2)}) copy-start(f32[1,2048]{1,0:T(1,128)} %get-tuple-element.57) | copy-start | bytes 24580
  533.1 23.9 %copy-start.5 = (bf16[64,6144]{1,0:T(8,128)(2,1)S(1)}, bf16[64,6144]{1,0:T(8,128)(2,1)}, u32[]{:S(2)}) copy-start(bf16[64,6144]{1,0:T(8,128)(2,1)} %get-tuple-element.59) | copy-start | bytes 2359300
  533.1 25.2 %copy-start.4 = (bf16[64,8192]{1,0:T(8,128)(2,1)S(1)}, bf16[64,8192]{1,0:T(8,128)(2,1)}, u32[]{:S(2)}) copy-start(bf16[64,8192]{1,0:T(8,128)(2,1)} %get-tuple-element.61) | copy-start | bytes 3145732
  537.2 24.2 %copy-start.7 = (bf16[128,2048]{1,0:T(8,128)(2,1)S(1)}, bf16[128,2048]{1,0:T(8,128)(2,1)}, u32[]{:S(2)}) copy-start(bf16[128,2048]{1,0:T(8,128)(2,1)} %get-tuple-element.122) | copy-start | bytes 1572868
  541.3 21.7 %copy-start.6 = (f32[64,2048]{1,0:T(8,128)S(1)}, f32[64,2048]{1,0:T(8,128)}, u32[]{:S(2)}) copy-start(f32[64,2048]{1,0:T(8,128)} %get-tuple-element.125) | copy-start | bytes 1572868
  557.0 6.8 %copy-start.3 = (f32[256,2048]{1,0:T(8,128)S(1)}, f32[256,2048]{1,0:T(8,128)}, u32[]{:S(2)}) copy-start(f32[256,2048]{1,0:T(8,128)} %get-tuple-element.127) | copy-start | bytes 6291460

commit v6 on v5

--- a/solution.py
+++ b/solution.py
@@ -3,6 +3,7 @@
 
 import jax
 import jax.numpy as jnp
+import numpy as np
 from jax import lax
 from jax.experimental import pallas as pl
 from jax.experimental.pallas import tpu as pltpu
@@ -889,6 +890,313 @@
 TN = ((0,), (0,))
 
 
+def head_number(h, heads, nz, pos):
+    x, c, z, y = pos
+    return block_of(h // (heads // 2), c, z, h % (heads // 2), nz)
+
+
+def head_kernel(heads, nz, runs_qkv, runs_up, runs_out, *refs):
+    refs = list(refs)
+
+    def take(n):
+        got = refs[:n]
+        del refs[:n]
+        return got
+
+    slopes, valid_in, blocks_in, parents_in = take(4)
+    vectors, bias_up = take(8), take(1)[0]
+    x_in, cot, w_qkv, w_up, w_out, w_down = take(6)
+    joined, mixed, mixed_own, x_own, rows_o, up_bias = take(6)
+    a1_o, far_o, cot_all, qkv_o, up_w, out_w, down_w = take(7)
+    pack, vecs, tab, tab_in, table, columns, member_s, reach_s, far_s, x_all, a1, qkv_w, bias_s = take(13)
+    x_sems, cot_sems, qkv_sems, up_sems, out_sems, down_sems = take(2), take(2), take(4), take(4), take(2), take(2)
+    vec_sems, tab_sems, mix_sems, (local_sem, far_sem) = take(2), take(2), take(2), take(2)
+
+    pos = place()
+    x, c, z, y = pos
+    n = 2 * nz
+    devices = 4 * n
+    me = block_of(x, c, z, y, nz)
+    rank = z * 2 + c
+    tree, cols = joined.shape[0], joined.shape[1] // 3
+    rows, width = x_own.shape
+    part = w_out.shape[0]
+
+    gx = line_gather(x_in, x_all, *x_sems, nz, True, pos)
+    gc = line_gather(cot, cot_all, *cot_sems, nz, True, pos)
+    gq = sliced_gather(w_qkv, qkv_w, runs_qkv, qkv_sems, nz, pos)
+    gu = sliced_gather(w_up, up_w, runs_up, up_sems, nz, pos)
+    go = full_gather(w_out, out_w, *out_sems, nz, pos)
+    gd = group_gather(w_down, down_w, *down_sems, pos)
+    ex = exchange_stages(mixed, mixed_own, runs_out, *mix_sems, nz, pos)
+    ts = trade_stages(tab, tab_in, *tab_sems, pos)
+    store_a = pltpu.make_async_copy(a1, a1_o, local_sem.at[0])
+    store_q = pltpu.make_async_copy(qkv_w, qkv_o, local_sem.at[1])
+
+    def each(fn):
+        def body(k, _):
+            fn((me + k) % devices)
+            return 0
+
+        lax.fori_loop(1, devices, body, 0)
+
+    def vec_copy(other):
+        return remote(pack, vecs.at[me], vec_sems[0].at[other], vec_sems[1].at[me], (other // n, other % n))
+
+    def vec_come(other):
+        remote(vecs.at[other], vecs.at[other], vec_sems[0].at[me], vec_sems[1].at[other], at(x, 1 - c, z, y)).wait_recv()
+
+    pack[...] = jnp.zeros_like(pack)
+    for i, v in enumerate(vectors):
+        pack[i : i + 1, 0:part] = v[...].astype(F32).reshape(1, part)
+    lined = pack[...]
+    pack[...] = jnp.where(y == 1, pltpu.roll(lined, part, 1), lined)
+    for i in range(bias_up.shape[0] // 128):
+        pack[8 + i : 9 + i, :] = bias_up[i * 128 : (i + 1) * 128].astype(F32).reshape(1, 128)
+    tab[...] = jnp.full_like(tab, -1)
+    tab[0:1, :] = valid_in[...]
+    tab[1:2, 0 : blocks_in.shape[1]] = blocks_in[...]
+    tab[2:3, 0 : parents_in.shape[1]] = parents_in[...]
+
+    greet_all(devices, n, me)
+    gx[0]()
+    gq[0]()
+    ts[0]()
+    go[0]()
+    gd[0]()
+    each(lambda other: vec_copy(other).start())
+    vecs[me] = pack[...]
+    gx[1]()
+
+    ts[1]()
+    seg = lax.broadcasted_iota(jnp.int32, (128, 128), 0)
+    lane = lax.broadcasted_iota(jnp.int32, (128, 128), 1)
+
+    def low(v):
+        return v.astype(F32).astype(BF)
+
+    parent = low(seg == tab_in[2:3, 0:128])
+    above = (parent.astype(F32) + dot(parent, parent, NN)) > 0.5
+    ancestor = low(above & (seg != lane))
+    owner = low(seg == tab_in[1:2, 0:128])
+    spread = low(
+        lax.shift_right_logical(lax.broadcasted_iota(jnp.int32, (128, tree), 1), BLK.bit_length() - 1)
+        == lax.broadcasted_iota(jnp.int32, (128, tree), 0)
+    )
+    member = dot(owner, spread, NN)
+    valid = tab_in[0:1, :].astype(F32)
+    counted = member * valid
+    member_s[...] = member.astype(BF)
+    reach_s[...] = (2.0 * dot(ancestor, member_s[...], NN) + member).astype(BF)
+    lens = jnp.broadcast_to(jnp.sum(counted, axis=1, keepdims=True), (128, 128))
+    offset = lax.dot_general(
+        ancestor.astype(F32), lens, (TN, ((), ())), precision=lax.Precision.HIGHEST, preferred_element_type=F32
+    )
+    table[...] = jnp.zeros_like(table)
+    table[1:2, :] = valid
+    for j in range(tree // 256):
+        here = slice(j * 256, (j + 1) * 256)
+        earlier = low(
+            lax.broadcasted_iota(jnp.int32, (tree, 256), 0) < lax.broadcasted_iota(jnp.int32, (tree, 256), 1) + j * 256
+        )
+        before = dot(counted.astype(BF), earlier, NN) + offset[:, 0:1]
+        table[0:1, here] = jnp.sum(before * member[:, here], axis=0, keepdims=True)
+    columns[...] = table[...].T
+
+    step = far_s.shape[2]
+    steps = tree // step
+    far_store = [
+        pltpu.make_async_copy(far_s.at[i % 2], far_o.at[:, pl.ds(i * step, step)], far_sem.at[i % 2]) for i in range(steps)
+    ]
+
+    def allow(value, key, query, key_valid):
+        return ((value > 1.5) | ((value > 0.5) & (key <= query))) & ((key_valid > 0.5) | (key == query))
+
+    def far_blocks():
+        for i in range(steps):
+            here = slice(i * step, (i + 1) * step)
+            key = lax.broadcasted_iota(jnp.int32, (tree, step), 0)
+            query = lax.broadcasted_iota(jnp.int32, (tree, step), 1) + i * step
+            allowed = allow(dot(member_s[...], reach_s[:, here], TN), key, query, columns[:, 1:2])
+            if i >= 2:
+                far_store[i - 2].wait()
+            far_s[i % 2] = jnp.where(allowed, columns[:, 0:1], MASKED)
+            far_store[i].start()
+
+    def whole_vectors():
+        each(vec_come)
+        for i in range(devices // 2):
+            rows_o[:, i * 128 : (i + 1) * 128] = vecs[2 * i, 0:8] + vecs[2 * i + 1, 0:8]
+        per = bias_up.shape[0] // 128
+        for g in range(4):
+            r = block_of(g // 2, c, z, g % 2, nz)
+            for i in range(per):
+                up_bias[:, (g * per + i) * 128 : (g * per + i + 1) * 128] = vecs[r, 8 + i : 9 + i]
+        bias_s[...] = jnp.zeros_like(bias_s)
+        for there, here, size in runs_out(rank):
+            there = pl.multiple_of(there, 128)
+            bias_s[:, here : here + size] = rows_o[2:3, pl.ds(there, size)]
+            bias_s[:, 2 * cols + here : 2 * cols + here + size] = rows_o[3:4, pl.ds(there, size)]
+
+    def norm(b):
+        def tile(j, _):
+            here = pl.ds(pl.multiple_of(j * 32, 32), 32)
+            normed, _ = norm_parts(x_all[b, here].astype(F32))
+            a1[b, here] = (normed * rows_o[0:1, :] + rows_o[1:2, :]).astype(BF)
+            return 0
+
+        lax.fori_loop(0, rows // 32, tile, 0)
+
+    def norm_at(k, core):
+        pl.when(z >= k)(lambda: norm((z - k) * 2 + core))
+        if k:
+            pl.when(z + k < nz)(lambda: norm((z + k) * 2 + core))
+
+    for stage in gq[1 : n + 1]:
+        stage()
+    gx[2]()
+    go[1]()
+    gd[1]()
+    far_blocks()
+    whole_vectors()
+    norm_at(0, c)
+    norm_at(1, c)
+    gx[3]()
+    gu[0]()
+    gc[0]()
+    norm_at(2, c)
+    go[2]()
+    for stage in gq[n + 1 : 2 * n + 1]:
+        stage()
+    gx[4]()
+    gc[1]()
+    norm_at(3, c)
+    go[3]()
+    gx[-1]()
+    x_own[...] = x_all[rank]
+    for k in range(nz):
+        norm_at(k, 1 - c)
+    store_a.start()
+    gq[-1]()
+    store_q.start()
+    for stage in gu[1 : n + 1]:
+        stage()
+
+    def project(i, _):
+        here = pl.ds(pl.multiple_of(i * 2 * rows, 2 * rows), 2 * rows)
+        tokens = a1[pl.ds(2 * i, 2)].reshape(2 * rows, width)
+
+        def tile(j, _):
+            u = pl.ds(pl.multiple_of(j * 256, 256), 256)
+            value = dot(tokens, qkv_w[:, :, u].reshape(width, 256), NN) + bias_s[:, u]
+            joined[here, u] = value.astype(BF)
+            return 0
+
+        lax.fori_loop(0, 3 * cols // 256, tile, 0)
+        return 0
+
+    lax.fori_loop(0, nz, project, 0)
+    slope = [slopes[head_number(h, heads, nz, pos)] for h in range(heads)]
+
+    gc[2]()
+    def attend_step(i, _):
+        here = pl.ds(pl.multiple_of(i * step, step), step)
+        per = step // rows
+        key = lax.broadcasted_iota(jnp.int32, (step, tree), 1)
+        query = lax.broadcasted_iota(jnp.int32, (step, tree), 0) + i * step
+        allowed = allow(dot(reach_s[:, here], member_s[...], TN), key, query, table[1:2, :])
+        gap = jnp.where(allowed, table[0:1, :], MASKED)
+        for h in range(heads):
+            lanes = slice(h * HD, (h + 1) * HD)
+            q = joined[here, lanes]
+            k = joined[:, cols + h * HD : cols + (h + 1) * HD]
+            v = joined[:, 2 * cols + h * HD : 2 * cols + (h + 1) * HD]
+            logits = dot(q, k, NT) * HD ** (-0.5) + slope[h] * gap
+            weights = jnp.exp(logits - jnp.max(logits, axis=1, keepdims=True))
+            probs = weights * (1.0 / jnp.sum(weights, axis=1, keepdims=True))
+            mixed[pl.ds(i * per, per), :, lanes] = dot(probs.astype(BF), v, NN).astype(BF).reshape(per, rows, HD)
+
+        def later(k, fns):
+            @pl.when(i == k)
+            def _():
+                for fn in fns:
+                    fn()
+
+        later(0, go[nz : 2 * nz])
+        later(1, gc[3:4] + gu[n + 1 : n + 1 + n // 2])
+        later(2, gc[4:5] + gu[n + 1 + n // 2 : 2 * n + 1])
+        later(3, go[2 * nz : 3 * nz])
+        return 0
+
+    lax.fori_loop(0, steps, attend_step, 0)
+    ex[0]()
+    ex[1]()
+    for stage in (go[-1], gc[-1], gu[-1], gd[-1]):
+        stage()
+    each(lambda other: vec_copy(other).wait_send())
+    for i in range(max(0, steps - 2), steps):
+        far_store[i].wait()
+    store_a.wait()
+    store_q.wait()
+
+
+def head_call(slopes, tables, vectors, bias_up, layer_in, cot, w_qkv, w_up, w_out, w_down, heads, nz, cid):
+    rows, width = layer_in.shape
+    n = 2 * nz
+    devices = 4 * n
+    tree = n * rows
+    cols = heads * HD
+    part, unit = w_out.shape[0], w_down.shape[0]
+    step = 256
+    runs_qkv, runs_up, runs_out = qkv_runs(nz, width, cols), up_runs(nz, unit), head_runs(nz, cols)
+    shape = jax.ShapeDtypeStruct
+    return pl.pallas_call(
+        functools.partial(head_kernel, heads, nz, runs_qkv, runs_up, runs_out),
+        out_shape=[
+            shape((tree, 3 * cols), BF),
+            shape((n, rows, cols), BF),
+            shape((rows, width), BF),
+            shape((rows, width), BF),
+            shape((8, width), F32),
+            shape((1, 4 * unit), F32),
+            shape((n, rows, width), BF),
+            shape((tree, tree), F32),
+            shape((n, rows, width), BF),
+            shape((devices, part, 3 * cols), BF),
+            shape((devices, part, 4 * unit), BF),
+            shape((devices, part, width), BF),
+            shape((4, unit, width), BF),
+        ],
+        in_specs=[pl.BlockSpec(memory_space=pltpu.SMEM)] + [VM] * 12 + [HBM] * 6,
+        out_specs=[VM] * 6 + [HBM] * 7,
+        scratch_shapes=[
+            pltpu.VMEM((16, 128), F32),
+            pltpu.VMEM((devices, 16, 128), F32),
+            pltpu.VMEM((8, tree), jnp.int32),
+            pltpu.VMEM((8, tree), jnp.int32),
+            pltpu.VMEM((128, tree), F32),
+            pltpu.VMEM((tree, 128), F32),
+            pltpu.VMEM((128, tree), BF),
+            pltpu.VMEM((128, tree), BF),
+            pltpu.VMEM((2, tree, step), F32),
+            pltpu.VMEM((n, rows, width), BF),
+            pltpu.VMEM((n, rows, width), BF),
+            pltpu.VMEM((devices, part, 3 * cols), BF),
+            pltpu.VMEM((1, 3 * cols), F32),
+        ]
+        + gather_sems(nz) * 2
+        + sliced_sems(nz) * 2
+        + full_sems(nz)
+        + [pltpu.SemaphoreType.DMA((5,))] * 2
+        + [pltpu.SemaphoreType.DMA((devices,))] * 2
+        + trade_sems()
+        + exchange_sems(runs_out, nz)
+        + [pltpu.SemaphoreType.DMA((2,))] * 2,
+        compiler_params=params(cid, 60 * MIB),
+        name="head",
+    )(slopes, *tables, *vectors, bias_up, layer_in, cot, w_qkv, w_up, w_out, w_down)
+
+
 def scatter_parts(nz, pos, own, other, acc, came, send, recv):
     x, c, z, y = pos
     S, U, D = 0, nz, 2 * nz
@@ -924,14 +1232,21 @@
 
         (rise if upward else fall)(t).start()
 
-    def events(s):
-        for t in range(nz):
-            zz = s - t
-            if 0 <= zz < t:
-                pl.when(z == zz)(functools.partial(event, t, True))
-            zz = 2 * (nz - 1) - s - t
-            if t < zz < nz:
-                pl.when(z == zz)(functools.partial(event, t, False))
+    def begin():
+        for i in range(nz - 1):
+            pl.when(z == 0)(functools.partial(event, nz - 1 - i, True))
+            pl.when(z == nz - 1)(functools.partial(event, i, False))
+
+    def near(i):
+        t = nz - 1 - i
+        pl.when((z > 0) & (z < nz // 2) & (z < t))(functools.partial(event, t, True))
+        pl.when((z >= nz // 2) & (z < nz - 1) & (z > i))(functools.partial(event, i, False))
+
+    def far():
+        for i in range(nz - 1):
+            t = nz - 1 - i
+            pl.when((z >= nz // 2) & (z < t))(functools.partial(event, t, True))
+            pl.when((z < nz // 2) & (z > i))(functools.partial(event, i, False))
 
     def total(out):
         swap(z).wait_recv()
@@ -953,7 +1268,7 @@
             pl.when(z < t)(lambda t=t: rise(t).wait_send())
             pl.when(z > t)(lambda t=t: fall(t).wait_send())
 
-    return swap, events, total, done
+    return swap, begin, near, far, total, done
 
 
 def reduce_parts(src, mine, near, far, send, recv, lsem, pos):
@@ -1057,10 +1372,10 @@
     down1, down2, down_total, down_done = reduce_parts(down_src, *down_refs, pos)
     qkv1, qkv2, qkv_total, qkv_done = reduce_parts(qkv_g, *qkv_refs, pos)
     out1, out2, out_total, out_done = reduce_parts(out_g, *out_refs, pos)
-    upd_swap, upd_events, upd_total, upd_done = scatter_parts(
+    upd_swap, upd_begin, upd_near, upd_far, upd_total, upd_done = scatter_parts(
         nz, pos, lambda t: upd_own[t], lambda t: upd_in.at[t * 2 + 1 - c], upd_acc, upd_came, upd_send, upd_recv
     )
-    att_swap, att_events, att_total, att_done = scatter_parts(
+    att_swap, att_begin, att_near, att_far, att_total, att_done = scatter_parts(
         nz, pos, lambda t: att_p[t * 2 + c], lambda t: att_p.at[t * 2 + 1 - c], att_acc, att_came, att_send, att_recv
     )
     ex_up = exchange_stages(up_sum, up_o, runs_up, *esems_up, nz, pos)
@@ -1079,9 +1394,7 @@
     greet(rank_partners(nz, pos) + group_partners(pos) + [(c != y, at(x, y, z, c))])
     es[0]()
     up1()
-    gb[0]()
-    gb[1]()
-    for t in list(range(nz - 1, 0, -1)) + [0]:
+    for t in range(nz):
         upd_swap(t).start()
     gap_load(0, 0).start()
     for copy in loads + [load_w, load_a]:
@@ -1091,8 +1404,12 @@
     for copy in loads:
         copy.wait()
     es[1]()
+    gb[0]()
+    gb[1]()
+    upd_begin()
 
     steps = tree // step
+    slope = [slopes[head_number(h, heads, nz, pos)] for h in range(heads)]
 
     def attend_step(i, _):
         slot = i % 2
@@ -1108,7 +1425,7 @@
             k = joined[:, cols + h * HD : cols + (h + 1) * HD]
             v = joined[:, 2 * cols + h * HD : 2 * cols + (h + 1) * HD]
             g = grads[:, lane]
-            logits = dot(k, q, NT) * HD ** (-0.5) + slopes[h] * gap
+            logits = dot(k, q, NT) * HD ** (-0.5) + slope[h] * gap
             weights = jnp.exp(logits - jnp.max(logits, axis=0, keepdims=True))
             probs = weights * (1.0 / jnp.sum(weights, axis=0, keepdims=True))
             grad_probs = dot(v, g, NT)
@@ -1124,10 +1441,10 @@
                 for fn in fns:
                     fn()
 
-        later(0, [down1, lambda: upd_events(0)])
-        later(1, [gb[2], lambda: upd_events(1)])
-        later(2, [up2] + gb[3:4] + [lambda: upd_events(2)])
-        later(3, gb[4:5] + [lambda: upd_events(3)])
+        later(0, [down1])
+        later(1, [gb[2], lambda: upd_near(0)])
+        later(2, [up2, gb[3], lambda: upd_near(1)])
+        later(3, [gb[4], upd_far])
         return 0
 
     lax.fori_loop(0, steps, attend_step, 0)
@@ -1162,12 +1479,28 @@
             qkv_g[d // 2 * 2 + f % 2, pl.ds(pl.multiple_of(p * part, part), part), :] = value[i * part : (i + 1) * part]
         return 0
 
-    att_events(0)
+    att_begin()
     lax.fori_loop(0, width // 256, qkv_tile, 0)
     qkv1()
-    upd_events(4)
-    att_events(1)
     down2()
+    att_near(0)
+
+    def put_ranks(dest):
+        def put(lower, value):
+            dest[pl.ds(lower * nz, nz)] = value.astype(BF).reshape(nz, part, -1)
+
+        return put
+
+    up_total(put_ranks(up_sum))
+    ex_up[0]()
+    att_near(1)
+    qkv2()
+    att_far()
+    upd_total(res)
+    res[...] += base[...]
+    res_low[...] = res[...].astype(BF)
+    home[0]()
+    square_o[...] = jnp.sum(res[...] * res[...], axis=0, keepdims=True)
     for stage in gb[5:]:
         stage()
     load_b.start()
@@ -1181,26 +1514,9 @@
 
     lax.fori_loop(0, width // 512, out_tile, 0)
     out1()
-    upd_events(5)
-    att_events(2)
-
-    def put_ranks(dest):
-        def put(lower, value):
-            dest[pl.ds(lower * nz, nz)] = value.astype(BF).reshape(nz, part, -1)
-
-        return put
-
-    up_total(put_ranks(up_sum))
-    ex_up[0]()
-    upd_events(6)
-    upd_total(res)
-    res[...] += base[...]
-    res_low[...] = res[...].astype(BF)
-    home[0]()
-    square_o[...] = jnp.sum(res[...] * res[...], axis=0, keepdims=True)
-    att_events(3)
-    qkv2()
-    att_events(4)
+    qkv_total(put_ranks(qkv_sum))
+    ex_qkv[0]()
+    att_total(grad_out)
     out2()
 
     def put_down(lower, value):
@@ -1208,18 +1524,12 @@
         down_o[pl.ds(lower * half, half), :] = value
 
     down_total(put_down)
-    att_events(5)
-    att_events(6)
-    att_total(grad_out)
-    ex_up[1]()
-
     def put_out(lower, value):
         half = value.shape[0]
         out_o[pl.ds(lower * half, half), :] = value
 
     out_total(put_out)
-    qkv_total(put_ranks(qkv_sum))
-    ex_qkv[0]()
+    ex_up[1]()
     home[1]()
     ex_qkv[1]()
     for fn in (up_done, down_done, qkv_done, out_done, upd_done, att_done):
@@ -1790,7 +2100,7 @@
     return jnp.pad(flat, [(0, 0)] * (flat.ndim - 1) + [(0, -flat.shape[-1] % lanes)])
 
 
-def per_device(
+def by_steps(
     layer_in,
     cotangent,
     w_qkv,
@@ -1899,25 +2209,18 @@
     normed_two, inverse_two = norm_parts(middle)
     mlp_own = (normed_two * gain_two + shift_two).astype(BF)
     cot_blocks = cot.reshape(fsdp, rows, width)
-    fused = aligned and nz == 4 and mlp_bytes(nz, rows, width, 4 * unit) < 50 * MIB
-    if fused:
-        grad_mlp_in, update, up_g, down_g, grad_bias_up = mlp_call(
-            mlp_own, cot_blocks, up_w, down_w, up_bias[None], nz, 3
-        )
-        grad_bias_up = grad_bias_up[0]
-    else:
-        mlp_in = gather_tokens(mlp_own, nz, 3).reshape(tree, width)
-        hidden = jnp.dot(mlp_in, up_w, preferred_element_type=F32) + up_bias
-        active_float, gelu_pull = jax.vjp(gelu_exact, hidden)
-        active = active_float.astype(BF)
-        grad_active = mm("td,fd->tf", cot, down_w)
-        grad_hidden = gelu_pull(grad_active)[0].astype(BF)
-        grad_mlp_in = mm("tf,df->td", grad_hidden, up_w).astype(BF).reshape(fsdp, rows, width)
-        grad_mlp_in = scatter_tokens(grad_mlp_in, nz, 4)
-        update = jnp.dot(active, down_w, preferred_element_type=F32).astype(BF).reshape(fsdp, rows, width)
-        down_g = mm("tf,td->fd", active, cot).astype(BF)
-        up_g = mm("td,tf->df", mlp_in, grad_hidden).astype(BF)
-        grad_bias_up = jnp.sum(grad_hidden.astype(F32), axis=0)
+    mlp_in = gather_tokens(mlp_own, nz, 3).reshape(tree, width)
+    hidden = jnp.dot(mlp_in, up_w, preferred_element_type=F32) + up_bias
+    active_float, gelu_pull = jax.vjp(gelu_exact, hidden)
+    active = active_float.astype(BF)
+    grad_active = mm("td,fd->tf", cot, down_w)
+    grad_hidden = gelu_pull(grad_active)[0].astype(BF)
+    grad_mlp_in = mm("tf,df->td", grad_hidden, up_w).astype(BF).reshape(fsdp, rows, width)
+    grad_mlp_in = scatter_tokens(grad_mlp_in, nz, 4)
+    update = jnp.dot(active, down_w, preferred_element_type=F32).astype(BF).reshape(fsdp, rows, width)
+    down_g = mm("tf,td->fd", active, cot).astype(BF)
+    up_g = mm("td,tf->df", mlp_in, grad_hidden).astype(BF)
+    grad_bias_up = jnp.sum(grad_hidden.astype(F32), axis=0)
     down_g = down_g.reshape(4, unit, width)
     cot_own = own_rows(cot).astype(F32)
     grad_middle = cot_own + norm_back(grad_mlp_in * gain_two, normed_two, inverse_two)
@@ -1931,46 +2234,37 @@
         grad_mixed = grad_mixed.reshape(rows, 2, 2, nz, 2 * HD).transpose(3, 2, 0, 1, 4).reshape(fsdp, rows, cols)
     else:
         grad_mixed = grad_mixed.reshape(rows, fsdp, cols).transpose(1, 0, 2)
-    if fused:
-        runs = up_runs(nz, unit), qkv_runs(nz, width, cols)
-        grad_attn_in, grad_down_w, grad_out_w, col, square, grad_up_w, grad_qkv_w, _, layer_out = tail_call(
-            slopes, far.T, grad_mixed, joined, attn_in.reshape(fsdp, rows, width), mixed, qkv_w, grad_branch,
-            update, up_g, down_g, middle + down_bias, runs, heads, nz, 6,
-        )
-        col, square = col[0], jnp.sum(square)
-    else:
-        up_g = up_g.reshape(devices, part, 4 * unit)
-        grad_heads = exchange(grad_mixed, nz, 5, "grad_to_heads")
-        grad_heads = grad_heads.reshape(tree, cols)
-        grad_q, grad_k, grad_v, branch_all, update, down_c, up_c = attend_back(
-            slopes, far.T, joined, grad_heads, grad_branch, update, [down_g, up_g], (False, True), heads, nz, 6
-        )
-        result = middle + update + down_bias
-        grad_joined = jnp.concatenate([grad_q, grad_k, grad_v], axis=1)
-
-        def mine(g, came):
-            g = g.reshape((2, 2, nz, 2) + g.shape[1:])
-            g = lax.dynamic_slice(g, (x, 0, 0, y, 0, 0), (1, 2, nz, 1) + g.shape[4:])
-            g = g.reshape((2, nz) + g.shape[4:]).swapaxes(0, 1)
-            return (g.reshape(came.shape[1:]).astype(F32) + jnp.sum(came.astype(F32), axis=0)).astype(BF)
-
-        def mine_flat(g, came):
-            return lax.dynamic_index_in_dim(g, x * 2 + y, 0, keepdims=False).astype(F32) + jnp.sum(came.astype(F32), axis=0)
-
-        grad_down_w = mine_flat(down_g, down_c)
-        qkv_g = mm("td,te->de", attn_in, grad_joined).astype(BF).reshape(devices, part, 3 * cols)
-        flat = []
-        if aligned:
-            flat = [mm("td,te->de", mixed, branch_all.reshape(tree, width)).astype(BF).reshape(4, part, width)]
-        kinds = (True,) + (False,) * len(flat)
-        grad_attn_in = mm("te,de->td", grad_joined, qkv_w).astype(BF).reshape(fsdp, rows, width)
-        grad_attn_in, grad_up_w, layer_out, qkv_c, *out_c = scatter_and_hand(
-            grad_attn_in, mine(up_g, up_c), up_runs(nz, unit), result.astype(BF), [qkv_g] + flat, kinds, nz, 10
-        )
-        grad_up_w = grad_up_w.astype(F32)
-        if aligned:
-            grad_out_w = mine_flat(flat[0], out_c[0])
-        col, square = jnp.sum(grad_joined.astype(F32), axis=0), jnp.sum(result * result)
+    up_g = up_g.reshape(devices, part, 4 * unit)
+    grad_heads = exchange(grad_mixed, nz, 5, "grad_to_heads")
+    grad_heads = grad_heads.reshape(tree, cols)
+    grad_q, grad_k, grad_v, branch_all, update, down_c, up_c = attend_back(
+        slopes, far.T, joined, grad_heads, grad_branch, update, [down_g, up_g], (False, True), heads, nz, 6
+    )
+    result = middle + update + down_bias
+    grad_joined = jnp.concatenate([grad_q, grad_k, grad_v], axis=1)
+
+    def mine(g, came):
+        g = g.reshape((2, 2, nz, 2) + g.shape[1:])
+        g = lax.dynamic_slice(g, (x, 0, 0, y, 0, 0), (1, 2, nz, 1) + g.shape[4:])
+        g = g.reshape((2, nz) + g.shape[4:]).swapaxes(0, 1)
+        return (g.reshape(came.shape[1:]).astype(F32) + jnp.sum(came.astype(F32), axis=0)).astype(BF)
+
+    def mine_flat(g, came):
+        return lax.dynamic_index_in_dim(g, x * 2 + y, 0, keepdims=False).astype(F32) + jnp.sum(came.astype(F32), axis=0)
+
+    grad_down_w = mine_flat(down_g, down_c)
+    qkv_g = mm("td,te->de", attn_in, grad_joined).astype(BF).reshape(devices, part, 3 * cols)
+    flat = []
+    if aligned:
+        flat = [mm("td,te->de", mixed, branch_all.reshape(tree, width)).astype(BF).reshape(4, part, width)]
+    kinds = (True,) + (False,) * len(flat)
+    grad_attn_in = mm("te,de->td", grad_joined, qkv_w).astype(BF).reshape(fsdp, rows, width)
+    grad_attn_in, grad_up_w, layer_out, qkv_c, *out_c = scatter_and_hand(
+        grad_attn_in, mine(up_g, up_c), up_runs(nz, unit), result.astype(BF), [qkv_g] + flat, kinds, nz, 10
+    )
+    if aligned:
+        grad_out_w = mine_flat(flat[0], out_c[0])
+    col, square = jnp.sum(grad_joined.astype(F32), axis=0), jnp.sum(result * result)
     grad_up_w = grad_up_w.astype(F32)
     grad_inputs = grad_middle + norm_back(grad_attn_in * gain_one, normed_one, inverse_one)
 
@@ -1993,11 +2287,8 @@
         axis=1,
     )
     packed = padded(packed, 1024).reshape(devices, -1, 128)
-    if fused:
-        grad_x, packed = finish(grad_inputs.astype(BF), packed, None, None, nz, 8)
-    else:
-        runs = qkv_runs(nz, width, cols) if aligned else None
-        grad_x, packed, grad_qkv_w = finish(grad_inputs.astype(BF), packed, mine(qkv_g, qkv_c), runs, nz, 8)
+    runs = qkv_runs(nz, width, cols) if aligned else None
+    grad_x, packed, grad_qkv_w = finish(grad_inputs.astype(BF), packed, mine(qkv_g, qkv_c), runs, nz, 8)
     if not aligned:
         grad_qkv_w = grad_qkv_w.reshape(fsdp, part, 3, cols).transpose(1, 2, 0, 3).reshape(part, -1)
     grad_qkv_w = grad_qkv_w.astype(F32)
@@ -2025,6 +2316,131 @@
     )
 
 
+def by_kernels(
+    layer_in,
+    cotangent,
+    w_qkv,
+    w_out,
+    w_up,
+    w_down,
+    gain_attn,
+    shift_attn,
+    bias_query,
+    bias_value,
+    bias_out,
+    gain_mlp,
+    shift_mlp,
+    bias_up,
+    bias_down,
+    parents,
+    seg_blocks,
+    token_valid,
+):
+    rows, width = layer_in.shape
+    fsdp = lax.axis_size("fsdp")
+    nz = fsdp // 2
+    devices = 4 * fsdp
+    x, c, z, y = place()
+    rank = z * 2 + c
+    heads = H // fsdp
+    cols = heads * HD
+    tree = token_valid.shape[1]
+    part = w_up.shape[0]
+    unit = w_down.shape[0]
+
+    slopes = jnp.asarray(np.exp2(-8.0 * (np.arange(H) + 1.0) / H).astype(np.float32))
+    vectors = (gain_attn, shift_attn, bias_query, bias_value, bias_out, gain_mlp, shift_mlp, bias_down)
+    joined, mixed, mixed_own, own, whole, up_bias, attn_in, far, cot, qkv_w, up_w, out_w, down_w = head_call(
+        slopes, (token_valid, seg_blocks, parents), vectors, bias_up, layer_in, cotangent, w_qkv, w_up, w_out, w_down,
+        heads, nz, 1,
+    )
+    qkv_w = qkv_w.reshape(width, 3 * cols)
+    up_w = up_w.reshape(width, 4 * unit)
+    out_w = out_w.reshape(width, width)
+    down_w = down_w.reshape(4 * unit, width)
+    gain_one, out_bias, gain_two, shift_two, down_bias = [whole[i] for i in (0, 4, 5, 6, 7)]
+
+    inputs = own.astype(F32)
+    normed_one, inverse_one = norm_parts(inputs)
+    branch = jnp.dot(mixed_own, out_w, preferred_element_type=F32) + out_bias
+    middle = inputs + branch
+    normed_two, inverse_two = norm_parts(middle)
+    mlp_own = (normed_two * gain_two + shift_two).astype(BF)
+    grad_mlp_in, update, up_g, down_g, grad_bias_up = mlp_call(mlp_own, cot, up_w, down_w, up_bias, nz, 3)
+    down_g = down_g.reshape(4, unit, width)
+
+    cot_own = lax.dynamic_index_in_dim(cot, rank, 0, keepdims=False).astype(F32)
+    grad_middle = cot_own + norm_back(grad_mlp_in * gain_two, normed_two, inverse_two)
+    grad_branch = grad_middle.astype(BF)
+    grad_mixed = mm("te,de->td", grad_branch, out_w).astype(BF)
+    grad_mixed = grad_mixed.reshape(rows, 2, 2, nz, 2 * HD).transpose(3, 2, 0, 1, 4).reshape(fsdp, rows, cols)
+    runs = up_runs(nz, unit), qkv_runs(nz, width, cols)
+    grad_attn_in, grad_down_w, grad_out_w, col, square, grad_up_w, grad_qkv_w, _, layer_out = tail_call(
+        slopes, far, grad_mixed, joined, attn_in, mixed.reshape(tree, cols), qkv_w, grad_branch,
+        update, up_g, down_g, middle + down_bias, runs, heads, nz, 6,
+    )
+    grad_inputs = grad_middle + norm_back(grad_attn_in * gain_one, normed_one, inverse_one)
+
+    def spread(v):
+        v = v.reshape(2, 1, 1, 2, HD)
+        return lax.dynamic_update_slice(jnp.zeros((2, 2, nz, 2, HD), F32), v, (0, c, z, 0, 0))
+
+    smalls = [
+        jnp.sum(grad_attn_in * normed_one, axis=0),
+        jnp.sum(grad_attn_in, axis=0),
+        spread(col[0, :cols]),
+        spread(col[0, 2 * cols :]),
+        jnp.sum(grad_branch.astype(F32), axis=0),
+        jnp.sum(grad_mlp_in * normed_two, axis=0),
+        jnp.sum(grad_mlp_in, axis=0),
+        jnp.sum(cot_own, axis=0),
+    ]
+    grad_bias_up = grad_bias_up.reshape(2, 1, 1, 2, unit)
+    grad_bias_up = lax.dynamic_update_slice(jnp.zeros((2, 2, nz, 2, unit), F32), grad_bias_up, (0, c, z, 0, 0))
+    squares = jnp.stack([jnp.sum(square), jnp.sum(branch * branch)])
+    packed = jnp.concatenate(
+        [v.reshape(devices, part) for v in smalls]
+        + [grad_bias_up.reshape(devices, unit), jnp.broadcast_to(squares, (devices, 2))],
+        axis=1,
+    )
+    packed = padded(packed, 1024).reshape(devices, -1, 128)
+    grad_x, packed = finish(grad_inputs.astype(BF), packed, None, None, nz, 8)
+    packed = packed.reshape(-1)
+    small = [packed[i * part : (i + 1) * part] for i in range(8)]
+    up_at = 8 * part
+    root_squares = jnp.sqrt(packed[up_at + unit : up_at + unit + 2] / (devices * rows * width))
+    return (
+        layer_out,
+        grad_x,
+        grad_qkv_w.astype(F32),
+        grad_out_w,
+        grad_up_w.astype(F32),
+        grad_down_w,
+        small[0],
+        small[1],
+        small[2],
+        small[3],
+        small[4],
+        small[5],
+        small[6],
+        packed[up_at : up_at + unit],
+        small[7],
+        root_squares,
+    )
+
+
+def per_device(*args):
+    layer_in, w_down, token_valid = args[0], args[5], args[17]
+    fsdp = lax.axis_size("fsdp")
+    rows, width = layer_in.shape
+    unit = w_down.shape[0]
+    fits = mlp_bytes(fsdp // 2, rows, width, 4 * unit) < 50 * MIB
+    whole_heads = args[2].shape[0] == HD and H // fsdp == 4 and width == H * HD
+    if fsdp == 8 and fits and whole_heads and unit % 128 == 0 and token_valid.shape[1] % 256 == 0 and rows == 128:
+        return by_kernels(*args)
+    return by_steps(*args)
+
+
 def solution(mesh):
     matrix, vector, table = P(BOTH, None), P(BOTH), P("dp", None)
     return jax.shard_map(

time: 574 us -> 467 us (0.81)
  Pallas kernels: 484 us -> 418 us
  other arithmetic: 35.9 us -> 18.8 us
  local copies, waits for them, and re-layouts: 24 us -> 10.6 us
  matrix products: 20.5 us -> 12.9 us
    pallas_call x3 -> x1, Pallas kernels: 203 us -> 159 us  [head_call(): pl.pallas_call(functools.partial(head_kernel, heads, nz, runs_qkv, runs_u...]
    pallas_call x1, Pallas kernels: 171 us -> 147 us  [tail_call(): pl.pallas_call(functools.partial(tail_kernel, heads, nz, runs_up, runs_qk...]
    dot_general x3 -> x1, matrix products: 14.1 us -> 6.58 us  [by_kernels(): branch = jnp.dot(mixed_own, out_w, preferred_element_type=F32) + out_bias]
    concatenate x3 -> x1, local copies, waits for them, and re-layouts: 6.93 us -> 0.09 us  [by_kernels(): jnp.concatenate([v.reshape(devices, part) for v in smalls] + [grad_bias_u...]
    select_n x1 -> x0, other arithmetic: 6.25 us -> none  [per_device(): jnp.where(mask, (position[None, :] - position[:, None]).astype(F32), MASKED)]
where the time goes in v6:
time: 467 us; the launch traced here: 461 us
  Pallas kernels  418 us (90%)
  other arithmetic  18.8 us (4%)
  matrix products  12.9 us (3%)
  local copies, waits for them, and re-layouts  10.6 us (2%)
    pallas_call x1, Pallas kernels, head_call(): pl.pallas_call(functools.partial(head_kernel, heads, nz, runs_qkv, runs_u...  159 us
    pallas_call x1, Pallas kernels, tail_call(): pl.pallas_call(functools.partial(tail_kernel, heads, nz, runs_up, runs_qk...  147 us
    pallas_call x1, Pallas kernels, mlp_call(): pl.pallas_call(functools.partial(mlp_kernel, nz), out_shape=[shape((rows,...  94.9 us
    pallas_call x1, Pallas kernels, finish(): pl.pallas_call(functools.partial(finish_kernel, nz, runs, has), out_shape...  16.8 us

profile of v6, /device:TPU:0, one launch (start us, length us, event | category | flops | bytes accessed | tf_op | source)
XLA Modules:
  0.0 461.5 jit_solution(16834299460312946485)
XLA Ops:
  0.7 159.3 %head.1 = (bf16[1024,768]{1,0:T(8,128)(2,1)}, bf16[8,128,256]{2,1,0:T(8,128)(2,1)}, bf16[128,2048]{1,0:T(8,128)(2,1)}, bf16[128,2048]{1,0:T(8,128)(2,1)}, f32[8,...) custom-call(f32[32]{0:T(128)} %constant.62.clone.refs_0_.slopes, ...), custom_call_target="tpu_custom_call" | custom-call | tf_op jit(solution)/shard_map/head/pallas_call | solution.py:1153
  160.0 1.2 convert_reduce_fusion
  161.2 1.1 fusion.14
  162.2 6.6 %broadcast_add_fusion = (f32[128,2048]{1,0:T(8,128)}, f32[128,2048]{1,0:T(8,128)S(1)}, f32[]{:T(128)}, f32[128]{0:T(128)S(1)}) fusion(f32[2048]{0:T(1024)S(1)} %bitcast.58, bf16[128,2048]{1,0:T(8,128)(2,1)} %get-tuple-element.46, f32[128]{0:T(128)S(1)} %broadcast_multiply_fusion.2, f32[2048]{0:T(1024)S(1)} %bitcast.59, ...), kind=kOutput, calls=%fused_computation.30 | convolution fusion | flops 1076100992 | bytes 11551748 | tf_op jit(solution)/shard_map/dot_general | solution.py:2365
  168.8 0.1 reduce_sum.144
  168.9 0.3 multiply_reduce_fusion.3
  169.2 1.1 add_convert_fusion.own
  170.3 94.9 %mlp.1 = (f32[128,2048]{1,0:T(8,128)}, bf16[8,128,2048]{2,1,0:T(8,128)(2,1)}, bf16[4,512,1024]{2,1,0:T(8,128)(2,1)}, bf16[1024,2048]{1,0:T(8,128)(2,1)}, f32[1,1024]{1,0:T(1,128)}) custom-call(bf16[128,2048]{1,0:T(8,128)(2,1)} %add_convert_fusion.own, bf16[8,128,2048]{2,1,0:T(8,128)(2,1)} %get-tuple-element.45.cot_in, bf16[2048,1024]{1,0:T(8,128)(2,1)} %bitcast.44, ...), custom_call_target="tpu_custom_call" | custom-call | tf_op jit(solution)/shard_map/mlp/pallas_call | solution.py:1845
  265.2 1.7 multiply_reduce_fusion.1
  266.9 2.9 convert_reduce_fusion.2
  269.7 0.8 copy-done.1
  270.5 6.3 %convolution_convert_fusion = bf16[128,2048]{1,0:T(8,128)(2,1)S(1)} fusion(bf16[128,2048]{1,0:T(8,128)(2,1)S(1)} %get-tuple-element.83.branch, bf16[2048,2048]{1,0:T(8,128)(2,1)} %bitcast.43), kind=kOutput, calls=%fused_computation.1 | convolution fusion | flops 1074003968 | bytes 9437184 | tf_op jit(solution)/shard_map/te,de->td/dot_general | solution.py:2096
  276.8 0.4 reshape.137
  277.2 0.4 copy.41
  277.6 1.1 reshape.138.grad_in
  278.7 147.1 %tail.1 = (f32[128,2048]{1,0:T(8,128)}, f32[256,2048]{1,0:T(8,128)}, f32[64,2048]{1,0:T(8,128)}, f32[1,768]{1,0:T(1,128)}, f32[1,2048]{1,0:T(1,128)}, /*index=5*...) custom-call(f32[32]{0:T(128)} %constant.62.clone.refs_0_.slopes, ...), custom_call_target="tpu_custom_call" | custom-call | tf_op jit(solution)/shard_map/tail/pallas_call | solution.py:1558
  425.8 0.0 copy-start.3
  425.9 1.4 reduce_sum.158
  427.3 1.4 pad_maximum_fusion
  428.6 0.0 copy-done
  428.6 1.7 fusion.10
  430.3 0.1 reshape.142
  430.4 0.1 reshape.143
  430.5 0.7 slice_reduce_fusion
  431.2 0.1 reshape_squeeze.6
  431.3 0.1 reshape_squeeze.7
  431.4 0.1 reshape.146
  431.4 0.5 broadcast.99
  431.9 0.0 copy-done.7
  431.9 0.7 reduce.12
  432.7 0.1 reshape.147
  432.8 0.1 reshape.148
  432.8 1.2 convert_reduce_fusion.1
  434.0 0.1 reshape.149
  434.1 0.1 concatenate.3
  434.3 2.0 fusion.9.refs_0_
  436.3 16.8 %finish.1 = (bf16[128,2048]{1,0:T(8,128)(2,1)S(1)}, f32[8,128]{1,0:T(8,128)S(1)}) custom-call(bf16[128,2048]{1,0:T(8,128)(2,1)S(1)} %fusion.9.refs_0_, f32[32,8,128]{2,1,0:T(8,128)S(1)} %bitcast.39), custom_call_target="tpu_custom_call" | custom-call | tf_op jit(solution)/shard_map/finish/pallas_call | solution.py:870
  453.2 0.6 fusion.15
  453.8 0.6 slice_bitcast_fusion
  454.3 0.5 multiply_sqrt_fusion
  454.8 1.5 convert_element_type.41
  456.3 0.0 copy-done.4
  456.3 1.2 convert_element_type.40
  457.6 0.0 copy-done.6
  457.6 0.8 copy.51
  458.4 0.8 copy.52
  459.2 0.8 copy.53
  459.9 1.3 copy.54
  (28 shorter events, 0.2 us)
Async XLA Ops:
  269.7 0.8 copy-start.1
  278.7 149.9 %copy-start = (bf16[128,2048]{1,0:T(8,128)(2,1)S(1)}, bf16[128,2048]{1,0:T(8,128)(2,1)}, u32[]{:S(2)}) copy-start(bf16[128,2048]{1,0:T(8,128)(2,1)} %get-tuple-element.46) | copy-start | bytes 1572868
  278.7 153.2 %copy-start.7 = (f32[1,1024]{1,0:T(1,128)S(1)}, f32[1,1024]{1,0:T(1,128)}, u32[]{:S(2)}) copy-start(f32[1,1024]{1,0:T(1,128)} %get-tuple-element.64) | copy-start | bytes 12292
  425.8 29.0 %copy-start.3 = (bf16[64,8192]{1,0:T(8,128)(2,1)S(1)}, bf16[64,8192]{1,0:T(8,128)(2,1)}, u32[]{:S(2)}) copy-start(bf16[64,8192]{1,0:T(8,128)(2,1)} %get-tuple-element.69) | copy-start | bytes 3145732
  432.8 23.5 %copy-start.4 = (bf16[64,6144]{1,0:T(8,128)(2,1)S(1)}, bf16[64,6144]{1,0:T(8,128)(2,1)}, u32[]{:S(2)}) copy-start(bf16[64,6144]{1,0:T(8,128)(2,1)} %get-tuple-element.67) | copy-start | bytes 2359300
  434.3 23.3 %copy-start.6 = (bf16[128,2048]{1,0:T(8,128)(2,1)S(1)}, bf16[128,2048]{1,0:T(8,128)(2,1)}, u32[]{:S(2)}) copy-start(bf16[128,2048]{1,0:T(8,128)(2,1)} %get-tuple-element.120) | copy-start | bytes 1572868
  436.3 22.8 %copy-start.5 = (f32[64,2048]{1,0:T(8,128)S(1)}, f32[64,2048]{1,0:T(8,128)}, u32[]{:S(2)}) copy-start(f32[64,2048]{1,0:T(8,128)} %get-tuple-element.123) | copy-start | bytes 1572868
  454.8 5.1 %copy-start.2 = (f32[256,2048]{1,0:T(8,128)S(1)}, f32[256,2048]{1,0:T(8,128)}, u32[]{:S(2)}) copy-start(f32[256,2048]{1,0:T(8,128)} %get-tuple-element.125) | copy-start | bytes 6291460

commit v7 on v6

--- a/solution.py
+++ b/solution.py
@@ -1199,8 +1199,9 @@
 
 def scatter_parts(nz, pos, own, other, acc, came, send, recv):
     x, c, z, y = pos
-    S, U, D = 0, nz, 2 * nz
+    S, U, D = 0, nz, 3 * nz
     sib = at(x, 1 - c, z, y)
+    half = acc.shape[1] // 2
 
     def f(v):
         return v.astype(F32)
@@ -1208,29 +1209,43 @@
     def swap(t):
         return remote(other(t), acc.at[t], send.at[S + t], recv.at[S + t], sib)
 
-    def rise(t):
-        return remote(acc.at[t], came.at[t], send.at[U + t], recv.at[U + t], at(x, c, z + 1, y))
-
-    def fall(t):
+    def piece(ref, t, h):
+        return ref.at[t, pl.ds(h * half, half)]
+
+    def rise(t, h):
+        sem = U + t * 2 + h
+        return remote(piece(acc, t, h), piece(came, t, h), send.at[sem], recv.at[sem], at(x, c, z + 1, y))
+
+    def fall(t, h):
         slot = jnp.where(z - 1 == t, nz, t)
-        return remote(acc.at[t], came.at[slot], send.at[D + t], recv.at[D + t], at(x, c, z - 1, y))
-
-    def arrival(slot, sem):
-        return remote(came.at[slot], came.at[slot], send.at[S], recv.at[sem], sib)
+        sem = D + t * 2 + h
+        return remote(piece(acc, t, h), piece(came, slot, h), send.at[sem], recv.at[sem], at(x, c, z - 1, y))
+
+    def arrival(slot, h, sem):
+        there = piece(came, slot, h)
+        return remote(there, there, send.at[S], recv.at[sem], sib)
 
     def event(t, upward):
         swap(t).wait_recv()
-
-        @pl.when(z > 0 if upward else z < nz - 1)
-        def _():
-            arrival(t, (U if upward else D) + t).wait_recv()
-            acc[t] = (f(acc[t]) + f(own(t)) + f(came[t])).astype(BF)
-
-        @pl.when(z == 0 if upward else z == nz - 1)
-        def _():
-            acc[t] = (f(acc[t]) + f(own(t))).astype(BF)
-
-        (rise if upward else fall)(t).start()
+        acc[t] = (f(acc[t]) + f(own(t))).astype(BF)
+        for h in range(2):
+
+            @pl.when(z > 0 if upward else z < nz - 1)
+            def _():
+                arrival(t, h, (U if upward else D) + t * 2 + h).wait_recv()
+                here = slice(h * half, (h + 1) * half)
+                acc[t, here] = (f(acc[t, here]) + f(came[t, here])).astype(BF)
+
+            (rise if upward else fall)(t, h).start()
+
+    def slot(k):
+        for t in range(nz):
+            zz = k - t
+            if 0 <= zz < t:
+                pl.when(z == zz)(functools.partial(event, t, True))
+            zz = 2 * (nz - 1) - k - t
+            if t < zz < nz:
+                pl.when(z == zz)(functools.partial(event, t, False))
 
     def begin():
         for i in range(nz - 1):
@@ -1251,24 +1266,23 @@
     def total(out):
         swap(z).wait_recv()
         out[...] = f(acc[z]) + f(own(z))
-
-        @pl.when(z > 0)
-        def _():
-            arrival(z, U + z).wait_recv()
-            out[...] += f(came[z])
-
-        @pl.when(z < nz - 1)
-        def _():
-            arrival(nz, D + z).wait_recv()
-            out[...] += f(came[nz])
+        for upward, slot, base in ((True, z, U), (False, nz, D)):
+
+            @pl.when(z > 0 if upward else z < nz - 1)
+            def _():
+                for h in range(2):
+                    here = slice(h * half, (h + 1) * half)
+                    arrival(slot, h, base + z * 2 + h).wait_recv()
+                    out[here, :] += f(came[slot, here])
 
     def done():
         for t in range(nz):
             swap(t).wait_send()
-            pl.when(z < t)(lambda t=t: rise(t).wait_send())
-            pl.when(z > t)(lambda t=t: fall(t).wait_send())
-
-    return swap, begin, near, far, total, done
+            for h in range(2):
+                pl.when(z < t)(lambda: rise(t, h).wait_send())
+                pl.when(z > t)(lambda: fall(t, h).wait_send())
+
+    return swap, slot, begin, near, far, total, done
 
 
 def reduce_parts(src, mine, near, far, send, recv, lsem, pos):
@@ -1340,7 +1354,8 @@
 
 def tail_kernel(
     heads, nz, runs_up, runs_qkv, slopes, far_in, grad_in, joined, a1_in, mixed, qkv_in, branch, upd_in, up_src, down_src,
-    base, grad_out, down_o, out_o, col_o, square_o, up_o, qkv_o, branch_all, layer_o, grad_s, *refs,
+    middle, x_own, whole, grad_middle, sums, bias_g,
+    down_o, out_o, small_o, bias_o, up_o, qkv_o, branch_all, layer_o, grad_o, grad_s, *refs,
 ):
     refs = list(refs)
 
@@ -1354,7 +1369,9 @@
     att_p, att_acc, att_came, att_send, att_recv = take(5)
     up_refs, down_refs, qkv_refs, out_refs = take(6), take(6), take(6), take(6)
     up_sum, qkv_sum, qkv_g, out_g, res, res_low = take(6)
-    gsems, esems, esems_up, esems_qkv, tsems = take(2), take(2), take(2), take(2), take(2)
+    grad_low, vec, came, bias_t, bias_c = take(5)
+    gsems, esems, esems_up, esems_qkv, tsems, tsems_x = take(2), take(2), take(2), take(2), take(2), take(2)
+    vsems, bsems = take(2), take(2)
     gap_sem, load_sem = take(2)
 
     pos = place()
@@ -1372,15 +1389,38 @@
     down1, down2, down_total, down_done = reduce_parts(down_src, *down_refs, pos)
     qkv1, qkv2, qkv_total, qkv_done = reduce_parts(qkv_g, *qkv_refs, pos)
     out1, out2, out_total, out_done = reduce_parts(out_g, *out_refs, pos)
-    upd_swap, upd_begin, upd_near, upd_far, upd_total, upd_done = scatter_parts(
+    upd_swap, _, upd_begin, upd_near, upd_far, upd_total, upd_done = scatter_parts(
         nz, pos, lambda t: upd_own[t], lambda t: upd_in.at[t * 2 + 1 - c], upd_acc, upd_came, upd_send, upd_recv
     )
-    att_swap, att_begin, att_near, att_far, att_total, att_done = scatter_parts(
+    att_swap, _, att_begin, att_near, att_far, att_total, att_done = scatter_parts(
         nz, pos, lambda t: att_p[t * 2 + c], lambda t: att_p.at[t * 2 + 1 - c], att_acc, att_came, att_send, att_recv
     )
     ex_up = exchange_stages(up_sum, up_o, runs_up, *esems_up, nz, pos)
     ex_qkv = exchange_stages(qkv_sum, qkv_o, runs_qkv, *esems_qkv, nz, pos)
     home = trade_stages(res_low, layer_o, *tsems, pos)
+    home_x = trade_stages(grad_low, grad_o, *tsems_x, pos)
+    devices = 4 * n
+    me = block_of(x, c, z, y, nz)
+    group = x * 2 + y
+
+    def each(fn):
+        def body(k, _):
+            fn((me + k) % devices)
+            return 0
+
+        lax.fori_loop(1, devices, body, 0)
+
+    def share(other):
+        tile = vec.at[:, pl.ds(pl.multiple_of(other // 2 * 128, 128), 128)]
+        return remote(tile, came.at[me], vsems[0].at[other], vsems[1].at[me], (other // n, other % n))
+
+    def share_come(other):
+        there = came.at[other]
+        remote(there, there, vsems[0].at[me], vsems[1].at[other], at(x, 1 - c, z, y)).wait_recv()
+
+    def bias_share(m):
+        target = at(x ^ (m // 2), c, z, y ^ (m % 2))
+        return remote(bias_t.at[group ^ m], bias_c.at[m - 1], bsems[0].at[m - 1], bsems[1].at[m - 1], target)
     loads = [pltpu.make_async_copy(upd_in.at[t * 2 + c], upd_own.at[t], load_sem.at[t]) for t in range(nz)]
     load_w = pltpu.make_async_copy(qkv_in, qkv_w, load_sem.at[nz])
     load_a = pltpu.make_async_copy(a1_in, tokens, load_sem.at[nz + 1])
@@ -1391,7 +1431,7 @@
             far_in.at[:, pl.ds(pl.multiple_of(i * step, step), step)], gap_s.at[slot], gap_sem.at[slot]
         )
 
-    greet(rank_partners(nz, pos) + group_partners(pos) + [(c != y, at(x, y, z, c))])
+    greet_all(devices, n, me)
     es[0]()
     up1()
     for t in range(nz):
@@ -1441,10 +1481,9 @@
                 for fn in fns:
                     fn()
 
-        later(0, [down1])
-        later(1, [gb[2], lambda: upd_near(0)])
-        later(2, [up2, gb[3], lambda: upd_near(1)])
-        later(3, [gb[4], upd_far])
+        later(1, [gb[2]])
+        later(2, [up2])
+        later(3, [down1, lambda: upd_near(0)])
         return 0
 
     lax.fori_loop(0, steps, attend_step, 0)
@@ -1452,6 +1491,12 @@
     grad_joined[:, 2 * cols :] = acc_v[...].astype(BF)
     load_w.wait()
 
+    def put_ranks(dest):
+        def put(lower, value):
+            dest[pl.ds(lower * nz, nz)] = value.astype(BF).reshape(nz, part, -1)
+
+        return put
+
     def back(t, _):
         here = pl.ds(pl.multiple_of(t * 2 * rows, 2 * rows), 2 * rows)
 
@@ -1465,7 +1510,6 @@
         return 0
 
     lax.fori_loop(0, nz, back, 0)
-    col_o[...] = jnp.sum(grad_joined[...].astype(F32), axis=0, keepdims=True)
     load_a.wait()
     blocks = 256 // part
 
@@ -1480,27 +1524,35 @@
         return 0
 
     att_begin()
+    col = jnp.sum(grad_joined[...].astype(F32), axis=0, keepdims=True)
+    vec[...] = jnp.zeros_like(vec)
+    for there, here, size in head_runs(nz, cols)(rank):
+        there = pl.multiple_of(there, 128)
+        vec[2:3, pl.ds(there, size)] = col[:, here : here + size]
+        vec[3:4, pl.ds(there, size)] = col[:, 2 * cols + here : 2 * cols + here + size]
+    for i, k in enumerate((2, 0, 1, 3)):
+        vec[4 + i : 5 + i, :] = sums[k : k + 1, :]
+    vec[9:10, :] = jnp.broadcast_to(jnp.sum(sums[4:5, :], axis=1, keepdims=True), (1, width))
+    bias_t[...] = jnp.zeros_like(bias_t)
+    per = bias_g.shape[1] // 512
+    for g in range(4):
+        for i in range(per):
+            bias_t[g, i : i + 1, :] = bias_g[:, (g * per + i) * 128 : (g * per + i + 1) * 128]
+    for m in (1, 2, 3):
+        bias_share(m).start()
+    gb[3]()
     lax.fori_loop(0, width // 256, qkv_tile, 0)
     qkv1()
-    down2()
-    att_near(0)
-
-    def put_ranks(dest):
-        def put(lower, value):
-            dest[pl.ds(lower * nz, nz)] = value.astype(BF).reshape(nz, part, -1)
-
-        return put
-
+    upd_near(1)
+    gb[4]()
     up_total(put_ranks(up_sum))
     ex_up[0]()
+    upd_far()
+    att_near(0)
     att_near(1)
     qkv2()
     att_far()
-    upd_total(res)
-    res[...] += base[...]
-    res_low[...] = res[...].astype(BF)
-    home[0]()
-    square_o[...] = jnp.sum(res[...] * res[...], axis=0, keepdims=True)
+    down2()
     for stage in gb[5:]:
         stage()
     load_b.start()
@@ -1516,7 +1568,27 @@
     out1()
     qkv_total(put_ranks(qkv_sum))
     ex_qkv[0]()
-    att_total(grad_out)
+    att_total(res)
+
+    def norm(j, _):
+        here = pl.ds(pl.multiple_of(j * 32, 32), 32)
+        normed, inverse = norm_parts(x_own[here, :].astype(F32))
+        value = res[here, :]
+        through = grad_middle[here, :] + norm_back(value * whole[0:1, :], normed, inverse)
+        grad_low[here, :] = through.astype(BF)
+        vec[0:1, :] += jnp.sum(value * normed, axis=0, keepdims=True)
+        vec[1:2, :] += jnp.sum(value, axis=0, keepdims=True)
+        return 0
+
+    lax.fori_loop(0, rows // 32, norm, 0)
+    home_x[0]()
+    upd_total(res)
+    res[...] += middle[...] + whole[7:8, :]
+    res_low[...] = res[...].astype(BF)
+    home[0]()
+    square = jnp.sum(jnp.sum(res[...] * res[...], axis=0, keepdims=True), axis=1, keepdims=True)
+    vec[8:9, :] = jnp.broadcast_to(square, (1, width))
+    each(lambda other: share(other).start())
     out2()
 
     def put_down(lower, value):
@@ -1529,14 +1601,28 @@
         out_o[pl.ds(lower * half, half), :] = value
 
     out_total(put_out)
+    each(share_come)
+    came[me] = vec[:, pl.ds(pl.multiple_of(me // 2 * 128, 128), 128)]
+    summed = jnp.sum(came[...], axis=0)
+    small_o[...] = jnp.where(y == 1, pltpu.roll(summed, 64, 1), summed)
+    for m in (1, 2, 3):
+        bias_share(m).wait_recv()
+    bias_o[...] = bias_t[group] + jnp.sum(bias_c[...], axis=0)
     ex_up[1]()
     home[1]()
+    home_x[1]()
     ex_qkv[1]()
+    each(lambda other: share(other).wait_send())
+    for m in (1, 2, 3):
+        bias_share(m).wait_send()
     for fn in (up_done, down_done, qkv_done, out_done, upd_done, att_done):
         fn()
 
 
-def tail_call(slopes, far_t, grad, joined, a1, mixed, qkv_w, branch, upd, up_g, down_g, base, runs, heads, nz, cid):
+def tail_call(
+    slopes, far_t, grad, joined, a1, mixed, qkv_w, branch, upd, up_g, down_g, middle, x_own, whole, grad_middle, sums, bias_g,
+    runs, heads, nz, cid,
+):
     tree, cols = mixed.shape
     rows, width = branch.shape
     n = 2 * nz
@@ -1551,25 +1637,25 @@
             pltpu.VMEM((own, rows, width), BF),
             pltpu.VMEM((nz, rows, width), BF),
             pltpu.VMEM((nz + 1, rows, width), BF),
-            pltpu.SemaphoreType.DMA((3 * nz,)),
-            pltpu.SemaphoreType.DMA((3 * nz,)),
+            pltpu.SemaphoreType.DMA((5 * nz,)),
+            pltpu.SemaphoreType.DMA((5 * nz,)),
         ]
 
     return pl.pallas_call(
         functools.partial(tail_kernel, heads, nz, runs_up, runs_qkv),
         out_shape=[
-            shape((rows, width), F32),
             shape((unit, width), F32),
             shape((part, width), F32),
-            shape((1, 3 * cols), F32),
-            shape((1, width), F32),
+            shape((16, 128), F32),
+            shape((8, 128), F32),
             shape((part, 4 * n * unit), BF),
             shape((part, 3 * width), BF),
             shape((n, rows, width), BF),
             shape((rows, width), BF),
+            shape((rows, width), BF),
         ],
-        in_specs=[pl.BlockSpec(memory_space=pltpu.SMEM), HBM, HBM, VM, HBM, VM, HBM, HBM, HBM, HBM, HBM, VM],
-        out_specs=[VM] * 5 + [HBM] * 4,
+        in_specs=[pl.BlockSpec(memory_space=pltpu.SMEM), HBM, HBM, VM, HBM, VM] + [HBM] * 5 + [VM] * 6,
+        out_specs=[VM] * 4 + [HBM] * 5,
         scratch_shapes=[
             pltpu.VMEM((n, rows, cols), BF),
             pltpu.VMEM((2, tree, step), F32),
@@ -1592,16 +1678,26 @@
             pltpu.VMEM((4, part, width), BF),
             pltpu.VMEM((rows, width), F32),
             pltpu.VMEM((rows, width), BF),
+            pltpu.VMEM((rows, width), BF),
+            pltpu.VMEM((16, width), F32),
+            pltpu.VMEM((4 * n, 16, 128), F32),
+            pltpu.VMEM((4, 8, 128), F32),
+            pltpu.VMEM((3, 8, 128), F32),
         ]
         + gather_sems(nz)
         + exchange_sems(None, nz)
         + exchange_sems(runs_up, nz)
         + exchange_sems(runs_qkv, nz)
-        + trade_sems()
+        + trade_sems() * 2
+        + [pltpu.SemaphoreType.DMA((4 * n,))] * 2
+        + [pltpu.SemaphoreType.DMA((3,))] * 2
         + [pltpu.SemaphoreType.DMA((2,)), pltpu.SemaphoreType.DMA((nz + 3,))],
         compiler_params=params(cid, 63 * MIB),
         name="tail",
-    )(slopes, far_t, grad, joined, a1, mixed, qkv_w, branch, upd, up_g, down_g, base)
+    )(
+        slopes, far_t, grad, joined, a1, mixed, qkv_w, branch, upd, up_g, down_g,
+        middle, x_own, whole, grad_middle, sums, bias_g,
+    )
 
 
 def gelu_and_slope(value):
@@ -1611,8 +1707,9 @@
 
 
 def mlp_kernel(
-    nz, own, cot_in, up_in, down_in, bias, out, upd_out, up_out, down_out, bias_g,
-    mlp, cot, up_w, down_w, p, upd, up_g, down_g, active, gh, acc, ups, dns, gsend, grecv, ssend, srecv, lsem,
+    nz, mixed, x_own, whole, out_in, cot_in, up_in, down_in, bias,
+    middle, grad_middle, grad_branch, grad_mixed, sums, bias_g, upd_out, up_out, down_out,
+    mlp, cot, up_w, down_w, p, upd, up_g, down_g, out_w, active, gh, grad, acc, came, gsend, grecv, ssend, srecv, lsem,
 ):
     pos = place()
     x, c, z, y = pos
@@ -1623,28 +1720,27 @@
     sib = at(x, 1 - c, z, y)
     up_dev, dn_dev = at(x, c, z + 1, y), at(x, c, z - 1, y)
     UP, DN, SU, SD = 0, nz, 2 * nz, 3 * nz
-    S, U, D = 0, nz, 2 * nz
+    part = out_w.shape[1]
 
     def f(v):
         return v.astype(F32)
 
     loads = [
         pltpu.make_async_copy(a, b, lsem.at[i])
-        for i, (a, b) in enumerate([(cot_in, cot), (down_in, down_w), (up_in, up_w)])
+        for i, (a, b) in enumerate([(out_in, out_w), (up_in, up_w), (cot_in, cot), (down_in, down_w)])
     ]
-    part = up_out.shape[1] // blocks
 
     def rank_rows(r):
         d, f = r // blocks, r % blocks
         return up_out.at[d // 2 * 2 + f % 2, pl.ds((f // 2 * 2 + d % 2) * part, part)]
 
     stores = [
-        [pltpu.make_async_copy(upd, upd_out, lsem.at[3])],
+        [pltpu.make_async_copy(upd, upd_out, lsem.at[4])],
         [
-            pltpu.make_async_copy(up_g.at[pl.ds(r * part, part)], rank_rows(r), lsem.at[5 + r])
+            pltpu.make_async_copy(up_g.at[pl.ds(r * part, part)], rank_rows(r), lsem.at[6 + r])
             for r in range(4 * blocks)
         ],
-        [pltpu.make_async_copy(down_g, down_out, lsem.at[4])],
+        [pltpu.make_async_copy(down_g, down_out, lsem.at[5])],
     ]
 
     def store(i):
@@ -1684,35 +1780,9 @@
         block(zi * 2 + 1 - c, jnp.where(below, SU, SD) + d, sib).wait_recv()
         return zi
 
-    def swap(t):
-        return remote(p.at[t * 2 + 1 - c], acc.at[t], ssend.at[S + t], srecv.at[S + t], sib)
-
-    def rise(t):
-        return remote(acc.at[t], ups.at[t], ssend.at[U + t], srecv.at[U + t], up_dev)
-
-    def fall(t):
-        return remote(acc.at[t], dns.at[t], ssend.at[D + t], srecv.at[D + t], dn_dev)
-
-    def event(t, upward):
-        swap(t).wait_recv()
-        acc[t] = (f(acc[t]) + f(p[t * 2 + c])).astype(BF)
-        move, came = (rise, ups) if upward else (fall, dns)
-
-        @pl.when(z > 0 if upward else z < nz - 1)
-        def _():
-            move(t).wait_recv()
-            acc[t] = (f(acc[t]) + f(came[t])).astype(BF)
-
-        move(t).start()
-
-    def events(s):
-        for t in range(nz):
-            zz = s - t
-            if 0 <= zz < t:
-                pl.when(z == zz)(functools.partial(event, t, True))
-            zz = 2 * (nz - 1) - s - t
-            if t < zz < nz:
-                pl.when(z == zz)(functools.partial(event, t, False))
+    swap, slot, _, _, _, total, done = scatter_parts(
+        nz, pos, lambda t: p[t * 2 + c], lambda t: p.at[t * 2 + 1 - c], acc, came, ssend, srecv
+    )
 
     def at_rows(ref, zi):
         return ref[pl.ds(zi * 2, 2)].reshape(pair, width)
@@ -1766,15 +1836,63 @@
 
         lax.fori_loop(0, units // 256, tile, 0)
 
-    mlp[me] = own[...]
+    def project():
+        def tile(j, _):
+            w = pl.ds(pl.multiple_of(j * 512, 512), 512)
+            branch = dot(mixed[...], out_w[:, :, w].reshape(width, 512), NN) + whole[4:5, w]
+            sums[4:5, w] = jnp.sum(branch * branch, axis=0, keepdims=True)
+            middle[:, w] = f(x_own[:, w]) + branch
+            return 0
+
+        lax.fori_loop(0, width // 512, tile, 0)
+
+        def norm(j, _):
+            here = pl.ds(pl.multiple_of(j * 32, 32), 32)
+            normed, _ = norm_parts(middle[here, :])
+            mlp[me, here] = (normed * whole[5:6, :] + whole[6:7, :]).astype(BF)
+            return 0
+
+        lax.fori_loop(0, rows // 32, norm, 0)
+
+    def finish_rows():
+        def norm(j, _):
+            here = pl.ds(pl.multiple_of(j * 32, 32), 32)
+            normed, inverse = norm_parts(middle[here, :])
+            value, own = grad[here, :], f(cot[me, here])
+            through = own + norm_back(value * whole[5:6, :], normed, inverse)
+            low = through.astype(BF)
+            grad_middle[here, :] = through
+            grad_branch[here, :] = low
+            for i, v in enumerate((value * normed, value, f(low), own)):
+                sums[i : i + 1, :] += jnp.sum(v, axis=0, keepdims=True)
+            return 0
+
+        lax.fori_loop(0, rows // 32, norm, 0)
+        each = 256 // part
+
+        def tile(j, _):
+            value = dot(grad_branch[...], out_w[pl.ds(j * each, each)].reshape(256, width), NT).astype(BF)
+            for i in range(2):
+                r = j * each + i * (each // 2)
+                d, fs = r // blocks, r % blocks
+                grad_mixed[fs // 2 * 2 + d % 2, :, pl.ds(pl.multiple_of(d // 2 * 128, 128), 128)] = value[
+                    :, i * 128 : (i + 1) * 128
+                ]
+            return 0
+
+        lax.fori_loop(0, width // 256, tile, 0)
+
+    for copy in loads:
+        copy.start()
+    bias_g[...] = jnp.zeros_like(bias_g)
+    sums[...] = jnp.zeros_like(sums)
     greet(line_partners(nz, pos))
+    loads[0].wait()
+    project()
     pl.when(z < nz - 1)(up(0).start)
     pl.when(z > 0)(dn(0).start)
     side(0, z >= 0).start()
-    for copy in loads:
-        copy.start()
-    bias_g[...] = jnp.zeros_like(bias_g)
-    for copy in loads:
+    for copy in loads[1:]:
         copy.wait()
     slots = 2 * nz - 1
     tiles = width // 256
@@ -1783,7 +1901,7 @@
             zi = arrive(s)
             hidden_part(zi, s)
             swap(zi).start()
-        events(s)
+        slot(s)
         if s < nz:
             forward_part(zi)
         if s == nz - 1:
@@ -1795,19 +1913,8 @@
         elif s == nz + 1:
             up_grads(tiles // 2, tiles - tiles // 2)
             store(1)
-    swap(z).wait_recv()
-    out[...] = f(acc[z]) + f(p[z * 2 + c])
-
-    @pl.when(z > 0)
-    def _():
-        rise(z).wait_recv()
-        out[...] += f(ups[z])
-
-    @pl.when(z < nz - 1)
-    def _():
-        fall(z).wait_recv()
-        out[...] += f(dns[z])
-
+    total(grad)
+    finish_rows()
     for copies in stores:
         for copy in copies:
             copy.wait()
@@ -1826,19 +1933,17 @@
             pl.when(z > 0)(dn(k).wait_send)
             side(k, z < 0).wait_send()
 
-    for t in range(nz):
-        swap(t).wait_send()
-        pl.when(z < t)(rise(t).wait_send)
-        pl.when(z > t)(fall(t).wait_send)
+    done()
 
 
 def mlp_bytes(nz, rows, width, units):
     tree = 2 * nz * rows
-    return 2 * (4 * tree * width + 4 * units * width + 2 * tree * units + 3 * nz * rows * width) + 8 * rows * width
-
-
-def mlp_call(own, cot, up_w, down_w, bias, nz, cid):
-    rows, width = own.shape
+    kept = 4 * tree * width + 4 * units * width + 2 * tree * units + 2 * nz * rows * width + width * width
+    return 2 * kept + 14 * rows * width
+
+
+def mlp_call(mixed, x_own, whole, out_w, cot, up_w, down_w, bias, nz, cid):
+    rows, width = x_own.shape
     units = down_w.shape[0]
     n = 2 * nz
     shape = jax.ShapeDtypeStruct
@@ -1846,13 +1951,17 @@
         functools.partial(mlp_kernel, nz),
         out_shape=[
             shape((rows, width), F32),
+            shape((rows, width), F32),
+            shape((rows, width), BF),
+            shape((n, rows, width // n), BF),
+            shape((8, width), F32),
+            shape((1, units), F32),
             shape((n, rows, width), BF),
             shape((4, width // 4, units), BF),
             shape((units, width), BF),
-            shape((1, units), F32),
         ],
-        in_specs=[VM, HBM, HBM, HBM, VM],
-        out_specs=[VM, HBM, HBM, HBM, VM],
+        in_specs=[VM] * 3 + [HBM] * 4 + [VM],
+        out_specs=[VM] * 6 + [HBM] * 3,
         scratch_shapes=[
             pltpu.VMEM((n, rows, width), BF),
             pltpu.VMEM((n, rows, width), BF),
@@ -1862,16 +1971,19 @@
             pltpu.VMEM((n, rows, width), BF),
             pltpu.VMEM((width, units), BF),
             pltpu.VMEM((units, width), BF),
+            pltpu.VMEM(out_w.shape, BF),
             pltpu.VMEM((n * rows, units), BF),
             pltpu.VMEM((n * rows, units), BF),
+            pltpu.VMEM((rows, width), F32),
+            pltpu.VMEM((nz, rows, width), BF),
+            pltpu.VMEM((nz + 1, rows, width), BF),
         ]
-        + [pltpu.VMEM((nz, rows, width), BF)] * 3
         + gather_sems(nz)
-        + [pltpu.SemaphoreType.DMA((3 * nz,))] * 2
-        + [pltpu.SemaphoreType.DMA((5 + 4 * n,))],
-        compiler_params=params(cid, 62 * MIB),
+        + [pltpu.SemaphoreType.DMA((5 * nz,))] * 2
+        + [pltpu.SemaphoreType.DMA((6 + 4 * n,))],
+        compiler_params=params(cid, 63 * MIB),
         name="mlp",
-    )(own, cot, up_w, down_w, bias)
+    )(mixed, x_own, whole, out_w, cot, up_w, down_w, bias)
 
 
 def attend_kernel(
@@ -2340,8 +2452,6 @@
     fsdp = lax.axis_size("fsdp")
     nz = fsdp // 2
     devices = 4 * fsdp
-    x, c, z, y = place()
-    rank = z * 2 + c
     heads = H // fsdp
     cols = heads * HD
     tree = token_valid.shape[1]
@@ -2356,59 +2466,18 @@
     )
     qkv_w = qkv_w.reshape(width, 3 * cols)
     up_w = up_w.reshape(width, 4 * unit)
-    out_w = out_w.reshape(width, width)
     down_w = down_w.reshape(4 * unit, width)
-    gain_one, out_bias, gain_two, shift_two, down_bias = [whole[i] for i in (0, 4, 5, 6, 7)]
-
-    inputs = own.astype(F32)
-    normed_one, inverse_one = norm_parts(inputs)
-    branch = jnp.dot(mixed_own, out_w, preferred_element_type=F32) + out_bias
-    middle = inputs + branch
-    normed_two, inverse_two = norm_parts(middle)
-    mlp_own = (normed_two * gain_two + shift_two).astype(BF)
-    grad_mlp_in, update, up_g, down_g, grad_bias_up = mlp_call(mlp_own, cot, up_w, down_w, up_bias, nz, 3)
+    middle, grad_middle, grad_branch, grad_mixed, sums, grad_bias_up, update, up_g, down_g = mlp_call(
+        mixed_own, own, whole, out_w, cot, up_w, down_w, up_bias, nz, 3
+    )
     down_g = down_g.reshape(4, unit, width)
-
-    cot_own = lax.dynamic_index_in_dim(cot, rank, 0, keepdims=False).astype(F32)
-    grad_middle = cot_own + norm_back(grad_mlp_in * gain_two, normed_two, inverse_two)
-    grad_branch = grad_middle.astype(BF)
-    grad_mixed = mm("te,de->td", grad_branch, out_w).astype(BF)
-    grad_mixed = grad_mixed.reshape(rows, 2, 2, nz, 2 * HD).transpose(3, 2, 0, 1, 4).reshape(fsdp, rows, cols)
     runs = up_runs(nz, unit), qkv_runs(nz, width, cols)
-    grad_attn_in, grad_down_w, grad_out_w, col, square, grad_up_w, grad_qkv_w, _, layer_out = tail_call(
-        slopes, far, grad_mixed, joined, attn_in, mixed.reshape(tree, cols), qkv_w, grad_branch,
-        update, up_g, down_g, middle + down_bias, runs, heads, nz, 6,
+    grad_down_w, grad_out_w, small, bias, grad_up_w, grad_qkv_w, _, layer_out, grad_x = tail_call(
+        slopes, far, grad_mixed, joined, attn_in, mixed.reshape(tree, cols), qkv_w, grad_branch, update, up_g, down_g,
+        middle, own, whole, grad_middle, sums, grad_bias_up, runs, heads, nz, 6,
     )
-    grad_inputs = grad_middle + norm_back(grad_attn_in * gain_one, normed_one, inverse_one)
-
-    def spread(v):
-        v = v.reshape(2, 1, 1, 2, HD)
-        return lax.dynamic_update_slice(jnp.zeros((2, 2, nz, 2, HD), F32), v, (0, c, z, 0, 0))
-
-    smalls = [
-        jnp.sum(grad_attn_in * normed_one, axis=0),
-        jnp.sum(grad_attn_in, axis=0),
-        spread(col[0, :cols]),
-        spread(col[0, 2 * cols :]),
-        jnp.sum(grad_branch.astype(F32), axis=0),
-        jnp.sum(grad_mlp_in * normed_two, axis=0),
-        jnp.sum(grad_mlp_in, axis=0),
-        jnp.sum(cot_own, axis=0),
-    ]
-    grad_bias_up = grad_bias_up.reshape(2, 1, 1, 2, unit)
-    grad_bias_up = lax.dynamic_update_slice(jnp.zeros((2, 2, nz, 2, unit), F32), grad_bias_up, (0, c, z, 0, 0))
-    squares = jnp.stack([jnp.sum(square), jnp.sum(branch * branch)])
-    packed = jnp.concatenate(
-        [v.reshape(devices, part) for v in smalls]
-        + [grad_bias_up.reshape(devices, unit), jnp.broadcast_to(squares, (devices, 2))],
-        axis=1,
-    )
-    packed = padded(packed, 1024).reshape(devices, -1, 128)
-    grad_x, packed = finish(grad_inputs.astype(BF), packed, None, None, nz, 8)
-    packed = packed.reshape(-1)
-    small = [packed[i * part : (i + 1) * part] for i in range(8)]
-    up_at = 8 * part
-    root_squares = jnp.sqrt(packed[up_at + unit : up_at + unit + 2] / (devices * rows * width))
+    root_squares = jnp.sqrt(small[8:10, 0] / (devices * rows * width))
+    vectors = [small[i, :part] for i in range(8)]
     return (
         layer_out,
         grad_x,
@@ -2416,15 +2485,9 @@
         grad_out_w,
         grad_up_w.astype(F32),
         grad_down_w,
-        small[0],
-        small[1],
-        small[2],
-        small[3],
-        small[4],
-        small[5],
-        small[6],
-        packed[up_at : up_at + unit],
-        small[7],
+        *vectors[:7],
+        bias.reshape(-1)[:unit],
+        vectors[7],
         root_squares,
     )
 
@@ -2434,7 +2497,7 @@
     fsdp = lax.axis_size("fsdp")
     rows, width = layer_in.shape
     unit = w_down.shape[0]
-    fits = mlp_bytes(fsdp // 2, rows, width, 4 * unit) < 50 * MIB
+    fits = mlp_bytes(fsdp // 2, rows, width, 4 * unit) < 60 * MIB
     whole_heads = args[2].shape[0] == HD and H // fsdp == 4 and width == H * HD
     if fsdp == 8 and fits and whole_heads and unit % 128 == 0 and token_valid.shape[1] % 256 == 0 and rows == 128:
         return by_kernels(*args)

time: 467 us -> 427 us (0.914)
  Pallas kernels: 418 us -> 405 us
  matrix products: 12.9 us -> 0 us
  other arithmetic: 18.8 us -> 6.63 us
    pallas_call x1 -> x0, Pallas kernels: 16.8 us -> none  [finish(): pl.pallas_call(functools.partial(finish_kernel, nz, runs, has), out_shape...]
    dot_general x2 -> x0, matrix products: 12.9 us -> none  [the longest x1 6.58 us: by_kernels(): branch = jnp.dot(mixed_own, out_w, preferred_element_type=F32) + out_bias]
    reduce_sum x8 -> x0, other arithmetic: 10.4 us -> none  [the longest x1 2.87 us: by_kernels(): jnp.sum(grad_branch.astype(F32), axis=0)]
    pallas_call x1, Pallas kernels: 94.9 us -> 102 us  [mlp_call(): pl.pallas_call(functools.partial(mlp_kernel, nz), out_shape=[shape((rows,...]
where the time goes in v7:
time: 427 us; the launch traced here: 419 us
  Pallas kernels  405 us (95%)
  other arithmetic  6.63 us (2%)
  local copies, waits for them, and re-layouts  6.47 us (2%)
    pallas_call x1, Pallas kernels, head_call(): pl.pallas_call(functools.partial(head_kernel, heads, nz, runs_qkv, runs_u...  159 us
    pallas_call x1, Pallas kernels, tail_call(): pl.pallas_call(functools.partial(tail_kernel, heads, nz, runs_up, runs_qk...  144 us
    pallas_call x1, Pallas kernels, mlp_call(): pl.pallas_call(functools.partial(mlp_kernel, nz), out_shape=[shape((rows,...  102 us

profile of v7, /device:TPU:0, one launch (start us, length us, event | category | flops | bytes accessed | tf_op | source)
XLA Modules:
  0.0 418.8 jit_solution(15405333537647221300)
XLA Ops:
  0.7 159.2 %head.1 = (bf16[1024,768]{1,0:T(8,128)(2,1)}, bf16[8,128,256]{2,1,0:T(8,128)(2,1)}, bf16[128,2048]{1,0:T(8,128)(2,1)}, bf16[128,2048]{1,0:T(8,128)(2,1)}, f32[8,...) custom-call(f32[32]{0:T(128)} %constant.5.clone.refs_0_.slopes, ...), custom_call_target="tpu_custom_call" | custom-call | tf_op jit(solution)/shard_map/head/pallas_call | solution.py:1153
  159.9 101.6 %mlp.1 = (f32[128,2048]{1,0:T(8,128)}, f32[128,2048]{1,0:T(8,128)}, bf16[128,2048]{1,0:T(8,128)(2,1)}, bf16[8,128,256]{2,1,0:T(8,128)(2,1)}, f32[8,2048]{1,0:T(8...) custom-call(bf16[128,2048]{1,0:T(8,128)(2,1)} %get-tuple-element.47., ...), custom_call_target="tpu_custom_call" | custom-call | tf_op jit(solution)/shard_map/mlp/pallas_call | solution.py:1950
  261.5 143.8 %tail.1 = (f32[256,2048]{1,0:T(8,128)}, f32[64,2048]{1,0:T(8,128)}, f32[16,128]{1,0:T(8,128)}, f32[8,128]{1,0:T(8,128)}, bf16[64,8192]{1,0:T(8,128)(2,1)}, /*ind...) custom-call(f32[32]{0:T(128)} %constant.5.clone.refs_0_.slopes, ...), custom_call_target="tpu_custom_call" | custom-call | tf_op jit(solution)/shard_map/tail/pallas_call | solution.py:1644
  405.3 0.0 copy-start.3
  405.3 0.0 copy-start.2
  405.3 0.0 copy-start.1
  405.3 1.4 sqrt_reduce_fusion
  406.7 1.5 slice_bitcast_fusion.1
  408.2 1.2 slice_bitcast_fusion
  409.5 0.0 copy-start
  409.5 2.5 convert_element_type.6
  412.0 2.7 convert_element_type.7
  414.7 0.0 copy-done.3
  414.7 0.8 copy.39
  415.5 0.0 copy-done.2
  415.5 0.8 copy.40
  416.3 0.0 copy-done.1
  416.3 0.8 copy.41
  417.1 0.0 copy-done
  417.1 1.3 copy.42
Async XLA Ops:
  405.3 9.4 %copy-start.3 = (bf16[128,2048]{1,0:T(8,128)(2,1)S(1)}, bf16[128,2048]{1,0:T(8,128)(2,1)}, u32[]{:S(2)}) copy-start(bf16[128,2048]{1,0:T(8,128)(2,1)} %get-tuple-element.100) | copy-start | bytes 1572868
  405.3 10.2 %copy-start.2 = (bf16[128,2048]{1,0:T(8,128)(2,1)S(1)}, bf16[128,2048]{1,0:T(8,128)(2,1)}, u32[]{:S(2)}) copy-start(bf16[128,2048]{1,0:T(8,128)(2,1)} %get-tuple-element.101) | copy-start | bytes 1572868
  405.3 11.0 %copy-start.1 = (f32[64,2048]{1,0:T(8,128)S(1)}, f32[64,2048]{1,0:T(8,128)}, u32[]{:S(2)}) copy-start(f32[64,2048]{1,0:T(8,128)} %get-tuple-element.103) | copy-start | bytes 1572868
  409.5 7.6 %copy-start = (f32[256,2048]{1,0:T(8,128)S(1)}, f32[256,2048]{1,0:T(8,128)}, u32[]{:S(2)}) copy-start(f32[256,2048]{1,0:T(8,128)} %get-tuple-element.105) | copy-start | bytes 6291460

commit v8 on v7

--- a/solution.py
+++ b/solution.py
@@ -314,11 +314,11 @@
     return (x * 2 + c) * 2 * nz + z * 2 + y
 
 
-def halves(ref, rows):
-    half = rows // 2
+def halves(ref, rows, cut=2):
+    half = rows // cut
     if half % 16:
         return {1: None, 2: ref}
-    return {1: ref.at[pl.ds(half, half)], 2: ref.at[pl.ds(0, half)]}
+    return {1: ref.at[pl.ds(half, rows - half)], 2: ref.at[pl.ds(0, half)]}
 
 
 def sliced_gather(src, dst, runs, sems, nz, pos):
@@ -429,7 +429,7 @@
         return remote(src, dst.at[x * 2 + y], send.at[m], recv.at[m], neighbour(m))
 
     def relay(m):
-        b = halves(there(m), rows)[m]
+        b = halves(there(m), rows, 4)[m]
         return b is not None and remote(b, b, send.at[2 + m], recv.at[2 + m], neighbour(3 - m))
 
     def arrival(b, sem):
@@ -448,7 +448,7 @@
 
     def last():
         local.wait()
-        parts = halves(there(3), rows)
+        parts = halves(there(3), rows, 4)
         for m in (1, 2):
             if parts[m] is not None:
                 arrival(parts[m], recv.at[2 + m]).wait_recv()
@@ -1108,10 +1108,10 @@
         gap = jnp.where(allowed, table[0:1, :], MASKED)
         for h in range(heads):
             lanes = slice(h * HD, (h + 1) * HD)
-            q = joined[here, lanes]
+            q = joined[here, lanes] * BF(HD ** (-0.5))
             k = joined[:, cols + h * HD : cols + (h + 1) * HD]
             v = joined[:, 2 * cols + h * HD : 2 * cols + (h + 1) * HD]
-            logits = dot(q, k, NT) * HD ** (-0.5) + slope[h] * gap
+            logits = dot(q, k, NT) + slope[h] * gap
             weights = jnp.exp(logits - jnp.max(logits, axis=1, keepdims=True))
             probs = weights * (1.0 / jnp.sum(weights, axis=1, keepdims=True))
             mixed[pl.ds(i * per, per), :, lanes] = dot(probs.astype(BF), v, NN).astype(BF).reshape(per, rows, HD)
@@ -1125,11 +1125,12 @@
         later(0, go[nz : 2 * nz])
         later(1, gc[3:4] + gu[n + 1 : n + 1 + n // 2])
         later(2, gc[4:5] + gu[n + 1 + n // 2 : 2 * n + 1])
-        later(3, go[2 * nz : 3 * nz])
         return 0
 
     lax.fori_loop(0, steps, attend_step, 0)
     ex[0]()
+    for stage in go[2 * nz : 3 * nz]:
+        stage()
     ex[1]()
     for stage in (go[-1], gc[-1], gu[-1], gd[-1]):
         stage()
@@ -1247,10 +1248,9 @@
             if t < zz < nz:
                 pl.when(z == zz)(functools.partial(event, t, False))
 
-    def begin():
-        for i in range(nz - 1):
-            pl.when(z == 0)(functools.partial(event, nz - 1 - i, True))
-            pl.when(z == nz - 1)(functools.partial(event, i, False))
+    def begin(i):
+        pl.when(z == 0)(functools.partial(event, nz - 1 - i, True))
+        pl.when(z == nz - 1)(functools.partial(event, i, False))
 
     def near(i):
         t = nz - 1 - i
@@ -1353,8 +1353,8 @@
 
 
 def tail_kernel(
-    heads, nz, runs_up, runs_qkv, slopes, far_in, grad_in, joined, a1_in, mixed, qkv_in, branch, upd_in, up_src, down_src,
-    middle, x_own, whole, grad_middle, sums, bias_g,
+    heads, nz, runs_up, runs_qkv, slopes, far_in, grad_in, joined, a1_in, mixed_in, qkv_in, branch, upd_in, up_src, down_src,
+    middle_in, x_in, whole, grad_in_middle, sums, bias_g,
     down_o, out_o, small_o, bias_o, up_o, qkv_o, branch_all, layer_o, grad_o, grad_s, *refs,
 ):
     refs = list(refs)
@@ -1369,7 +1369,7 @@
     att_p, att_acc, att_came, att_send, att_recv = take(5)
     up_refs, down_refs, qkv_refs, out_refs = take(6), take(6), take(6), take(6)
     up_sum, qkv_sum, qkv_g, out_g, res, res_low = take(6)
-    grad_low, vec, came, bias_t, bias_c = take(5)
+    grad_low, vec, came, bias_t, bias_c, mixed, middle, x_own, grad_middle = take(9)
     gsems, esems, esems_up, esems_qkv, tsems, tsems_x = take(2), take(2), take(2), take(2), take(2), take(2)
     vsems, bsems = take(2), take(2)
     gap_sem, load_sem = take(2)
@@ -1377,7 +1377,7 @@
     pos = place()
     x, c, z, y = pos
     n = 2 * nz
-    tree, cols = mixed.shape
+    tree, cols = mixed_in.shape
     rows, width = branch.shape
     part = up_sum.shape[1]
     rank = z * 2 + c
@@ -1437,7 +1437,11 @@
     for t in range(nz):
         upd_swap(t).start()
     gap_load(0, 0).start()
-    for copy in loads + [load_w, load_a]:
+    lates = [
+        pltpu.make_async_copy(a, b, load_sem.at[nz + 3 + i])
+        for i, (a, b) in enumerate([(mixed_in, mixed), (middle_in, middle), (x_in, x_own), (grad_in_middle, grad_middle)])
+    ]
+    for copy in loads + [load_w, load_a] + lates:
         copy.start()
     acc_k[...] = jnp.zeros_like(acc_k)
     acc_v[...] = jnp.zeros_like(acc_v)
@@ -1446,7 +1450,8 @@
     es[1]()
     gb[0]()
     gb[1]()
-    upd_begin()
+    for i in range(nz - 1):
+        upd_begin(i)
 
     steps = tree // step
     slope = [slopes[head_number(h, heads, nz, pos)] for h in range(heads)]
@@ -1462,15 +1467,16 @@
         for h in range(heads):
             lane = slice(h * HD, (h + 1) * HD)
             q = joined[here, lane]
+            scale = BF(HD ** (-0.5))
             k = joined[:, cols + h * HD : cols + (h + 1) * HD]
             v = joined[:, 2 * cols + h * HD : 2 * cols + (h + 1) * HD]
             g = grads[:, lane]
-            logits = dot(k, q, NT) * HD ** (-0.5) + slope[h] * gap
+            logits = dot(k, q * scale, NT) + slope[h] * gap
             weights = jnp.exp(logits - jnp.max(logits, axis=0, keepdims=True))
             probs = weights * (1.0 / jnp.sum(weights, axis=0, keepdims=True))
-            grad_probs = dot(v, g, NT)
+            grad_probs = dot(v, g * scale, NT)
             delta = jnp.sum(probs * grad_probs, axis=0, keepdims=True)
-            grad_raw = (probs * (grad_probs - delta) * HD ** (-0.5)).astype(BF)
+            grad_raw = (probs * (grad_probs - delta)).astype(BF)
             acc_v[:, lane] += dot(probs.astype(BF), g, NN)
             acc_k[:, lane] += dot(grad_raw, q, NN)
             grad_joined[here, lane] = dot(grad_raw, k, TN).astype(BF)
@@ -1497,7 +1503,7 @@
 
         return put
 
-    def back(t, _):
+    def back(t):
         here = pl.ds(pl.multiple_of(t * 2 * rows, 2 * rows), 2 * rows)
 
         def tile(j, _):
@@ -1507,9 +1513,11 @@
 
         lax.fori_loop(0, width // 512, tile, 0)
         att_swap(t).start()
-        return 0
-
-    lax.fori_loop(0, nz, back, 0)
+
+    for i in range(nz):
+        back(jnp.where(z < nz // 2, nz - 1 - i, i))
+        if i:
+            att_begin(i - 1)
     load_a.wait()
     blocks = 256 // part
 
@@ -1523,7 +1531,6 @@
             qkv_g[d // 2 * 2 + f % 2, pl.ds(pl.multiple_of(p * part, part), part), :] = value[i * part : (i + 1) * part]
         return 0
 
-    att_begin()
     col = jnp.sum(grad_joined[...].astype(F32), axis=0, keepdims=True)
     vec[...] = jnp.zeros_like(vec)
     for there, here, size in head_runs(nz, cols)(rank):
@@ -1557,6 +1564,8 @@
         stage()
     load_b.start()
     load_b.wait()
+    for copy in lates:
+        copy.wait()
 
     def out_tile(j, _):
         w = pl.ds(pl.multiple_of(j * 512, 512), 512)
@@ -1654,7 +1663,7 @@
             shape((rows, width), BF),
             shape((rows, width), BF),
         ],
-        in_specs=[pl.BlockSpec(memory_space=pltpu.SMEM), HBM, HBM, VM, HBM, VM] + [HBM] * 5 + [VM] * 6,
+        in_specs=[pl.BlockSpec(memory_space=pltpu.SMEM), HBM, HBM, VM] + [HBM] * 9 + [VM, HBM, VM, VM],
         out_specs=[VM] * 4 + [HBM] * 5,
         scratch_shapes=[
             pltpu.VMEM((n, rows, cols), BF),
@@ -1683,6 +1692,10 @@
             pltpu.VMEM((4 * n, 16, 128), F32),
             pltpu.VMEM((4, 8, 128), F32),
             pltpu.VMEM((3, 8, 128), F32),
+            pltpu.VMEM((tree, cols), BF),
+            pltpu.VMEM((rows, width), F32),
+            pltpu.VMEM((rows, width), BF),
+            pltpu.VMEM((rows, width), F32),
         ]
         + gather_sems(nz)
         + exchange_sems(None, nz)
@@ -1691,7 +1704,7 @@
         + trade_sems() * 2
         + [pltpu.SemaphoreType.DMA((4 * n,))] * 2
         + [pltpu.SemaphoreType.DMA((3,))] * 2
-        + [pltpu.SemaphoreType.DMA((2,)), pltpu.SemaphoreType.DMA((nz + 3,))],
+        + [pltpu.SemaphoreType.DMA((2,)), pltpu.SemaphoreType.DMA((nz + 7,))],
         compiler_params=params(cid, 63 * MIB),
         name="tail",
     )(
@@ -1787,15 +1800,15 @@
     def at_rows(ref, zi):
         return ref[pl.ds(zi * 2, 2)].reshape(pair, width)
 
-    def hidden_part(zi, early):
+    def hidden_part(zi):
         here = pl.ds(pl.multiple_of(zi * pair, pair), pair)
 
         def tile(j, _):
             u = pl.ds(pl.multiple_of(j * 256, 256), 256)
             value = dot(at_rows(mlp, zi), up_w[:, u], NN) + bias[:, u]
-            grad = dot(at_rows(cot, zi), down_w[u, :], NT)
+            grad_act = dot(at_rows(cot, zi), down_w[u, :], NT)
             act, slope = gelu_and_slope(value)
-            low = (grad * slope).astype(BF)
+            low = (grad_act * slope).astype(BF)
             active[here, u] = act.astype(BF)
             gh[here, u] = low
             bias_g[:, u] += jnp.sum(f(low), axis=0, keepdims=True)
@@ -1899,7 +1912,7 @@
     for s in range(slots):
         if s < nz:
             zi = arrive(s)
-            hidden_part(zi, s)
+            hidden_part(zi)
             swap(zi).start()
         slot(s)
         if s < nz:

time: 427 us -> 424 us (level)
  no operation moved by 1% of the time
where the time goes in v8:
time: 424 us; the launch traced here: 415 us
  Pallas kernels  401 us (95%)
  other arithmetic  6.63 us (2%)
  local copies, waits for them, and re-layouts  6.47 us (2%)
    pallas_call x1, Pallas kernels, head_call(): pl.pallas_call(functools.partial(head_kernel, heads, nz, runs_qkv, runs_u...  159 us
    pallas_call x1, Pallas kernels, tail_call(): pl.pallas_call(functools.partial(tail_kernel, heads, nz, runs_up, runs_qk...  144 us
    pallas_call x1, Pallas kernels, mlp_call(): pl.pallas_call(functools.partial(mlp_kernel, nz), out_shape=[shape((rows,...  98.3 us

profile of v8, /device:TPU:0, one launch (start us, length us, event | category | flops | bytes accessed | tf_op | source)
XLA Modules:
  0.0 415.4 jit_solution(7721167464164322127)
XLA Ops:
  0.7 159.2 %head.1 = (bf16[1024,768]{1,0:T(8,128)(2,1)}, bf16[8,128,256]{2,1,0:T(8,128)(2,1)}, bf16[128,2048]{1,0:T(8,128)(2,1)}, bf16[128,2048]{1,0:T(8,128)(2,1)}, f32[8,...) custom-call(f32[32]{0:T(128)} %constant.5.clone.refs_0_.slopes, ...), custom_call_target="tpu_custom_call" | custom-call | tf_op jit(solution)/shard_map/head/pallas_call | solution.py:1154
  159.9 98.3 %mlp.1 = (f32[128,2048]{1,0:T(8,128)}, f32[128,2048]{1,0:T(8,128)}, bf16[128,2048]{1,0:T(8,128)(2,1)}, bf16[8,128,256]{2,1,0:T(8,128)(2,1)}, f32[8,2048]{1,0:T(8...) custom-call(bf16[128,2048]{1,0:T(8,128)(2,1)} %get-tuple-element.47., ...), custom_call_target="tpu_custom_call" | custom-call | tf_op jit(solution)/shard_map/mlp/pallas_call | solution.py:1963
  258.2 143.7 %tail.1 = (f32[256,2048]{1,0:T(8,128)}, f32[64,2048]{1,0:T(8,128)}, f32[16,128]{1,0:T(8,128)}, f32[8,128]{1,0:T(8,128)}, bf16[64,8192]{1,0:T(8,128)(2,1)}, /*ind...) custom-call(f32[32]{0:T(128)} %constant.5.clone.refs_0_.slopes, ...), custom_call_target="tpu_custom_call" | custom-call | tf_op jit(solution)/shard_map/tail/pallas_call | solution.py:1653
  401.8 0.0 copy-start.3
  401.8 0.0 copy-start.2
  401.9 0.0 copy-start.1
  401.9 1.4 sqrt_reduce_fusion
  403.3 1.5 slice_bitcast_fusion.1
  404.8 1.2 slice_bitcast_fusion
  406.0 0.0 copy-start
  406.0 2.5 convert_element_type.6
  408.6 2.7 convert_element_type.7
  411.2 0.0 copy-done.3
  411.3 0.8 copy.39
  412.0 0.0 copy-done.2
  412.0 0.8 copy.40
  412.8 0.0 copy-done.1
  412.8 0.8 copy.41
  413.6 0.0 copy-done
  413.6 1.3 copy.42
Async XLA Ops:
  401.8 9.4 %copy-start.3 = (bf16[128,2048]{1,0:T(8,128)(2,1)S(1)}, bf16[128,2048]{1,0:T(8,128)(2,1)}, u32[]{:S(2)}) copy-start(bf16[128,2048]{1,0:T(8,128)(2,1)} %get-tuple-element.100) | copy-start | bytes 1572868
  401.8 10.2 %copy-start.2 = (bf16[128,2048]{1,0:T(8,128)(2,1)S(1)}, bf16[128,2048]{1,0:T(8,128)(2,1)}, u32[]{:S(2)}) copy-start(bf16[128,2048]{1,0:T(8,128)(2,1)} %get-tuple-element.101) | copy-start | bytes 1572868
  401.9 11.0 %copy-start.1 = (f32[64,2048]{1,0:T(8,128)S(1)}, f32[64,2048]{1,0:T(8,128)}, u32[]{:S(2)}) copy-start(f32[64,2048]{1,0:T(8,128)} %get-tuple-element.103) | copy-start | bytes 1572868
  406.0 7.6 %copy-start = (f32[256,2048]{1,0:T(8,128)S(1)}, f32[256,2048]{1,0:T(8,128)}, u32[]{:S(2)}) copy-start(f32[256,2048]{1,0:T(8,128)} %get-tuple-element.105) | copy-start | bytes 6291460
